TPU v7x, 32 devices: a whole 2x2x4 slice. The times are simulated.
32 devices in a mesh: context: 2 (over y), tensor: 4 (over z), fsdp: 4 (over x, core).
Axes of the slice: x: 2, y: 2, z: 4, core: 2. Of those that a mesh axis runs over, the one named last changes fastest.
Arguments:
- queries: bfloat16 [4, 256, 4096], P('fsdp', 'context', 'tensor'), may hold values from -8 to 8
- keys: bfloat16 [4, 256, 4096], P('fsdp', 'context', 'tensor'), may hold values from -8 to 8
- values: bfloat16 [4, 256, 4096], P('fsdp', 'context', 'tensor'), may hold values from -6 to 6
- out_grad: bfloat16 [4, 256, 4096], P('fsdp', 'context', 'tensor'), may hold values from -6 to 6
- out_weight: bfloat16 [4096, 4096], P('fsdp', 'tensor'), may hold values from -0.09375 to 0.09375
- slopes: float32 [32], P('tensor'), may hold values from 0.00048828125 to 0.05
- counts: int32 [4, 2], P('fsdp', 'context'), may hold values from 1 to 128, 160 in all within a row
- gaps: int32 [4, 256], P('fsdp', 'context'), may hold values from 1 to 12
Outputs:
- query_grad: bfloat16 [4, 256, 4096], P('fsdp', 'context', 'tensor')
- key_grad: bfloat16 [4, 256, 4096], P('fsdp', 'context', 'tensor')
- value_grad: bfloat16 [4, 256, 4096], P('fsdp', 'context', 'tensor')
- weight_grad: float32 [4096, 4096], P('fsdp', 'tensor')
Inputs may be any that keep to these rules, and one draw needn't show every extreme that they name: In each sequence the counts sum to 160 and the largest is 128.
All inputs are finite; a program needn't handle non-finite values. No bound on the sum of `counts` on one device may be relied on, other than what follows from the above.
Results may differ from a plain program's by a relative error of at most 0.022.
Values may be sent and summed in bfloat16 or wider, within the bound.
No kernel may reach another device: no remote copies, remote signals or barrier semaphores. Data moves between devices by JAX's collectives and lax.ppermute only.
A program may use at most 64 MiB of HBM per device.

v0:
```python
import jax
import jax.numpy as jnp
from jax import lax
from jax.sharding import PartitionSpec as P

NEG = -1e30


def per_device(queries, keys, values, out_grad, out_weight, slopes, counts, gaps):
    row_count = queries.shape[1]
    width = queries.shape[2]
    head_count = slopes.shape[0]
    head_size = width // head_count
    scaling = head_size ** (-0.5)
    shard_count = lax.axis_size("context")
    my_start = lax.axis_index("context") * row_count
    total_slots = shard_count * row_count
    all_gaps, all_counts = (
        lax.all_gather(gaps, "context", axis=1, tiled=True),
        lax.all_gather(counts, "context", axis=1, tiled=True),
    )
    slot_index = jnp.arange(total_slots, dtype=jnp.int32)
    owner = slot_index // row_count
    shard_ids = jnp.arange(shard_count, dtype=jnp.int32)
    slot_limit = jnp.sum(
        jnp.where(owner[:, None] == shard_ids[None, :], all_counts[0][None, :], 0), axis=1
    )
    slot_valid = slot_index % row_count < slot_limit
    offsets = jnp.cumsum(jnp.where(slot_valid, all_gaps[0], 0)).astype(jnp.float32)
    my_valid = lax.dynamic_slice_in_dim(slot_valid, my_start, row_count)
    grad_full = lax.all_gather(out_grad[0], "tensor", axis=1, tiled=True)
    grad_masked = jnp.where(my_valid[:, None], grad_full, jnp.zeros_like(grad_full))
    columns = grad_masked
    grad_heads = jnp.dot(
        columns,
        lax.all_gather(out_weight, "fsdp", axis=0, tiled=True),
        preferred_element_type=jnp.float32,
    ).astype(jnp.bfloat16)
    local_q = queries[0]
    local_k = keys[0]
    local_v = values[0]
    key_full, value_full = (
        lax.all_gather(local_k, "context", axis=0, tiled=True),
        lax.all_gather(local_v, "context", axis=0, tiled=True),
    )

    def split(block):
        return block.reshape(block.shape[0], head_count, head_size)

    def scores(q_block, q_start, k_block, k_start):
        query_count = q_block.shape[0]
        key_count = k_block.shape[0]
        logits = (
            jnp.einsum(
                "qhd,khd->hqk", split(q_block), split(k_block), preferred_element_type=jnp.float32
            )
            * scaling
        )
        q_offset = lax.dynamic_slice_in_dim(offsets, q_start, query_count)
        k_offset = lax.dynamic_slice_in_dim(offsets, k_start, key_count)
        k_valid = lax.dynamic_slice_in_dim(slot_valid, k_start, key_count)
        q_slot = q_start + jnp.arange(query_count, dtype=jnp.int32)
        k_slot = k_start + jnp.arange(key_count, dtype=jnp.int32)
        allowed = k_valid[None, :] & (k_slot[None, :] <= q_slot[:, None])
        logits = logits - slopes[:, None, None] * (
            q_offset[None, :, None] - k_offset[None, None, :]
        )
        return (jnp.where(allowed[None], logits, NEG), allowed)

    def tile_terms(q_block, g_block, q_lse, q_delta, q_start, k_block, v_block, k_start):
        logits, allowed = scores(q_block, q_start, k_block, k_start)
        probs = jnp.where(allowed[None], jnp.exp(logits - q_lse[:, :, None]), 0.0)
        value_dots = jnp.einsum(
            "qhd,khd->hqk", split(g_block), split(v_block), preferred_element_type=jnp.float32
        )
        dscore = (probs * (value_dots - q_delta[:, :, None])).astype(jnp.bfloat16)
        return (probs.astype(jnp.bfloat16), dscore)

    block = 2 * row_count
    block_total = total_slots // block

    def mass_step(block_index, carry):
        k_start = block_index * block
        k_block = lax.dynamic_slice_in_dim(key_full, k_start, block, 0)

        def work(state):
            peak, mass = state
            logits, allowed = scores(local_q, my_start, k_block, k_start)
            new_peak = jnp.maximum(peak, jnp.max(logits, axis=2))
            weights = jnp.where(allowed[None], jnp.exp(logits - new_peak[:, :, None]), 0.0)
            return (new_peak, mass * jnp.exp(peak - new_peak) + jnp.sum(weights, axis=2))

        return work(carry)

    start_state = (
        jnp.full((head_count, row_count), NEG, jnp.float32),
        jnp.zeros((head_count, row_count), jnp.float32),
    )
    peak, mass = lax.fori_loop(0, block_total, mass_step, start_state)
    log_total = peak + jnp.log(mass)

    def output_step(block_index, carry):
        k_start = block_index * block
        k_block = lax.dynamic_slice_in_dim(key_full, k_start, block, 0)
        v_block = lax.dynamic_slice_in_dim(value_full, k_start, block, 0)

        def work(acc):
            logits, allowed = scores(local_q, my_start, k_block, k_start)
            probs_b = jnp.where(allowed[None], jnp.exp(logits - log_total[:, :, None]), 0.0).astype(
                jnp.bfloat16
            )
            return acc + jnp.einsum(
                "hqk,khd->qhd", probs_b, split(v_block), preferred_element_type=jnp.float32
            ).reshape(row_count, width)

        return work(carry)

    output_b = lax.fori_loop(
        0, block_total, output_step, jnp.zeros((row_count, width), jnp.float32)
    ).astype(jnp.bfloat16)
    delta = jnp.sum(
        (grad_heads.astype(jnp.float32) * output_b.astype(jnp.float32)).reshape(
            row_count, head_count, head_size
        ),
        axis=2,
    ).T

    def query_step(block_index, carry):
        k_start = block_index * block
        k_block = lax.dynamic_slice_in_dim(key_full, k_start, block, 0)
        v_block = lax.dynamic_slice_in_dim(value_full, k_start, block, 0)

        def work(acc):
            probs_b, dscore = tile_terms(
                local_q, grad_heads, log_total, delta, my_start, k_block, v_block, k_start
            )
            return (
                acc
                + jnp.einsum(
                    "hqk,khd->qhd", dscore, split(k_block), preferred_element_type=jnp.float32
                ).reshape(row_count, width)
                * scaling
            )

        return work(carry)

    query_grad = lax.fori_loop(
        0, block_total, query_step, jnp.zeros((row_count, width), jnp.float32)
    ).astype(jnp.bfloat16)
    stats_lse, stats_delta = (
        lax.all_gather(log_total, "context", axis=1, tiled=True),
        lax.all_gather(delta, "context", axis=1, tiled=True),
    )
    start = jnp.int32(0)
    q_piece = lax.all_gather(local_q, "context", axis=0, tiled=True)
    g_piece = lax.all_gather(grad_heads, "context", axis=0, tiled=True)

    def work(held):
        probs_b, dscore = tile_terms(
            q_piece, g_piece, stats_lse, stats_delta, start, local_k, local_v, my_start
        )
        key_part = (
            jnp.einsum(
                "hqk,qhd->khd", dscore, split(q_piece), preferred_element_type=jnp.float32
            ).reshape(row_count, width)
            * scaling
        )
        value_part = jnp.einsum(
            "hqk,qhd->khd", probs_b, split(g_piece), preferred_element_type=jnp.float32
        ).reshape(row_count, width)
        return jnp.concatenate([key_part, value_part], axis=1)

    key_value_grads = work(jnp.zeros((row_count, 2 * width), jnp.float32))
    key_grad = key_value_grads[:, :width].astype(jnp.bfloat16)
    value_grad = key_value_grads[:, width:].astype(jnp.bfloat16)
    columns = grad_masked
    weight_share = lax.psum_scatter(
        lax.dot_general(
            columns, output_b, (((0,), (0,)), ((), ())), preferred_element_type=jnp.float32
        ),
        "fsdp",
        scatter_dimension=0,
        tiled=True,
    )
    weight_grad = lax.psum(weight_share, "context")
    return (query_grad[None], key_grad[None], value_grad[None], weight_grad)


def solution(mesh):
    placed = (
        P("fsdp", "context", "tensor"),
        P("fsdp", "context", "tensor"),
        P("fsdp", "context", "tensor"),
        P("fsdp", "context", "tensor"),
        P("fsdp", "tensor"),
        P("tensor"),
        P("fsdp", "context"),
        P("fsdp", "context"),
    )
    return jax.shard_map(
        per_device,
        mesh=mesh,
        in_specs=placed,
        out_specs=(
            P("fsdp", "context", "tensor"),
            P("fsdp", "context", "tensor"),
            P("fsdp", "context", "tensor"),
            P("fsdp", "tensor"),
        ),
        check_vma=False,
    )
```

profile of v0, /device:TPU:0, one launch (start us, length us, event | category | flops | bytes accessed | tf_op | source)
XLA Modules:
  0.0 366.1 jit_solution(6148472627785532288)
XLA Ops:
  7.2 0.7 all-gather.9.cloned.1.call-update
  8.6 1.2 dynamic-slice
  10.6 5.2 %all-reduce = s32[2]{0:T(128)S(1)} all-reduce(s32[2]{0:T(128)S(1)} %bitcast_dynamic-update-slice_fusion), channel_id=1, replica_groups=mesh['context'=2,'tensor'=4,'fsdp'=4] {'context'}, use_global_device_ids=true, to_apply=%add | all-reduce | flops 2 | bytes 16
  15.8 4.4 %all_gather.32 = s32[1,256]{1,0:T(1,128)S(1)} all-gather(s32[1,128]{1,0:T(1,128)} %param.15), channel_id=1, replica_groups=mesh['context'=2,'tensor'=4,'fsdp'=4] {'context'}, dimensions={1}, use_global_device_ids=true | all-gather | bytes 1536 | tf_op jit(solution)/shard_map/all_gather | solution.py:19
  20.9 1.1 copy.69
  22.1 7.1 %all-gather = bf16[1,256,1024]{1,2,0:T(8,128)(2,1)S(1)} all-gather(bf16[1,128,1024]{1,2,0:T(8,128)(2,1)S(1)} %copy.69), channel_id=2, replica_groups=mesh['context'=2,'tensor'=4,'fsdp'=4] {'context'}, dimensions={1}, use_global_device_ids=true | all-gather | bytes 786432 | tf_op jit(solution)/shard_map/all_gather | solution.py:43
  29.4 1.0 copy.93
  30.4 1.1 copy.72
  31.5 7.1 %all-gather.2 = bf16[1,256,1024]{1,2,0:T(8,128)(2,1)S(1)} all-gather(bf16[1,128,1024]{1,2,0:T(8,128)(2,1)S(1)} %copy.72), channel_id=4, replica_groups=mesh['context'=2,'tensor'=4,'fsdp'=4] {'context'}, dimensions={1}, use_global_device_ids=true | all-gather | bytes 786432 | tf_op jit(solution)/shard_map/all_gather | solution.py:44
  38.7 1.1 fusion.47
  40.6 9.4 %fusion.28 = f32[4096,1024]{1,0:T(8,128)} fusion(bf16[128,1024]{0,1:T(8,128)(2,1)S(1)} %bitcast.62, bf16[1,128,4096]{2,1,0:T(8,128)(2,1)} %all-gather.9.cloned.1.call-done, pred[128]{0:T(512)(128)(4,1)S(1)} %dynamic_slice.36), kind=kOutput, calls=%fused_computation.38 | convolution fusion | flops 1074266112 | bytes 18088064 | tf_op jit(solution)/shard_map/dot_general | solution.py:178
  50.1 0.7 all-gather.7.cloned.1.call-update
  50.8 127.2 %reduce-scatter.2.cloned.1.call-done = f32[1024,1024]{1,0:T(8,128)} async-done(((f32[4096,1024]{1,0:T(8,128)}), f32[1024,1024]{1,0:T(8,128)}) %reduce-scatter.2.cloned.1.call-update) | async-done | bytes 4194320 | tf_op jit(solution)/shard_map/reduce_scatter | solution.py:177
  178.2 0.9 copy.90
  179.2 4.3 %all_gather.37 = f32[8,256]{1,0:T(8,128)S(1)} all-gather(f32[8,128]{1,0:T(8,128)S(1)} %log_add_fusion), channel_id=1, replica_groups=mesh['context'=2,'tensor'=4,'fsdp'=4] {'context'}, dimensions={1}, use_global_device_ids=true | all-gather | bytes 12288 | tf_op jit(solution)/shard_map/all_gather | solution.py:151
  183.5 7.6 %all-gather.3 = bf16[1,256,1024]{1,2,0:T(8,128)(2,1)S(1)} all-gather(bf16[1,128,1024]{1,2,0:T(8,128)(2,1)S(1)} %copy.77), channel_id=5, replica_groups=mesh['context'=2,'tensor'=4,'fsdp'=4] {'context'}, dimensions={1}, use_global_device_ids=true | all-gather | bytes 786432 | tf_op jit(solution)/shard_map/all_gather | solution.py:155
  192.5 45.5 %all-gather.7.cloned.1.call-done = bf16[4096,1024]{1,0:T(8,128)(2,1)} async-done(((bf16[1024,1024]{1,0:T(8,128)(2,1)}), bf16[4096,1024]{1,0:T(8,128)(2,1)}) %all-gather.7.cloned.1.call-update) | async-done | bytes 8388624 | tf_op jit(solution)/shard_map/all_gather | solution.py:36
  238.0 5.0 %convolution_convert_fusion = bf16[128,1024]{1,0:T(8,128)(2,1)S(1)} fusion(bf16[4096,1024]{1,0:T(8,128)(2,1)} %all-gather.7.cloned.1.call-done, bf16[1,128,4096]{2,1,0:T(8,128)(2,1)} %all-gather.9.cloned.1.call-done, pred[128]{0:T(512)(128)(4,1)S(1)} %dynamic_slice.36), kind=kOutput, calls=%fused_computation.21 | convolution fusion | flops 1074397184 | bytes 9699456 | tf_op jit(solution)/shard_map/dot_general | solution.py:34
  243.0 0.7 copy-done.4
  243.7 14.9 %all_gather.38 = bf16[256,1024]{1,0:T(8,128)(2,1)} all-gather(bf16[128,1024]{1,0:T(8,128)(2,1)S(1)} %convolution_convert_fusion), channel_id=1, replica_groups=mesh['context'=2,'tensor'=4,'fsdp'=4] {'context'}, dimensions={0}, use_global_device_ids=true | all-gather | bytes 786432 | tf_op jit(solution)/shard_map/all_gather | solution.py:156
  258.6 1.2 copy.91
  259.8 1.1 multiply_bitcast_fusion
  260.9 0.9 copy.94
  261.8 1.2 reduce_sum.33
  263.2 2.5 fusion.15
  265.6 1.8 copy.84
  267.4 6.4 %all_gather.39 = f32[8,256]{0,1:T(8,128)S(1)} all-gather(f32[8,128]{0,1:T(8,128)S(1)} %bitcast.76), channel_id=1, replica_groups=mesh['context'=2,'tensor'=4,'fsdp'=4] {'context'}, dimensions={1}, use_global_device_ids=true | all-gather | bytes 12288 | tf_op jit(solution)/shard_map/all_gather | solution.py:152
  274.2 0.9 copy.86
  275.0 1.7 fusion.16
  276.8 0.9 copy.85
  277.6 77.1 %all-reduce.3.cloned.1.call-done = f32[1024,1024]{1,0:T(8,128)} async-done(((f32[1024,1024]{1,0:T(8,128)}), f32[1024,1024]{1,0:T(8,128)}) %all-reduce.3.cloned.1.call-update) | async-done | bytes 4194320 | tf_op jit(solution)/shard_map/psum | solution.py:185
  354.7 4.8 %copy.114 = f32[1024,1024]{1,0:T(8,128)} copy(f32[1024,1024]{1,0:T(8,128)} %all-reduce.3.cloned.1.call-done) | data formatting | bytes 8388608
  (49 shorter events, 4.8 us)
Async XLA Ops:
  7.2 33.4 %all-gather.9.cloned.1.call-start = ((), (), s32[]{:S(2)}) async-start(), calls=%async_computation.4 | async-start | bytes 1310720 | tf_op jit(solution)/shard_map/all_gather | solution.py:31
  7.9 170.1 %reduce-scatter.2.cloned.1.call-start = ((), (), s32[]{:S(2)}) async-start(), calls=%async_computation.2 | async-start | bytes 20971520 | tf_op jit(solution)/shard_map/reduce_scatter | solution.py:177
  29.2 11.0 %copy-start.5 = (bf16[1,256,1024]{1,2,0:T(8,128)(2,1)}, bf16[1,256,1024]{1,2,0:T(8,128)(2,1)S(1)}, u32[]{:S(2)}) copy-start(bf16[1,256,1024]{1,2,0:T(8,128)(2,1)S(1)} %all-gather) | copy-start | bytes 1572868
  50.0 128.0 %copy-start.1 = (bf16[1,128,1024]{2,1,0:T(8,128)(2,1)S(1)}, bf16[1,128,1024]{2,1,0:T(8,128)(2,1)}, u32[]{:S(2)}) copy-start(bf16[1,128,1024]{2,1,0:T(8,128)(2,1)} %param.8) | copy-start | bytes 786436
  50.0 129.1 %copy-start.2 = (bf16[1,128,1024]{2,1,0:T(8,128)(2,1)S(1)}, bf16[1,128,1024]{2,1,0:T(8,128)(2,1)}, u32[]{:S(2)}) copy-start(bf16[1,128,1024]{2,1,0:T(8,128)(2,1)} %param.10) | copy-start | bytes 786436
  50.0 129.1 %copy-start.3 = (bf16[1,128,1024]{2,1,0:T(8,128)(2,1)S(1)}, bf16[1,128,1024]{2,1,0:T(8,128)(2,1)}, u32[]{:S(2)}) copy-start(bf16[1,128,1024]{2,1,0:T(8,128)(2,1)} %param.9) | copy-start | bytes 786436
  50.0 141.9 %copy-start.6 = (f32[8]{0:T(128)S(1)}, f32[8]{0:T(128)}, u32[]{:S(2)}) copy-start(f32[8]{0:T(128)} %param.13) | copy-start | bytes 100
  50.0 187.9 %all-gather.7.cloned.1.call-start = ((), (), s32[]{:S(2)}) async-start(), calls=%async_computation.1 | async-start | bytes 10485760 | tf_op jit(solution)/shard_map/all_gather | solution.py:36
  50.8 304.0 %all-reduce.3.cloned.1.call-start = ((), (), s32[]{:S(2)}) async-start(), calls=%async_computation.3 | async-start | bytes 8388608 | tf_op jit(solution)/shard_map/psum | solution.py:185
  191.1 0.8 copy-start
  243.0 0.7 copy-start.4
Sparse Core Ops, SparseCore 0:
  9.6 30.6 all-gather.8
  50.1 127.8 reduce-scatter.1
  179.7 58.2 all-gather.6
  240.4 114.2 all-reduce.2
where the time goes:
time: 367 us; the launch traced here: 366 us
  waiting for transfers between devices  251 us (68%)
  blocking collectives  57 us (16%)
  matrix products  20.9 us (6%)
  local copies, waits for them, and re-layouts  18.6 us (5%)
  between operations  14.7 us (4%)
    reduce_scatter x1, waiting for transfers between devices, per_device(): lax.psum_scatter(lax.dot_general(columns, output_b, (((0,), (0,)), ((), (...  127 us
    psum x1, waiting for transfers between devices, per_device(): weight_grad = lax.psum(weight_share, 'context')  77.1 us
    all_gather x1, waiting for transfers between devices, per_device(): lax.all_gather(out_weight, 'fsdp', axis=0, tiled=True)  45.5 us
    unnamed x28, local copies, waits for them, and re-layouts  16 us
    all_gather x1, blocking collectives, per_device(): g_piece = lax.all_gather(grad_heads, 'context', axis=0, tiled=True)  14.9 us
    dot_general x1, matrix products, per_device(): lax.dot_general(columns, output_b, (((0,), (0,)), ((), ())), preferred_el...  9.39 us
    all_gather x1, blocking collectives, per_device(): q_piece = lax.all_gather(local_q, 'context', axis=0, tiled=True)  7.59 us
  transfers between devices with their start and end apart: 4, of which 3 were waited for; matrix products, arithmetic and copies ran while one was open for 8% of the time, Pallas kernels for 0%

commit v1 on v0

--- a/solution.py
+++ b/solution.py
@@ -1,12 +1,333 @@
+import functools
+
 import jax
 import jax.numpy as jnp
 from jax import lax
+from jax.experimental import pallas as pl
+from jax.experimental.pallas import tpu as pltpu
 from jax.sharding import PartitionSpec as P
 
 NEG = -1e30
-
-
-def per_device(queries, keys, values, out_grad, out_weight, slopes, counts, gaps):
+F32 = jnp.float32
+BF16 = jnp.bfloat16
+NN = (((1,), (0,)), ((), ()))
+NT = (((1,), (1,)), ((), ()))
+TN = (((0,), (0,)), ((), ()))
+
+
+def dot(a, b, dims=NN):
+    return lax.dot_general(a, b, dims, preferred_element_type=F32)
+
+
+def iota(shape, axis):
+    return lax.broadcasted_iota(jnp.int32, shape, axis)
+
+
+def onehot(mask):
+    return jnp.where(mask, 1.0, 0.0).astype(BF16)
+
+
+def call(body, outs, args, smem=(), scratch=(), vmem=32):
+    return pl.pallas_call(
+        body,
+        out_shape=outs,
+        in_specs=[
+            pl.BlockSpec(memory_space=pltpu.SMEM if i in smem else pltpu.VMEM)
+            for i in range(len(args))
+        ],
+        out_specs=jax.tree.map(lambda _: pl.BlockSpec(memory_space=pltpu.VMEM), outs),
+        scratch_shapes=list(scratch),
+        compiler_params=pltpu.CompilerParams(vmem_limit_bytes=vmem * 2**20),
+    )(*args)
+
+
+def packed_slot(index, half, rows, count0, count1):
+    own0 = jnp.where(index < count0, index, rows + half + index - count0)
+    other = index - half
+    own1 = jnp.where(other < count1, rows + other, half + other - count1)
+    return jnp.where(index < half, own0, own1)
+
+
+def pack_message_kernel(q_ref, k_ref, v_ref, gaps_ref, out_ref):
+    rows, width = q_ref.shape
+    part = width // 2
+    away = pl.ds(pl.multiple_of((1 - lax.axis_index("context")) * part, part), part)
+    for n, ref in enumerate((q_ref, k_ref, v_ref)):
+        out_ref[n * rows : (n + 1) * rows, :] = ref[:, away]
+    tail = jnp.zeros((16, part), F32)
+    line = jnp.broadcast_to(gaps_ref[...].astype(F32), (16, rows))
+    out_ref[3 * rows :, :] = tail.astype(BF16)
+    out_ref[3 * rows :, :rows] = line.astype(BF16)
+
+
+def pack_rows_kernel(count_ref, own_ref, extra_ref, out_ref):
+    half = out_ref.shape[0]
+    extra = extra_ref.shape[0]
+    count = count_ref[0, 0]
+    at, row = iota((half, half), 0), iota((half, half), 1)
+    first = onehot((at == row) & (at < count))
+    at, row = iota((half, extra), 0), iota((half, extra), 1)
+    second = onehot((at >= count) & (at - count == row))
+    out_ref[...] = (dot(first, own_ref[:half, :]) + dot(second, extra_ref[...])).astype(BF16)
+
+
+def forward_kernel(
+    count_ref, slopes_ref, q_ref, k_ref, v_ref, gaps_ref, message_ref,
+    q_out, k_out, v_out, probs_out, output_ref,
+):
+    rows, width = q_ref.shape
+    part = width // 2
+    total = q_out.shape[0]
+    half = total // 2
+    heads = probs_out.shape[0]
+    size = part // heads
+    c = lax.axis_index("context")
+    count = count_ref[0, 0]
+    count0 = jnp.where(c == 0, count, total - count)
+    count1 = total - count0
+    slot_down = packed_slot(iota((total, rows), 0), half, rows, count0, count1)
+    slot_here = iota((total, rows), 1)
+    own_slot = c * rows + slot_here
+    peer_slot = (1 - c) * rows + slot_here
+    own_pick, peer_pick = onehot(slot_down == own_slot), onehot(slot_down == peer_slot)
+    own_until = onehot((own_slot <= slot_down) & (slot_here < count))
+    peer_until = onehot((peer_slot <= slot_down) & (slot_here < total - count))
+    own_gaps = jnp.broadcast_to(gaps_ref[...].astype(F32), (16, rows)).astype(BF16)
+    peer_gaps = message_ref[3 * rows :, :rows]
+    offset_down = (dot(own_until, own_gaps, NT) + dot(peer_until, peer_gaps, NT))[:, :1]
+    offset_across = (dot(own_gaps, own_until, NT) + dot(peer_gaps, peer_until, NT))[:1, :]
+    slot_q = packed_slot(iota((total, total), 0), half, rows, count0, count1)
+    slot_k = packed_slot(iota((total, total), 1), half, rows, count0, count1)
+    allowed = slot_k <= slot_q
+    distance = offset_down - offset_across
+    mine = pl.ds(pl.multiple_of(c * part, part), part)
+    for n, (ref, out) in enumerate(((q_ref, q_out), (k_ref, k_out), (v_ref, v_out))):
+        out[...] = (
+            dot(own_pick, ref[:, mine]) + dot(peer_pick, message_ref[n * rows : (n + 1) * rows, :])
+        ).astype(BF16)
+    for h in range(heads):
+        cols = slice(h * size, (h + 1) * size)
+        slope = slopes_ref[0, c * heads + h]
+        score = dot(q_out[:, cols], k_out[:, cols], NT) * (size**-0.5) - slope * distance
+        score = jnp.where(allowed, score, NEG)
+        peak = jnp.max(score, axis=1, keepdims=True)
+        mass = jnp.where(allowed, jnp.exp(score - peak), 0.0)
+        probs = mass / jnp.sum(mass, axis=1, keepdims=True)
+        probs_out[h] = probs
+        output_ref[:, cols] = dot(probs.astype(BF16), v_out[:, cols]).astype(BF16)
+
+
+def partial_kernel(
+    b00_ref, b01_ref, b10_ref, b11_ref, own_w_ref, near_w_ref,
+    partial_ref, send_ref, own_g_ref, near_g_ref,
+):
+    half = send_ref.shape[0]
+    t, f = lax.axis_index("tensor"), lax.axis_index("fsdp")
+    h, l, x, core = t // 2, t % 2, f // 2, f % 2
+    swap_seq = (h + x) % 2 == 1
+    swap_chunk = (l + core) % 2 == 1
+
+    def pick(a, b, swap):
+        return jnp.where(swap, b[...], a[...])
+
+    def place(own00, own01, own10, own11):
+        own_g_ref[:half], near_g_ref[:half] = own00[...], own01[...]
+        own_g_ref[half:], near_g_ref[half:] = own10[...], own11[...]
+
+    for seq in (False, True):
+        for chunk in (False, True):
+            blocks = ((b00_ref, b01_ref), (b10_ref, b11_ref))
+            first, second = blocks[seq], blocks[not seq]
+
+            @pl.when((swap_seq == seq) & (swap_chunk == chunk))
+            def _(first=first, second=second, chunk=chunk):
+                place(first[chunk], first[not chunk], second[chunk], second[not chunk])
+
+    total = dot(own_g_ref[...], own_w_ref[...]) + dot(near_g_ref[...], near_w_ref[...])
+    partial_ref[...] = total[:half]
+    send_ref[...] = total[half:].astype(BF16)
+
+
+def backward_kernel(
+    count_ref, q_ref, k_ref, v_ref, probs_ref, output_ref, partial_ref, arrived_ref, peer_ref,
+    own_ref, send_ref, g_ref, grads_ref,
+):
+    total, part = q_ref.shape
+    half = total // 2
+    heads = probs_ref.shape[0]
+    size = part // heads
+    rows = own_ref.shape[0] // 3
+    c = lax.axis_index("context")
+    count = count_ref[0, 0]
+    count0 = jnp.where(c == 0, count, total - count)
+    mine = pl.ds(pl.multiple_of(c * part, part), part)
+    here = (partial_ref[:, mine] + arrived_ref[:, mine].astype(F32)).astype(BF16)
+    g_ref[pl.ds(pl.multiple_of(c * half, half), half), :] = here
+    g_ref[pl.ds(pl.multiple_of((1 - c) * half, half), half), :] = peer_ref[...]
+    for h in range(heads):
+        cols = slice(h * size, (h + 1) * size)
+        probs = probs_ref[h]
+        g, q, k, v = g_ref[:, cols], q_ref[:, cols], k_ref[:, cols], v_ref[:, cols]
+        delta = jnp.sum(g.astype(F32) * output_ref[:, cols].astype(F32), axis=1, keepdims=True)
+        dscore = (probs * (dot(g, v, NT) - delta)).astype(BF16)
+        grads_ref[0, :, cols] = (dot(dscore, k) * (size**-0.5)).astype(BF16)
+        grads_ref[1, :, cols] = (dot(dscore, q, TN) * (size**-0.5)).astype(BF16)
+        grads_ref[2, :, cols] = dot(probs.astype(BF16), g, TN).astype(BF16)
+    slot = packed_slot(iota((rows, total), 1), half, rows, count0, total - count0)
+    row = iota((rows, total), 0)
+    own_pick, peer_pick = onehot(slot == c * rows + row), onehot(slot == (1 - c) * rows + row)
+    for n in range(3):
+        send_ref[n * rows : (n + 1) * rows, :] = dot(peer_pick, grads_ref[n]).astype(BF16)
+        own_ref[n * rows : (n + 1) * rows, :] = dot(own_pick, grads_ref[n]).astype(BF16)
+
+
+def finish_kernel(own_ref, peer_ref, q_ref, k_ref, v_ref):
+    rows, width = q_ref.shape
+    part = width // 2
+    c = lax.axis_index("context")
+    mine = pl.ds(pl.multiple_of(c * part, part), part)
+    away = pl.ds(pl.multiple_of((1 - c) * part, part), part)
+    for n, ref in enumerate((q_ref, k_ref, v_ref)):
+        ref[:, mine] = own_ref[n * rows : (n + 1) * rows, :]
+        ref[:, away] = peer_ref[n * rows : (n + 1) * rows, :]
+
+
+def weight_kernel(
+    own_g_ref, near_g_ref, peer_g_ref, out_a_ref, out_b_ref, out_ref, right_ref, left_ref
+):
+    pair = own_g_ref.shape[0]
+    half = pair // 2
+    part = right_ref.shape[1] // 2
+    total = 2 * half
+
+    @pl.when(pl.program_id(0) == 0)
+    def _():
+        c = lax.axis_index("context")
+        for s in range(4):
+            source = out_a_ref if s < 2 else out_b_ref
+            for side in range(2):
+                base = ((s % 2) * 2 + side) * total
+                at = pl.ds(pl.multiple_of((c if side == 0 else 1 - c) * part, part), part)
+                for which in range(2):
+                    rows = (c if which == 0 else 1 - c) * half + base
+                    to = (which * 4 + s) * half
+                    right_ref[to : to + half, at] = source[
+                        pl.ds(pl.multiple_of(rows, half), half), :
+                    ]
+
+    left_ref[:pair, :] = own_g_ref[...]
+    left_ref[pair : 2 * pair, :] = near_g_ref[...]
+    left_ref[2 * pair :, :] = peer_g_ref[...]
+    out_ref[...] = dot(left_ref[...], right_ref[...], TN)
+
+
+def weight_gradient(own_g, near_g, peer_g, out_a, out_b, blocks=4):
+    pair, features = own_g.shape
+    width = 2 * out_a.shape[1]
+    block = features // blocks
+    column = lambda i: (0, i)
+    whole = lambda i: (0, 0)
+    return pl.pallas_call(
+        weight_kernel,
+        grid=(blocks,),
+        out_shape=jax.ShapeDtypeStruct((features, width), F32),
+        in_specs=[
+            pl.BlockSpec((pair, block), column),
+            pl.BlockSpec((pair, block), column),
+            pl.BlockSpec((2 * pair, block), column),
+            pl.BlockSpec(out_a.shape, whole),
+            pl.BlockSpec(out_b.shape, whole),
+        ],
+        out_specs=pl.BlockSpec((block, width), lambda i: (i, 0)),
+        scratch_shapes=[pltpu.VMEM((4 * pair, width), BF16), pltpu.VMEM((4 * pair, block), BF16)],
+        compiler_params=pltpu.CompilerParams(vmem_limit_bytes=32 * 2**20),
+    )(own_g, near_g, peer_g, out_a, out_b)
+
+
+def spread(flip_seq, flip_chunk):
+    pairs = []
+    for t in range(4):
+        for f in range(4):
+            h, l, x, core = t >> 1, t & 1, f >> 1, f & 1
+            to_t = ((x ^ flip_seq) << 1) | (l ^ flip_chunk)
+            pairs.append((t * 4 + f, to_t * 4 + (h << 1 | core)))
+    return pairs
+
+
+def packed_device(queries, keys, values, out_grad, out_weight, slopes, counts, gaps):
+    rows, width = queries.shape[1:]
+    part = width // 2
+    total = 2 * rows * 5 // 8
+    half = total // 2
+    heads = slopes.shape[0] // 2
+    shape = jax.ShapeDtypeStruct
+    over_y = lambda a: lax.ppermute(a, "context", [(0, 1), (1, 0)])
+    over_x = lambda a: lax.ppermute(a, "fsdp", [(i, i ^ 2) for i in range(4)])
+    over_core = lambda a: lax.ppermute(a, "fsdp", [(i, i ^ 1) for i in range(4)])
+    slopes = slopes[None]
+
+    grad = out_grad[0]
+    extra = over_y(grad[half:])
+    message = call(
+        pack_message_kernel,
+        shape((3 * rows + 16, part), BF16),
+        (queries[0], keys[0], values[0], gaps),
+    )
+    message = over_y(message)
+    near_weight = over_core(out_weight)
+    packed = call(pack_rows_kernel, shape((half, width), BF16), (counts, grad, extra), smem=(0,))
+    blocks = [
+        lax.ppermute(packed, ("tensor", "fsdp"), spread(a, b)) for a in (0, 1) for b in (0, 1)
+    ]
+    q, k, v, probs, output = call(
+        forward_kernel,
+        (
+            shape((total, part), BF16),
+            shape((total, part), BF16),
+            shape((total, part), BF16),
+            shape((heads, total, total), F32),
+            shape((total, part), BF16),
+        ),
+        (counts, slopes, queries[0], keys[0], values[0], gaps, message),
+        smem=(0, 1),
+    )
+    peer_output = over_y(output)
+    partial, send, own_g, near_g = call(
+        partial_kernel,
+        (
+            shape((half, width), F32),
+            shape((half, width), BF16),
+            shape((total, width), BF16),
+            shape((total, width), BF16),
+        ),
+        (*blocks, out_weight, near_weight),
+    )
+    arrived = over_x(send)
+    near_g = over_core(near_g)
+    both = jnp.concatenate([output, peer_output], axis=0)
+    out_a = jnp.concatenate([both, over_x(both)], axis=0)
+    out_b = over_core(out_a)
+    c = lax.axis_index("context")
+    away = (1 - c) * part
+    here = lax.dynamic_slice_in_dim(partial, away, part, 1) + lax.dynamic_slice_in_dim(
+        arrived, away, part, 1
+    ).astype(F32)
+    peer_head = over_y(here.astype(BF16))
+    peer_g = over_y(jnp.concatenate([own_g, near_g], axis=0))
+    own, send = call(
+        backward_kernel,
+        (shape((3 * rows, part), BF16), shape((3 * rows, part), BF16)),
+        (counts, q, k, v, probs, output, partial, arrived, peer_head),
+        smem=(0,),
+        scratch=(pltpu.VMEM((total, part), BF16), pltpu.VMEM((3, total, part), BF16)),
+    )
+    peer = over_y(send)
+    weight_grad = weight_gradient(own_g, near_g, peer_g, out_a, out_b)
+    grads = call(finish_kernel, tuple(shape((rows, width), BF16) for _ in range(3)), (own, peer))
+    return (grads[0][None], grads[1][None], grads[2][None], weight_grad)
+
+
+def general_device(queries, keys, values, out_grad, out_weight, slopes, counts, gaps):
     row_count = queries.shape[1]
     width = queries.shape[2]
     head_count = slopes.shape[0]
@@ -197,8 +518,10 @@
         P("fsdp", "context"),
         P("fsdp", "context"),
     )
+    sizes = dict(mesh.shape)
+    packs = sizes["context"] == 2 and sizes["tensor"] == 4 and sizes["fsdp"] == 4
     return jax.shard_map(
-        per_device,
+        packed_device if packs else general_device,
         mesh=mesh,
         in_specs=placed,
         out_specs=(

time: 367 us -> 91.6 us (0.25)
  waiting for transfers between devices: 251 us -> 51 us
  blocking collectives: 57 us -> 0 us
  matrix products: 20.9 us -> 0 us
  starting transfers between devices: 0.16 us -> 20.5 us
  between operations: 14.7 us -> 1.41 us
  local copies, waits for them, and re-layouts: 18.6 us -> 6.17 us
  Pallas kernels: 0 us -> 11.3 us
    reduce_scatter x1 -> x0, waiting for transfers between devices: 127 us -> none  [per_device(): lax.psum_scatter(lax.dot_general(columns, output_b, (((0,), (0,)), ((), (...]
    psum x1 -> x0, waiting for transfers between devices: 77.1 us -> none  [per_device(): weight_grad = lax.psum(weight_share, 'context')]
    all_gather x7 -> x0, blocking collectives: 51.7 us -> none  [the longest x1 14.9 us: per_device(): g_piece = lax.all_gather(grad_heads, 'context', axis=0, tiled=True)]
    ppermute x0 -> x15, waiting for transfers between devices: none -> 51 us  [the longest x6 37 us: packed_device(): over_y = lambda a: lax.ppermute(a, 'context', [(0, 1), (1, 0)])]
    all_gather x2 -> x0, waiting for transfers between devices: 45.5 us -> none  [the longest x1 45.5 us: per_device(): lax.all_gather(out_weight, 'fsdp', axis=0, tiled=True)]
    dot_general x8 -> x0, matrix products: 20.9 us -> none  [the longest x1 9.39 us: per_device(): lax.dot_general(columns, output_b, (((0,), (0,)), ((), ())), preferred_el...]
    ppermute x0 -> x15, starting transfers between devices: none -> 20.5 us  [the longest x6 9.47 us: packed_device(): over_y = lambda a: lax.ppermute(a, 'context', [(0, 1), (1, 0)])]
    pallas_call x0 -> x7, Pallas kernels: none -> 11.3 us  [the longest x6 6.16 us: call(): pl.pallas_call(body, out_shape=outs, in_specs=[pl.BlockSpec(memory_space=...]
  transfers between devices with their start and end apart: 4 -> 15, of which waited for: 3 -> 9; matrix products, arithmetic and copies ran while one was open for 8% -> 1% of each run, Pallas kernels for 0% -> 7%
where the time goes in v1:
time: 91.6 us; the launch traced here: 91.3 us
  waiting for transfers between devices  51 us (56%)
  starting transfers between devices  20.5 us (22%)
  Pallas kernels  11.3 us (12%)
  local copies, waits for them, and re-layouts  6.17 us (7%)
  between operations  1.41 us (2%)
  other arithmetic  0.93 us (1%)
    ppermute x6, waiting for transfers between devices, packed_device(): over_y = lambda a: lax.ppermute(a, 'context', [(0, 1), (1, 0)])  37 us
    ppermute x6, starting transfers between devices, packed_device(): over_y = lambda a: lax.ppermute(a, 'context', [(0, 1), (1, 0)])  9.47 us
    ppermute x2, waiting for transfers between devices, packed_device(): over_x = lambda a: lax.ppermute(a, 'fsdp', [(i, i ^ 2) for i in range(4)])  8.75 us
    ppermute x4, starting transfers between devices, packed_device(): lax.ppermute(packed, ('tensor', 'fsdp'), spread(a, b))  6.24 us
    pallas_call x6, Pallas kernels, call(): pl.pallas_call(body, out_shape=outs, in_specs=[pl.BlockSpec(memory_space=...  6.16 us
    unnamed x24, local copies, waits for them, and re-layouts  6.14 us
    ppermute x4, waiting for transfers between devices, packed_device(): lax.ppermute(packed, ('tensor', 'fsdp'), spread(a, b))  5.19 us
    pallas_call x1, Pallas kernels, weight_gradient(): pl.pallas_call(weight_kernel, grid=(blocks,), out_shape=jax.ShapeDtypeStr...  5.15 us
  transfers between devices with their start and end apart: 15, of which 9 were waited for; matrix products, arithmetic and copies ran while one was open for 1% of the time, Pallas kernels for 7%

profile of v1, /device:TPU:0, one launch (start us, length us, event | category | flops | bytes accessed | tf_op | source)
XLA Modules:
  0.0 91.3 jit_solution(8753143965064491329)
XLA Ops:
  1.2 1.1 %copy-done.1 = bf16[1,128,1024]{2,1,0:T(8,128)(2,1)S(1)} copy-done((bf16[1,128,1024]{2,1,0:T(8,128)(2,1)S(1)}, bf16[1,128,1024]{2,1,0:T(8,128)(2,1)}, u32[]{:S(2)}) %copy-start.1) | copy-done | bytes 262168
  2.2 0.9 %copy-done.2 = bf16[1,128,1024]{2,1,0:T(8,128)(2,1)S(1)} copy-done((bf16[1,128,1024]{2,1,0:T(8,128)(2,1)S(1)}, bf16[1,128,1024]{2,1,0:T(8,128)(2,1)}, u32[]{:S(2)}) %copy-start.2) | copy-done | bytes 262168
  3.2 0.9 %copy-done.3 = bf16[1,128,1024]{2,1,0:T(8,128)(2,1)S(1)} copy-done((bf16[1,128,1024]{2,1,0:T(8,128)(2,1)S(1)}, bf16[1,128,1024]{2,1,0:T(8,128)(2,1)}, u32[]{:S(2)}) %copy-start.3) | copy-done | bytes 262168
  4.1 0.7 copy-done.9
  4.8 2.6 %collective-permute-start = (bf16[400,512]{1,0:T(8,128)(2,1)S(1)}, bf16[400,512]{1,0:T(8,128)(2,1)S(1)}, u32[]{:S(2)}, u32[]{:S(2)}) collective-permute-start(bf16[400,512]{1,0:T(8,128)(2,1)S(1)} %shard_map.111), channel_id=1, source_target_pairs={{0,16},{16,0},{1,17},{17,1},{2,18},{18,2},{3,19},{19,3},{4,20},{20... | collective-permute-start | bytes 1228808 | tf_op jit(solution)/shard_map/ppermute | solution.py:264
  8.1 9.3 %collective-permute-done.message_ref = bf16[400,512]{1,0:T(8,128)(2,1)S(1)} collective-permute-done((bf16[400,512]{1,0:T(8,128)(2,1)S(1)}, bf16[400,512]{1,0:T(8,128)(2,1)S(1)}, u32[]{:S(2)}, u32[]{:S(2)}) %collective-permute-start) | collective-permute-done | bytes 409632 | tf_op jit(solution)/shard_map/ppermute | solution.py:264
  17.4 0.7 copy-done.10
  18.1 1.9 %shard_map.112 = (bf16[160,512]{1,0:T(8,128)(2,1)S(1)}, bf16[160,512]{1,0:T(8,128)(2,1)S(1)}, bf16[160,512]{1,0:T(8,128)(2,1)S(1)}, f32[4,160,160]{2,1,0:T(8,128)S(1)}, bf16[160,512]{1,0:T(8,128)(2,1)S(1)}) custom-call(s32[1,1]{1,0:T(1,128)S(6)} %copy.14.count_ref, f32[1,8]{1,0:T(1,128)S(1)} %bitcast.17, bf16[128,1024]{1,0:T(8,128)(2,1)S(1)} %bitcast.11, ...), custom_call_target="tpu_custom_call" | custom-call | tf_op jit(solution)/shard_map/pallas_call | solution.py:31
  20.0 1.8 %collective-permute-start.12 = (bf16[160,512]{1,0:T(8,128)(2,1)S(1)}, bf16[160,512]{1,0:T(8,128)(2,1)S(1)}, u32[]{:S(2)}, u32[]{:S(2)}) collective-permute-start(bf16[160,512]{1,0:T(8,128)(2,1)S(1)} %get-tuple-element.22.output_ref), channel_id=1, source_target_pairs={{0,16},{16,0},{1,17},{17,1},{2,18},{18,2},{3,19},{19,3},{4,20},{20... | collective-permute-start | bytes 491528 | tf_op jit(solution)/shard_map/ppermute | solution.py:264
  22.2 5.9 %collective-permute-done.1.extra_ref = bf16[48,1024]{1,0:T(8,128)(2,1)S(1)} collective-permute-done((bf16[48,1024]{1,0:T(8,128)(2,1)S(1)}, bf16[48,1024]{1,0:T(8,128)(2,1)S(1)}, u32[]{:S(2)}, u32[]{:S(2)}) %collective-permute-start.1) | collective-permute-done | bytes 98336 | tf_op jit(solution)/shard_map/ppermute | solution.py:264
  28.3 3.6 %collective-permute-start.5 = (bf16[80,1024]{1,0:T(8,128)(2,1)S(1)}, bf16[80,1024]{1,0:T(8,128)(2,1)S(1)}, u32[]{:S(2)}, u32[]{:S(2)}) collective-permute-start(bf16[80,1024]{1,0:T(8,128)(2,1)S(1)} %shard_map.113), channel_id=1, source_target_pairs={{0,12},{1,13},{2,4},{3,5},{4,8},{5,9},{6,0},{7,1},{8,14},{9,15},{1... | collective-permute-start | bytes 491528 | tf_op jit(solution)/shard_map/ppermute | solution.py:280
  31.9 1.5 %collective-permute-start.4 = (bf16[80,1024]{1,0:T(8,128)(2,1)S(1)}, bf16[80,1024]{1,0:T(8,128)(2,1)S(1)}, u32[]{:S(2)}, u32[]{:S(2)}) collective-permute-start(bf16[80,1024]{1,0:T(8,128)(2,1)S(1)} %shard_map.113), channel_id=1, source_target_pairs={{0,8},{1,9},{2,0},{3,1},{4,12},{5,13},{6,4},{7,5},{8,10},{9,11},{1... | collective-permute-start | bytes 491528 | tf_op jit(solution)/shard_map/ppermute | solution.py:280
  33.9 0.7 collective-permute-start.2
  34.6 2.7 %collective-permute-done.5.b11_ref = bf16[80,1024]{1,0:T(8,128)(2,1)S(1)} collective-permute-done((bf16[80,1024]{1,0:T(8,128)(2,1)S(1)}, bf16[80,1024]{1,0:T(8,128)(2,1)S(1)}, u32[]{:S(2)}, u32[]{:S(2)}) %collective-permute-start.5) | collective-permute-done | bytes 163872 | tf_op jit(solution)/shard_map/ppermute | solution.py:280
  37.2 1.5 %collective-permute-start.13 = (bf16[320,512]{1,0:T(8,128)(2,1)S(1)}, bf16[320,512]{1,0:T(8,128)(2,1)S(1)}, u32[]{:S(2)}, u32[]{:S(2)}) collective-permute-start(bf16[320,512]{1,0:T(8,128)(2,1)S(1)} %pad_maximum_fusion.1), channel_id=1, source_target_pairs={{0,2},{1,3},{2,0},{3,1},{4,6},{5,7},{6,4},{7,5},{8,10},{9,11},{10,... | collective-permute-start | bytes 983048 | tf_op jit(solution)/shard_map/ppermute | solution.py:265
  38.7 0.8 collective-permute-done.4.b10_ref
  39.5 1.8 %collective-permute-done.3.b01_ref = bf16[80,1024]{1,0:T(8,128)(2,1)S(1)} collective-permute-done((bf16[80,1024]{1,0:T(8,128)(2,1)S(1)}, bf16[80,1024]{1,0:T(8,128)(2,1)S(1)}, u32[]{:S(2)}, u32[]{:S(2)}) %collective-permute-start.3) | collective-permute-done | bytes 163872 | tf_op jit(solution)/shard_map/ppermute | solution.py:280
  41.3 1.6 %shard_map.114 = (f32[80,1024]{1,0:T(8,128)S(1)}, bf16[80,1024]{1,0:T(8,128)(2,1)}, bf16[160,1024]{1,0:T(8,128)(2,1)S(1)}, bf16[160,1024]{1,0:T(8,128)(2,1)S(1)}) custom-call(bf16[80,1024]{1,0:T(8,128)(2,1)S(1)} %collective-permute-done.2.b00_ref, bf16[80,1024]{1,0:T(8,128)(2,1)S(1)} %collective-permute-done.3.b01_ref, ...), custom_call_target="tpu_custom_call" | custom-call | tf_op jit(solution)/shard_map/pallas_call | solution.py:31
  42.9 6.3 %collective-permute-done.13 = bf16[320,512]{1,0:T(8,128)(2,1)S(1)} collective-permute-done((bf16[320,512]{1,0:T(8,128)(2,1)S(1)}, bf16[320,512]{1,0:T(8,128)(2,1)S(1)}, u32[]{:S(2)}, u32[]{:S(2)}) %collective-permute-start.13) | collective-permute-done | bytes 327712 | tf_op jit(solution)/shard_map/ppermute | solution.py:265
  49.3 2.7 %collective-permute-start.7 = (bf16[80,1024]{1,0:T(8,128)(2,1)}, bf16[80,1024]{1,0:T(8,128)(2,1)S(1)}, u32[]{:S(2)}, u32[]{:S(2)}) collective-permute-start(bf16[80,1024]{1,0:T(8,128)(2,1)} %get-tuple-element.24), channel_id=1, source_target_pairs={{0,2},{1,3},{2,0},{3,1},{4,6},{5,7},{6,4},{7,5},{8,10},{9,11},{10,... | collective-permute-start | bytes 491528 | tf_op jit(solution)/shard_map/ppermute | solution.py:265
  52.0 0.9 pad_maximum_fusion
  52.9 1.5 %collective-permute-start.11 = (bf16[320,1024]{1,0:T(8,128)(2,1)}, bf16[320,1024]{1,0:T(8,128)(2,1)}, u32[]{:S(2)}, u32[]{:S(2)}) collective-permute-start(bf16[320,1024]{1,0:T(8,128)(2,1)} %pad_maximum_fusion), channel_id=1, source_target_pairs={{0,16},{16,0},{1,17},{17,1},{2,18},{18,2},{3,19},{19,3},{4,20},{20... | collective-permute-start | bytes 1966088 | tf_op jit(solution)/shard_map/ppermute | solution.py:264
  54.4 2.5 %collective-permute-done.7.arrived_ref = bf16[80,1024]{1,0:T(8,128)(2,1)S(1)} collective-permute-done((bf16[80,1024]{1,0:T(8,128)(2,1)}, bf16[80,1024]{1,0:T(8,128)(2,1)S(1)}, u32[]{:S(2)}, u32[]{:S(2)}) %collective-permute-start.7) | collective-permute-done | bytes 163872 | tf_op jit(solution)/shard_map/ppermute | solution.py:265
  56.9 1.6 %collective-permute-start.8 = (bf16[80,512]{1,0:T(8,128)(2,1)S(1)}, bf16[80,512]{1,0:T(8,128)(2,1)S(1)}, u32[]{:S(2)}, u32[]{:S(2)}) collective-permute-start(bf16[80,512]{1,0:T(8,128)(2,1)S(1)} %add_convert_fusion), channel_id=1, source_target_pairs={{0,16},{16,0},{1,17},{17,1},{2,18},{18,2},{3,19},{19,3},{4,20},{20... | collective-permute-start | bytes 245768 | tf_op jit(solution)/shard_map/ppermute | solution.py:264
  58.5 13.0 %collective-permute-done.8.peer_ref = bf16[80,512]{1,0:T(8,128)(2,1)S(1)} collective-permute-done((bf16[80,512]{1,0:T(8,128)(2,1)S(1)}, bf16[80,512]{1,0:T(8,128)(2,1)S(1)}, u32[]{:S(2)}, u32[]{:S(2)}) %collective-permute-start.8) | collective-permute-done | bytes 81952 | tf_op jit(solution)/shard_map/ppermute | solution.py:264
  71.5 0.9 %copy-done.6 = bf16[160,512]{1,0:T(8,128)(2,1)S(1)} copy-done((bf16[160,512]{1,0:T(8,128)(2,1)S(1)}, bf16[160,512]{1,0:T(8,128)(2,1)}, u32[]{:S(2)}) %copy-start.6) | copy-done | bytes 163864
  72.4 0.9 %copy-done.8 = bf16[160,512]{1,0:T(8,128)(2,1)S(1)} copy-done((bf16[160,512]{1,0:T(8,128)(2,1)S(1)}, bf16[160,512]{1,0:T(8,128)(2,1)}, u32[]{:S(2)}) %copy-start.8) | copy-done | bytes 163864
  73.3 1.5 %shard_map.115 = (bf16[384,512]{1,0:T(8,128)(2,1)S(1)}, bf16[384,512]{1,0:T(8,128)(2,1)S(1)}) custom-call(s32[1,1]{1,0:T(1,128)S(6)} %copy.14.count_ref, bf16[160,512]{1,0:T(8,128)(2,1)S(1)} %get-tuple-element.18.q_ref, bf16[160,512]{1,0:T(8,128)(2,1)S(1)} %copy-done.6, bf16[160,512]{1,0:T(8,128)(2,1)S(1)} %copy-done.8, ...), custom_call_target="tpu_custom_call" | custom-call | tf_op jit(solution)/shard_map/pallas_call | solution.py:31
  74.8 1.6 %collective-permute-start.9 = (bf16[384,512]{1,0:T(8,128)(2,1)S(1)}, bf16[384,512]{1,0:T(8,128)(2,1)S(1)}, u32[]{:S(2)}, u32[]{:S(2)}) collective-permute-start(bf16[384,512]{1,0:T(8,128)(2,1)S(1)} %get-tuple-element.26), channel_id=1, source_target_pairs={{0,16},{16,0},{1,17},{17,1},{2,18},{18,2},{3,19},{19,3},{4,20},{20... | collective-permute-start | bytes 1179656 | tf_op jit(solution)/shard_map/ppermute | solution.py:264
  76.4 8.8 %collective-permute-done.9.peer_ref = bf16[384,512]{1,0:T(8,128)(2,1)S(1)} collective-permute-done((bf16[384,512]{1,0:T(8,128)(2,1)S(1)}, bf16[384,512]{1,0:T(8,128)(2,1)S(1)}, u32[]{:S(2)}, u32[]{:S(2)}) %collective-permute-start.9) | collective-permute-done | bytes 393248 | tf_op jit(solution)/shard_map/ppermute | solution.py:264
  85.2 0.9 %shard_map.116 = (bf16[128,1024]{1,0:T(8,128)(2,1)}, bf16[128,1024]{1,0:T(8,128)(2,1)}, bf16[128,1024]{1,0:T(8,128)(2,1)}) custom-call(bf16[384,512]{1,0:T(8,128)(2,1)S(1)} %get-tuple-element.25.own_ref, bf16[384,512]{1,0:T(8,128)(2,1)S(1)} %collective-permute-done.9.peer_ref), custom_call_target="tpu_custom_call" | custom-call | tf_op jit(solution)/shard_map/pallas_call | solution.py:31
  86.1 5.2 %shard_map.117 = f32[1024,1024]{1,0:T(8,128)} custom-call(bf16[160,1024]{1,0:T(8,128)(2,1)S(1)} %get-tuple-element.30.own_g_ref, bf16[160,1024]{1,0:T(8,128)(2,1)S(1)} %collective-permute-done.10.near_g_ref, bf16[320,1024]{1,0:T(8,128)(2,1)} %collective-permute-done.11.peer_g_ref, bf16[640,512]{1,0:T(8,128)(2,1)S(1)} %constant_dynamic-update-slice_fusion.out_a_ref, ...), custom_call_target="tpu_custom_call" | custom-call | tf_op jit(solution)/shard_map/pallas_call | solution.py:230
  (34 shorter events, 1.8 us)
Async XLA Ops:
  0.6 40.6 %copy-start = (bf16[1024,1024]{1,0:T(8,128)(2,1)S(1)}, bf16[1024,1024]{1,0:T(8,128)(2,1)}, u32[]{:S(2)}) copy-start(bf16[1024,1024]{1,0:T(8,128)(2,1)} %own_w_ref.1) | copy-start | bytes 6291460
  0.6 40.6 %collective-permute-start.6 = (bf16[1024,1024]{1,0:T(8,128)(2,1)}, bf16[1024,1024]{1,0:T(8,128)(2,1)S(1)}, u32[]{:S(2)}, u32[]{:S(2)}) collective-permute-start(bf16[1024,1024]{1,0:T(8,128)(2,1)} %own_w_ref.1), channel_id=1, source_target_pairs={{0,1},{1,0},{2,3},{3,2},{4,5},{5,4},{6,7},{7,6},{8,9},{9,8},{10,11... | collective-permute-start | bytes 6291464 | tf_op jit(solution)/shard_map/ppermute | solution.py:266
  1.2 1.1 %copy-start.1 = (bf16[1,128,1024]{2,1,0:T(8,128)(2,1)S(1)}, bf16[1,128,1024]{2,1,0:T(8,128)(2,1)}, u32[]{:S(2)}) copy-start(bf16[1,128,1024]{2,1,0:T(8,128)(2,1)} %param.8) | copy-start | bytes 786436
  2.2 0.9 %copy-start.2 = (bf16[1,128,1024]{2,1,0:T(8,128)(2,1)S(1)}, bf16[1,128,1024]{2,1,0:T(8,128)(2,1)}, u32[]{:S(2)}) copy-start(bf16[1,128,1024]{2,1,0:T(8,128)(2,1)} %param.9) | copy-start | bytes 786436
  3.2 0.9 %copy-start.3 = (bf16[1,128,1024]{2,1,0:T(8,128)(2,1)S(1)}, bf16[1,128,1024]{2,1,0:T(8,128)(2,1)}, u32[]{:S(2)}) copy-start(bf16[1,128,1024]{2,1,0:T(8,128)(2,1)} %param.10) | copy-start | bytes 786436
  4.1 0.7 copy-start.9
  4.8 17.0 %copy-start.4 = (bf16[1,128,1024]{2,1,0:T(8,128)(2,1)S(1)}, bf16[1,128,1024]{2,1,0:T(8,128)(2,1)}, u32[]{:S(2)}) copy-start(bf16[1,128,1024]{2,1,0:T(8,128)(2,1)} %param.11) | copy-start | bytes 786436
  4.8 12.6 %collective-permute-start = (bf16[400,512]{1,0:T(8,128)(2,1)S(1)}, bf16[400,512]{1,0:T(8,128)(2,1)S(1)}, u32[]{:S(2)}, u32[]{:S(2)}) collective-permute-start(bf16[400,512]{1,0:T(8,128)(2,1)S(1)} %shard_map.111), channel_id=1, source_target_pairs={{0,16},{16,0},{1,17},{17,1},{2,18},{18,2},{3,19},{19,3},{4,20},{20... | collective-permute-start | bytes 1228808 | tf_op jit(solution)/shard_map/ppermute | solution.py:264
  17.4 0.7 copy-start.10
  20.0 22.9 %copy-start.5 = (bf16[160,512]{1,0:T(8,128)(2,1)}, bf16[160,512]{1,0:T(8,128)(2,1)S(1)}, u32[]{:S(2)}) copy-start(bf16[160,512]{1,0:T(8,128)(2,1)S(1)} %get-tuple-element.19.k_ref) | copy-start | bytes 491524
  20.0 22.9 %copy-start.7 = (bf16[160,512]{1,0:T(8,128)(2,1)}, bf16[160,512]{1,0:T(8,128)(2,1)S(1)}, u32[]{:S(2)}) copy-start(bf16[160,512]{1,0:T(8,128)(2,1)S(1)} %get-tuple-element.20.v_ref) | copy-start | bytes 491524
  20.0 13.9 %collective-permute-start.12 = (bf16[160,512]{1,0:T(8,128)(2,1)S(1)}, bf16[160,512]{1,0:T(8,128)(2,1)S(1)}, u32[]{:S(2)}, u32[]{:S(2)}) collective-permute-start(bf16[160,512]{1,0:T(8,128)(2,1)S(1)} %get-tuple-element.22.output_ref), channel_id=1, source_target_pairs={{0,16},{16,0},{1,17},{17,1},{2,18},{18,2},{3,19},{19,3},{4,20},{20... | collective-permute-start | bytes 491528 | tf_op jit(solution)/shard_map/ppermute | solution.py:264
  21.8 6.2 %collective-permute-start.1 = (bf16[48,1024]{1,0:T(8,128)(2,1)S(1)}, bf16[48,1024]{1,0:T(8,128)(2,1)S(1)}, u32[]{:S(2)}, u32[]{:S(2)}) collective-permute-start(bf16[48,1024]{1,0:T(8,128)(2,1)S(1)} %slice_bitcast_fusion), channel_id=1, source_target_pairs={{0,16},{16,0},{1,17},{17,1},{2,18},{18,2},{3,19},{19,3},{4,20},{20... | collective-permute-start | bytes 294920 | tf_op jit(solution)/shard_map/ppermute | solution.py:264
  28.3 9.0 %collective-permute-start.5 = (bf16[80,1024]{1,0:T(8,128)(2,1)S(1)}, bf16[80,1024]{1,0:T(8,128)(2,1)S(1)}, u32[]{:S(2)}, u32[]{:S(2)}) collective-permute-start(bf16[80,1024]{1,0:T(8,128)(2,1)S(1)} %shard_map.113), channel_id=1, source_target_pairs={{0,12},{1,13},{2,4},{3,5},{4,8},{5,9},{6,0},{7,1},{8,14},{9,15},{1... | collective-permute-start | bytes 491528 | tf_op jit(solution)/shard_map/ppermute | solution.py:280
  31.9 7.6 %collective-permute-start.4 = (bf16[80,1024]{1,0:T(8,128)(2,1)S(1)}, bf16[80,1024]{1,0:T(8,128)(2,1)S(1)}, u32[]{:S(2)}, u32[]{:S(2)}) collective-permute-start(bf16[80,1024]{1,0:T(8,128)(2,1)S(1)} %shard_map.113), channel_id=1, source_target_pairs={{0,8},{1,9},{2,0},{3,1},{4,12},{5,13},{6,4},{7,5},{8,10},{9,11},{1... | collective-permute-start | bytes 491528 | tf_op jit(solution)/shard_map/ppermute | solution.py:280
  33.4 7.9 %collective-permute-start.3 = (bf16[80,1024]{1,0:T(8,128)(2,1)S(1)}, bf16[80,1024]{1,0:T(8,128)(2,1)S(1)}, u32[]{:S(2)}, u32[]{:S(2)}) collective-permute-start(bf16[80,1024]{1,0:T(8,128)(2,1)S(1)} %shard_map.113), channel_id=1, source_target_pairs={{0,4},{1,5},{2,12},{3,13},{4,0},{5,1},{6,8},{7,9},{8,6},{9,7},{10,... | collective-permute-start | bytes 491528 | tf_op jit(solution)/shard_map/ppermute | solution.py:280
  33.9 7.4 %collective-permute-start.2 = (bf16[80,1024]{1,0:T(8,128)(2,1)S(1)}, bf16[80,1024]{1,0:T(8,128)(2,1)S(1)}, u32[]{:S(2)}, u32[]{:S(2)}) collective-permute-start(bf16[80,1024]{1,0:T(8,128)(2,1)S(1)} %shard_map.113), channel_id=1, source_target_pairs={{0,0},{1,1},{2,8},{3,9},{4,4},{5,5},{6,12},{7,13},{8,2},{9,3},{10,... | collective-permute-start | bytes 491528 | tf_op jit(solution)/shard_map/ppermute | solution.py:280
  37.2 12.0 %collective-permute-start.13 = (bf16[320,512]{1,0:T(8,128)(2,1)S(1)}, bf16[320,512]{1,0:T(8,128)(2,1)S(1)}, u32[]{:S(2)}, u32[]{:S(2)}) collective-permute-start(bf16[320,512]{1,0:T(8,128)(2,1)S(1)} %pad_maximum_fusion.1), channel_id=1, source_target_pairs={{0,2},{1,3},{2,0},{3,1},{4,6},{5,7},{6,4},{7,5},{8,10},{9,11},{10,... | collective-permute-start | bytes 983048 | tf_op jit(solution)/shard_map/ppermute | solution.py:265
  42.9 9.1 %collective-permute-start.10 = (bf16[160,1024]{1,0:T(8,128)(2,1)S(1)}, bf16[160,1024]{1,0:T(8,128)(2,1)S(1)}, u32[]{:S(2)}, u32[]{:S(2)}) collective-permute-start(bf16[160,1024]{1,0:T(8,128)(2,1)S(1)} %get-tuple-element.31), channel_id=1, source_target_pairs={{0,1},{1,0},{2,3},{3,2},{4,5},{5,4},{6,7},{7,6},{8,9},{9,8},{10,11... | collective-permute-start | bytes 983048 | tf_op jit(solution)/shard_map/ppermute | solution.py:266
  49.2 36.9 %collective-permute-start.14 = (bf16[640,512]{1,0:T(8,128)(2,1)S(1)}, bf16[640,512]{1,0:T(8,128)(2,1)S(1)}, u32[]{:S(2)}, u32[]{:S(2)}) collective-permute-start(bf16[640,512]{1,0:T(8,128)(2,1)S(1)} %constant_dynamic-update-slice_fusion.out_a_ref), channel_id=1, source_target_pairs={{0,1},{1,0},{2,3},{3,2},{4,5},{5,4},{6,7},{7,6},{8,9},{9,8},{10,11... | collective-permute-start | bytes 1966088 | tf_op jit(solution)/shard_map/ppermute | solution.py:266
  49.3 7.6 %collective-permute-start.7 = (bf16[80,1024]{1,0:T(8,128)(2,1)}, bf16[80,1024]{1,0:T(8,128)(2,1)S(1)}, u32[]{:S(2)}, u32[]{:S(2)}) collective-permute-start(bf16[80,1024]{1,0:T(8,128)(2,1)} %get-tuple-element.24), channel_id=1, source_target_pairs={{0,2},{1,3},{2,0},{3,1},{4,6},{5,7},{6,4},{7,5},{8,10},{9,11},{10,... | collective-permute-start | bytes 491528 | tf_op jit(solution)/shard_map/ppermute | solution.py:265
  52.9 33.2 %collective-permute-start.11 = (bf16[320,1024]{1,0:T(8,128)(2,1)}, bf16[320,1024]{1,0:T(8,128)(2,1)}, u32[]{:S(2)}, u32[]{:S(2)}) collective-permute-start(bf16[320,1024]{1,0:T(8,128)(2,1)} %pad_maximum_fusion), channel_id=1, source_target_pairs={{0,16},{16,0},{1,17},{17,1},{2,18},{18,2},{3,19},{19,3},{4,20},{20... | collective-permute-start | bytes 1966088 | tf_op jit(solution)/shard_map/ppermute | solution.py:264
  56.9 14.6 %collective-permute-start.8 = (bf16[80,512]{1,0:T(8,128)(2,1)S(1)}, bf16[80,512]{1,0:T(8,128)(2,1)S(1)}, u32[]{:S(2)}, u32[]{:S(2)}) collective-permute-start(bf16[80,512]{1,0:T(8,128)(2,1)S(1)} %add_convert_fusion), channel_id=1, source_target_pairs={{0,16},{16,0},{1,17},{17,1},{2,18},{18,2},{3,19},{19,3},{4,20},{20... | collective-permute-start | bytes 245768 | tf_op jit(solution)/shard_map/ppermute | solution.py:264
  71.5 0.9 %copy-start.6 = (bf16[160,512]{1,0:T(8,128)(2,1)S(1)}, bf16[160,512]{1,0:T(8,128)(2,1)}, u32[]{:S(2)}) copy-start(bf16[160,512]{1,0:T(8,128)(2,1)} %copy-done.5) | copy-start | bytes 491524
  72.4 0.9 %copy-start.8 = (bf16[160,512]{1,0:T(8,128)(2,1)S(1)}, bf16[160,512]{1,0:T(8,128)(2,1)}, u32[]{:S(2)}) copy-start(bf16[160,512]{1,0:T(8,128)(2,1)} %copy-done.7) | copy-start | bytes 491524
  74.8 10.3 %collective-permute-start.9 = (bf16[384,512]{1,0:T(8,128)(2,1)S(1)}, bf16[384,512]{1,0:T(8,128)(2,1)S(1)}, u32[]{:S(2)}, u32[]{:S(2)}) collective-permute-start(bf16[384,512]{1,0:T(8,128)(2,1)S(1)} %get-tuple-element.26), channel_id=1, source_target_pairs={{0,16},{16,0},{1,17},{17,1},{2,18},{18,2},{3,19},{19,3},{4,20},{20... | collective-permute-start | bytes 1179656 | tf_op jit(solution)/shard_map/ppermute | solution.py:264

commit v2 on v1

--- a/solution.py
+++ b/solution.py
@@ -27,14 +27,12 @@
     return jnp.where(mask, 1.0, 0.0).astype(BF16)
 
 
-def call(body, outs, args, smem=(), scratch=(), vmem=32):
+def call(body, outs, args, smem=(), hbm=(), scratch=(), vmem=8):
+    where = {i: pltpu.SMEM for i in smem} | {i: pltpu.HBM for i in hbm}
     return pl.pallas_call(
         body,
         out_shape=outs,
-        in_specs=[
-            pl.BlockSpec(memory_space=pltpu.SMEM if i in smem else pltpu.VMEM)
-            for i in range(len(args))
-        ],
+        in_specs=[pl.BlockSpec(memory_space=where.get(i, pltpu.VMEM)) for i in range(len(args))],
         out_specs=jax.tree.map(lambda _: pl.BlockSpec(memory_space=pltpu.VMEM), outs),
         scratch_shapes=list(scratch),
         compiler_params=pltpu.CompilerParams(vmem_limit_bytes=vmem * 2**20),
@@ -48,16 +46,31 @@
     return jnp.where(index < half, own0, own1)
 
 
-def pack_message_kernel(q_ref, k_ref, v_ref, gaps_ref, out_ref):
+def pack_message_kernel(
+    q_ref, k_ref, v_ref, grad_ref, weight_ref, gaps_ref,
+    mine_ref, away_ref, grad_here, weight_here, gaps_here, sems, others,
+):
     rows, width = q_ref.shape
     part = width // 2
-    away = pl.ds(pl.multiple_of((1 - lax.axis_index("context")) * part, part), part)
-    for n, ref in enumerate((q_ref, k_ref, v_ref)):
-        out_ref[n * rows : (n + 1) * rows, :] = ref[:, away]
-    tail = jnp.zeros((16, part), F32)
-    line = jnp.broadcast_to(gaps_ref[...].astype(F32), (16, rows))
-    out_ref[3 * rows :, :] = tail.astype(BF16)
-    out_ref[3 * rows :, :rows] = line.astype(BF16)
+    c = lax.axis_index("context")
+    copies = [
+        pltpu.make_async_copy(gaps_ref, gaps_here, others.at[0]),
+        pltpu.make_async_copy(grad_ref.at[: grad_here.shape[0], :], grad_here, others.at[1]),
+        pltpu.make_async_copy(weight_ref, weight_here, others.at[2]),
+    ]
+    for side, out in enumerate((mine_ref, away_ref)):
+        at = pl.ds(pl.multiple_of((c if side == 0 else 1 - c) * part, part), part)
+        for n, ref in enumerate((q_ref, k_ref, v_ref)):
+            to = out.at[n * rows : (n + 1) * rows, :]
+            copies.append(pltpu.make_async_copy(ref.at[:, at], to, sems.at[side, n]))
+    for copy in copies:
+        copy.start()
+    for copy in copies:
+        copy.wait()
+    line = jnp.broadcast_to(gaps_here[...].astype(F32), (16, rows)).astype(BF16)
+    for out in (mine_ref, away_ref):
+        out[3 * rows :, :] = jnp.zeros((16, part), BF16)
+        out[3 * rows :, :rows] = line
 
 
 def pack_rows_kernel(count_ref, own_ref, extra_ref, out_ref):
@@ -68,15 +81,14 @@
     first = onehot((at == row) & (at < count))
     at, row = iota((half, extra), 0), iota((half, extra), 1)
     second = onehot((at >= count) & (at - count == row))
-    out_ref[...] = (dot(first, own_ref[:half, :]) + dot(second, extra_ref[...])).astype(BF16)
+    out_ref[...] = (dot(first, own_ref[...]) + dot(second, extra_ref[...])).astype(BF16)
 
 
 def forward_kernel(
-    count_ref, slopes_ref, q_ref, k_ref, v_ref, gaps_ref, message_ref,
-    q_out, k_out, v_out, probs_out, output_ref,
+    count_ref, slopes_ref, mine_ref, message_ref, q_out, k_out, v_out, probs_out, output_ref
 ):
-    rows, width = q_ref.shape
-    part = width // 2
+    part = mine_ref.shape[1]
+    rows = (mine_ref.shape[0] - 16) // 3
     total = q_out.shape[0]
     half = total // 2
     heads = probs_out.shape[0]
@@ -92,7 +104,7 @@
     own_pick, peer_pick = onehot(slot_down == own_slot), onehot(slot_down == peer_slot)
     own_until = onehot((own_slot <= slot_down) & (slot_here < count))
     peer_until = onehot((peer_slot <= slot_down) & (slot_here < total - count))
-    own_gaps = jnp.broadcast_to(gaps_ref[...].astype(F32), (16, rows)).astype(BF16)
+    own_gaps = mine_ref[3 * rows :, :rows]
     peer_gaps = message_ref[3 * rows :, :rows]
     offset_down = (dot(own_until, own_gaps, NT) + dot(peer_until, peer_gaps, NT))[:, :1]
     offset_across = (dot(own_gaps, own_until, NT) + dot(peer_gaps, peer_until, NT))[:1, :]
@@ -100,14 +112,12 @@
     slot_k = packed_slot(iota((total, total), 1), half, rows, count0, count1)
     allowed = slot_k <= slot_q
     distance = offset_down - offset_across
-    mine = pl.ds(pl.multiple_of(c * part, part), part)
-    for n, (ref, out) in enumerate(((q_ref, q_out), (k_ref, k_out), (v_ref, v_out))):
-        out[...] = (
-            dot(own_pick, ref[:, mine]) + dot(peer_pick, message_ref[n * rows : (n + 1) * rows, :])
-        ).astype(BF16)
+    for n, out in enumerate((q_out, k_out, v_out)):
+        at = slice(n * rows, (n + 1) * rows)
+        out[...] = (dot(own_pick, mine_ref[at, :]) + dot(peer_pick, message_ref[at, :])).astype(BF16)
     for h in range(heads):
         cols = slice(h * size, (h + 1) * size)
-        slope = slopes_ref[0, c * heads + h]
+        slope = slopes_ref[c * heads + h]
         score = dot(q_out[:, cols], k_out[:, cols], NT) * (size**-0.5) - slope * distance
         score = jnp.where(allowed, score, NEG)
         peak = jnp.max(score, axis=1, keepdims=True)
@@ -117,39 +127,45 @@
         output_ref[:, cols] = dot(probs.astype(BF16), v_out[:, cols]).astype(BF16)
 
 
+def place(blocks, own_ref, near_ref):
+    half = own_ref.shape[0] // 2
+    t, f = lax.axis_index("tensor"), lax.axis_index("fsdp")
+    h, l, x, core = t // 2, t % 2, f // 2, f % 2
+    swap_seq = (h + x) % 2
+    swap_chunk = (l + core) % 2
+    for seq in range(2):
+        for chunk in range(2):
+
+            @pl.when((swap_seq == seq) & (swap_chunk == chunk))
+            def _(seq=seq, chunk=chunk):
+                for n in range(2):
+                    at = slice(n * half, (n + 1) * half)
+                    own_ref[at, :] = blocks[n ^ seq][chunk][...]
+                    near_ref[at, :] = blocks[n ^ seq][1 - chunk][...]
+
+
+def place_kernel(b00_ref, b01_ref, b10_ref, b11_ref, own_ref, near_ref):
+    place(((b00_ref, b01_ref), (b10_ref, b11_ref)), own_ref, near_ref)
+
+
 def partial_kernel(
     b00_ref, b01_ref, b10_ref, b11_ref, own_w_ref, near_w_ref,
-    partial_ref, send_ref, own_g_ref, near_g_ref,
+    keep_ref, send_x_ref, send_y_ref, send_xy_ref, own_g_ref, near_g_ref, total_ref,
 ):
-    half = send_ref.shape[0]
-    t, f = lax.axis_index("tensor"), lax.axis_index("fsdp")
-    h, l, x, core = t // 2, t % 2, f // 2, f % 2
-    swap_seq = (h + x) % 2 == 1
-    swap_chunk = (l + core) % 2 == 1
-
-    def pick(a, b, swap):
-        return jnp.where(swap, b[...], a[...])
-
-    def place(own00, own01, own10, own11):
-        own_g_ref[:half], near_g_ref[:half] = own00[...], own01[...]
-        own_g_ref[half:], near_g_ref[half:] = own10[...], own11[...]
-
-    for seq in (False, True):
-        for chunk in (False, True):
-            blocks = ((b00_ref, b01_ref), (b10_ref, b11_ref))
-            first, second = blocks[seq], blocks[not seq]
-
-            @pl.when((swap_seq == seq) & (swap_chunk == chunk))
-            def _(first=first, second=second, chunk=chunk):
-                place(first[chunk], first[not chunk], second[chunk], second[not chunk])
-
-    total = dot(own_g_ref[...], own_w_ref[...]) + dot(near_g_ref[...], near_w_ref[...])
-    partial_ref[...] = total[:half]
-    send_ref[...] = total[half:].astype(BF16)
+    half, part = keep_ref.shape
+    place(((b00_ref, b01_ref), (b10_ref, b11_ref)), own_g_ref, near_g_ref)
+    total_ref[...] = dot(own_g_ref[...], own_w_ref[...]) + dot(near_g_ref[...], near_w_ref[...])
+    c = lax.axis_index("context")
+    mine = pl.ds(pl.multiple_of(c * part, part), part)
+    away = pl.ds(pl.multiple_of((1 - c) * part, part), part)
+    keep_ref[...] = total_ref[:half, mine]
+    send_x_ref[...] = total_ref[half:, mine].astype(BF16)
+    send_y_ref[...] = total_ref[:half, away].astype(BF16)
+    send_xy_ref[...] = total_ref[half:, away].astype(BF16)
 
 
 def backward_kernel(
-    count_ref, q_ref, k_ref, v_ref, probs_ref, output_ref, partial_ref, arrived_ref, peer_ref,
+    count_ref, q_ref, k_ref, v_ref, probs_ref, output_ref, keep_ref, from_x_ref, from_y_ref, from_xy_ref,
     own_ref, send_ref, g_ref, grads_ref,
 ):
     total, part = q_ref.shape
@@ -160,10 +176,10 @@
     c = lax.axis_index("context")
     count = count_ref[0, 0]
     count0 = jnp.where(c == 0, count, total - count)
-    mine = pl.ds(pl.multiple_of(c * part, part), part)
-    here = (partial_ref[:, mine] + arrived_ref[:, mine].astype(F32)).astype(BF16)
+    here = (keep_ref[...] + from_x_ref[...].astype(F32)).astype(BF16)
+    there = (from_y_ref[...].astype(F32) + from_xy_ref[...].astype(F32)).astype(BF16)
     g_ref[pl.ds(pl.multiple_of(c * half, half), half), :] = here
-    g_ref[pl.ds(pl.multiple_of((1 - c) * half, half), half), :] = peer_ref[...]
+    g_ref[pl.ds(pl.multiple_of((1 - c) * half, half), half), :] = there
     for h in range(heads):
         cols = slice(h * size, (h + 1) * size)
         probs = probs_ref[h]
@@ -193,21 +209,21 @@
 
 
 def weight_kernel(
-    own_g_ref, near_g_ref, peer_g_ref, out_a_ref, out_b_ref, out_ref, right_ref, left_ref
+    own_g_ref, near_g_ref, own_p_ref, near_p_ref, mine_ref, mine_x_ref, mine_core_ref,
+    away_ref, away_x_ref, away_core_ref, out_ref, right_ref, left_ref,
 ):
     pair = own_g_ref.shape[0]
     half = pair // 2
     part = right_ref.shape[1] // 2
-    total = 2 * half
 
     @pl.when(pl.program_id(0) == 0)
     def _():
         c = lax.axis_index("context")
-        for s in range(4):
-            source = out_a_ref if s < 2 else out_b_ref
-            for side in range(2):
-                base = ((s % 2) * 2 + side) * total
-                at = pl.ds(pl.multiple_of((c if side == 0 else 1 - c) * part, part), part)
+        sides = (mine_ref, mine_x_ref, mine_core_ref), (away_ref, away_x_ref, away_core_ref)
+        for side, refs in enumerate(sides):
+            at = pl.ds(pl.multiple_of((c if side == 0 else 1 - c) * part, part), part)
+            for s in range(4):
+                source, base = refs[min(s, 2)], 2 * half * max(s - 2, 0)
                 for which in range(2):
                     rows = (c if which == 0 else 1 - c) * half + base
                     to = (which * 4 + s) * half
@@ -215,42 +231,33 @@
                         pl.ds(pl.multiple_of(rows, half), half), :
                     ]
 
-    left_ref[:pair, :] = own_g_ref[...]
-    left_ref[pair : 2 * pair, :] = near_g_ref[...]
-    left_ref[2 * pair :, :] = peer_g_ref[...]
+    for n, ref in enumerate((own_g_ref, near_g_ref, own_p_ref, near_p_ref)):
+        left_ref[n * pair : (n + 1) * pair, :] = ref[...]
     out_ref[...] = dot(left_ref[...], right_ref[...], TN)
 
 
-def weight_gradient(own_g, near_g, peer_g, out_a, out_b, blocks=4):
-    pair, features = own_g.shape
-    width = 2 * out_a.shape[1]
+def weight_gradient(grads, outputs, blocks=4):
+    pair, features = grads[0].shape
+    width = 2 * outputs[0].shape[1]
     block = features // blocks
-    column = lambda i: (0, i)
-    whole = lambda i: (0, 0)
     return pl.pallas_call(
         weight_kernel,
         grid=(blocks,),
         out_shape=jax.ShapeDtypeStruct((features, width), F32),
-        in_specs=[
-            pl.BlockSpec((pair, block), column),
-            pl.BlockSpec((pair, block), column),
-            pl.BlockSpec((2 * pair, block), column),
-            pl.BlockSpec(out_a.shape, whole),
-            pl.BlockSpec(out_b.shape, whole),
-        ],
+        in_specs=[pl.BlockSpec((pair, block), lambda i: (0, i)) for _ in grads]
+        + [pl.BlockSpec(a.shape, lambda i: (0, 0)) for a in outputs],
         out_specs=pl.BlockSpec((block, width), lambda i: (i, 0)),
         scratch_shapes=[pltpu.VMEM((4 * pair, width), BF16), pltpu.VMEM((4 * pair, block), BF16)],
-        compiler_params=pltpu.CompilerParams(vmem_limit_bytes=32 * 2**20),
-    )(own_g, near_g, peer_g, out_a, out_b)
-
-
-def spread(flip_seq, flip_chunk):
+        compiler_params=pltpu.CompilerParams(vmem_limit_bytes=16 * 2**20),
+    )(*grads, *outputs)
+
+
+def spread(flip):
     pairs = []
     for t in range(4):
         for f in range(4):
             h, l, x, core = t >> 1, t & 1, f >> 1, f & 1
-            to_t = ((x ^ flip_seq) << 1) | (l ^ flip_chunk)
-            pairs.append((t * 4 + f, to_t * 4 + (h << 1 | core)))
+            pairs.append((t * 4 + f, ((x ^ flip) << 1 | l) * 4 + (h << 1 | core)))
     return pairs
 
 
@@ -264,21 +271,31 @@
     over_y = lambda a: lax.ppermute(a, "context", [(0, 1), (1, 0)])
     over_x = lambda a: lax.ppermute(a, "fsdp", [(i, i ^ 2) for i in range(4)])
     over_core = lambda a: lax.ppermute(a, "fsdp", [(i, i ^ 1) for i in range(4)])
-    slopes = slopes[None]
+    after = lax.optimization_barrier
 
     grad = out_grad[0]
-    extra = over_y(grad[half:])
-    message = call(
-        pack_message_kernel,
-        shape((3 * rows + 16, part), BF16),
-        (queries[0], keys[0], values[0], gaps),
-    )
+    extra = grad[half:]
+    extra, q0, near_weight = after((extra, queries, out_weight))
+    near_weight = over_core(near_weight)
+    extra = over_y(extra)
+    own_weight, grad_here = out_weight, grad[:half]
+    c = lax.axis_index("context")
+    tail = jnp.broadcast_to(gaps.astype(BF16), (16, rows))
+    tail = jnp.concatenate([tail] * (part // rows), axis=1)
+
+    def side(which):
+        cut = lambda a: lax.dynamic_slice_in_dim(a, which * part, part, 1)
+        return jnp.concatenate([cut(q0[0]), cut(keys[0]), cut(values[0]), tail], axis=0)
+
+    mine, message = side(c), side(1 - c)
+    packed = call(
+        pack_rows_kernel, shape((half, width), BF16), (counts, grad_here, extra), smem=(0,)
+    )
+    packed, near_weight, message = after((packed, near_weight, message))
     message = over_y(message)
-    near_weight = over_core(out_weight)
-    packed = call(pack_rows_kernel, shape((half, width), BF16), (counts, grad, extra), smem=(0,))
-    blocks = [
-        lax.ppermute(packed, ("tensor", "fsdp"), spread(a, b)) for a in (0, 1) for b in (0, 1)
-    ]
+    first, second = [lax.ppermute(packed, ("tensor", "fsdp"), spread(a)) for a in (0, 1)]
+    over_z = lambda a: lax.ppermute(a, "tensor", [(i, i ^ 1) for i in range(4)])
+    blocks = [first, over_z(first), second, over_z(second)]
     q, k, v, probs, output = call(
         forward_kernel,
         (
@@ -288,41 +305,57 @@
             shape((heads, total, total), F32),
             shape((total, part), BF16),
         ),
-        (counts, slopes, queries[0], keys[0], values[0], gaps, message),
+        (counts, slopes, mine, message),
         smem=(0, 1),
     )
     peer_output = over_y(output)
-    partial, send, own_g, near_g = call(
+    peer_first, peer_second = over_y(blocks[0]), over_y(blocks[2])
+    *blocks, output = after((*blocks, output))
+    keep, send_x, send_y, send_xy, own_g, near_g = call(
         partial_kernel,
         (
-            shape((half, width), F32),
-            shape((half, width), BF16),
+            shape((half, part), F32),
+            shape((half, part), BF16),
+            shape((half, part), BF16),
+            shape((half, part), BF16),
             shape((total, width), BF16),
             shape((total, width), BF16),
         ),
-        (*blocks, out_weight, near_weight),
-    )
-    arrived = over_x(send)
+        (*blocks, own_weight, near_weight),
+        scratch=(pltpu.VMEM((total, width), F32),),
+    )
+    from_xy = lax.ppermute(
+        send_xy,
+        ("context", "fsdp"),
+        [(c * 4 + f, (1 - c) * 4 + (f ^ 2)) for c in range(2) for f in range(4)],
+    )
+    from_x, from_y = over_x(send_x), over_y(send_y)
     near_g = over_core(near_g)
-    both = jnp.concatenate([output, peer_output], axis=0)
-    out_a = jnp.concatenate([both, over_x(both)], axis=0)
-    out_b = over_core(out_a)
-    c = lax.axis_index("context")
-    away = (1 - c) * part
-    here = lax.dynamic_slice_in_dim(partial, away, part, 1) + lax.dynamic_slice_in_dim(
-        arrived, away, part, 1
-    ).astype(F32)
-    peer_head = over_y(here.astype(BF16))
-    peer_g = over_y(jnp.concatenate([own_g, near_g], axis=0))
+    mine_x = over_x(output)
+    mine_core = over_core(jnp.concatenate([output, mine_x], axis=0))
+    from_x, from_y, from_xy, peer_output = after((from_x, from_y, from_xy, peer_output))
+    away_x = over_x(peer_output)
+    peer_blocks = [peer_first, over_z(peer_first), peer_second, over_z(peer_second)]
     own, send = call(
         backward_kernel,
         (shape((3 * rows, part), BF16), shape((3 * rows, part), BF16)),
-        (counts, q, k, v, probs, output, partial, arrived, peer_head),
+        (counts, q, k, v, probs, output, keep, from_x, from_y, from_xy),
         smem=(0,),
         scratch=(pltpu.VMEM((total, part), BF16), pltpu.VMEM((3, total, part), BF16)),
     )
     peer = over_y(send)
-    weight_grad = weight_gradient(own_g, near_g, peer_g, out_a, out_b)
+    peer_blocks = after((send, *peer_blocks))[1:]
+    own_p, near_p = call(
+        place_kernel, (shape((total, width), BF16), shape((total, width), BF16)), peer_blocks
+    )
+    near_p = over_core(near_p)
+    own_g, away_x = after((send, own_g, away_x))[1:]
+    away_core = over_core(jnp.concatenate([peer_output, away_x], axis=0))
+    weight_grad = weight_gradient(
+        (own_g, near_g, own_p, near_p),
+        (output, mine_x, mine_core, peer_output, away_x, away_core),
+    )
+    weight_grad, own = after((weight_grad, own))
     grads = call(finish_kernel, tuple(shape((rows, width), BF16) for _ in range(3)), (own, peer))
     return (grads[0][None], grads[1][None], grads[2][None], weight_grad)
 

time: 91.6 us -> 59.4 us (0.65)
  waiting for transfers between devices: 51 us -> 18.2 us
  starting transfers between devices: 20.5 us -> 25 us
  local copies, waits for them, and re-layouts: 6.17 us -> 4.12 us
  Pallas kernels: 11.3 us -> 9.63 us
    ppermute x6 -> x7, waiting for transfers between devices: 37 us -> 3.42 us  [packed_device(): over_y = lambda a: lax.ppermute(a, 'context', [(0, 1), (1, 0)])]
    ppermute x2 -> x3, waiting for transfers between devices: 8.75 us -> 1.07 us  [packed_device(): over_x = lambda a: lax.ppermute(a, 'fsdp', [(i, i ^ 2) for i in range(4)])]
    ppermute x4 -> x7, waiting for transfers between devices: 5.19 us -> 12.1 us  [the longest x4 5.44 us: packed_device(): over_z = lambda a: lax.ppermute(a, 'tensor', [(i, i ^ 1) for i in range(4)])]
    ppermute x4 -> x7, starting transfers between devices: 6.24 us -> 12.5 us  [the longest x4 6.99 us: packed_device(): over_z = lambda a: lax.ppermute(a, 'tensor', [(i, i ^ 1) for i in range(4)])]
    unnamed x24 -> x4, local copies, waits for them, and re-layouts: 6.14 us -> 0.01 us
    dynamic_slice x0 -> x2, local copies, waits for them, and re-layouts: none -> 2.28 us  [side(): cut = lambda a: lax.dynamic_slice_in_dim(a, which * part, part, 1)]
    slice x1 -> x2, local copies, waits for them, and re-layouts: 0.01 us -> 1.83 us  [the longest x1 0.93 us: packed_device(): own_weight, grad_here = (out_weight, grad[:half])]
    ppermute x3 -> x5, waiting for transfers between devices: 0.01 us -> 1.6 us  [packed_device(): lax.ppermute(a, 'fsdp', [(i, i ^ 1) for i in range(4)])]
  transfers between devices with their start and end apart: 15 -> 22, of which waited for: 9 -> 9; matrix products, arithmetic and copies ran while one was open for 1% -> 7% of each run, Pallas kernels for 7% -> 15%
where the time goes in v2:
time: 59.4 us; the launch traced here: 59.2 us
  starting transfers between devices  25 us (42%)
  waiting for transfers between devices  18.2 us (31%)
  Pallas kernels  9.63 us (16%)
  local copies, waits for them, and re-layouts  4.12 us (7%)
  between operations  1.44 us (2%)
  other arithmetic  0.76 us (1%)
    ppermute x7, starting transfers between devices, packed_device(): over_y = lambda a: lax.ppermute(a, 'context', [(0, 1), (1, 0)])  7.97 us
    ppermute x4, starting transfers between devices, packed_device(): over_z = lambda a: lax.ppermute(a, 'tensor', [(i, i ^ 1) for i in range(4)])  6.99 us
    pallas_call x6, Pallas kernels, call(): pl.pallas_call(body, out_shape=outs, in_specs=[pl.BlockSpec(memory_space=...  5.57 us
    ppermute x4, waiting for transfers between devices, packed_device(): over_z = lambda a: lax.ppermute(a, 'tensor', [(i, i ^ 1) for i in range(4)])  5.44 us
    pallas_call x1, Pallas kernels, weight_gradient(): pl.pallas_call(weight_kernel, grid=(blocks,), out_shape=jax.ShapeDtypeStr...  4.05 us
    ppermute x1, waiting for transfers between devices, packed_device(): lax.ppermute(send_xy, ('context', 'fsdp'), [(c * 4 + f, (1 - c) * 4 + (f...  3.83 us
    ppermute x7, waiting for transfers between devices, packed_device(): over_y = lambda a: lax.ppermute(a, 'context', [(0, 1), (1, 0)])  3.42 us
    ppermute x3, starting transfers between devices, packed_device(): over_x = lambda a: lax.ppermute(a, 'fsdp', [(i, i ^ 2) for i in range(4)])  3.36 us
  transfers between devices with their start and end apart: 22, of which 9 were waited for; matrix products, arithmetic and copies ran while one was open for 7% of the time, Pallas kernels for 15%

profile of v2, /device:TPU:0, one launch (start us, length us, event | category | flops | bytes accessed | tf_op | source)
XLA Modules:
  0.0 59.2 jit_solution(2882230350487659774)
XLA Ops:
  0.6 0.9 %slice_bitcast_fusion.1 = bf16[48,1024]{1,0:T(8,128)(2,1)S(1)} fusion(bf16[1,128,1024]{2,1,0:T(8,128)(2,1)} %param.11), kind=kLoop, calls=%fused_computation.12 | loop fusion | bytes 196608 | tf_op jit(solution)/shard_map/slice | solution.py:277
  2.0 2.6 %collective-permute-start = (bf16[48,1024]{1,0:T(8,128)(2,1)S(1)}, bf16[48,1024]{1,0:T(8,128)(2,1)S(1)}, u32[]{:S(2)}, u32[]{:S(2)}) collective-permute-start(bf16[48,1024]{1,0:T(8,128)(2,1)S(1)} %slice_bitcast_fusion.1), channel_id=1, source_target_pairs={{0,16},{16,0},{1,17},{17,1},{2,18},{18,2},{3,19},{19,3},{4,20},{20... | collective-permute-start | bytes 294920 | tf_op jit(solution)/shard_map/ppermute | solution.py:271
  5.2 1.0 %dynamic-slice_bitcast_fusion.2 = (bf16[128,512]{1,0:T(8,128)(2,1)S(1)}, bf16[128,512]{1,0:T(8,128)(2,1)S(1)}) fusion(bf16[1,128,1024]{2,1,0:T(8,128)(2,1)} %param.8, s32[]{:T(128)S(6)} %select_n.5, s32[]{:T(128)S(6)} %select_n.4), kind=kLoop, calls=%fused_computation.8 | loop fusion | bytes 524296 | tf_op jit(solution)/shard_map/dynamic_slice | solution.py:287
  6.2 1.3 %dynamic-slice_bitcast_fusion = (bf16[128,512]{1,0:T(8,128)(2,1)S(1)}, bf16[128,512]{1,0:T(8,128)(2,1)S(1)}, bf16[128,512]{1,0:T(8,128)(2,1)S(1)}, bf16[128,512]{1,0:T(8,128)(2,1)S(1)}) fusion(bf16[1,128,1024]{2,1,0:T(8,128)(2,1)} %param.10, s32[]{:T(128)S(6)} %select_n.5, s32[]{:T(128)S(6)} %select_n.4, bf16[1,128,1024]{2,1,0:T(8,128)(2,1)} %param.9), kind=kLoop, calls=%fused_computation.6 | loop fusion | bytes 1048584 | tf_op jit(solution)/shard_map/dynamic_slice | solution.py:287
  7.5 0.7 %convert_bitcast_fusion = bf16[128]{0:T(256)(128)(2,1)S(1)} fusion(s32[1,128]{1,0:T(1,128)} %param.15), kind=kLoop, calls=%fused_computation.13 | loop fusion | flops 128 | bytes 768 | tf_op jit(solution)/shard_map/broadcast_in_dim | solution.py:283
  8.2 0.9 %slice_bitcast_fusion.own_ref = bf16[80,1024]{1,0:T(8,128)(2,1)S(1)} fusion(bf16[1,128,1024]{2,1,0:T(8,128)(2,1)} %param.11), kind=kLoop, calls=%fused_computation.5 | loop fusion | bytes 327680 | tf_op jit(solution)/shard_map/slice | solution.py:281
  9.4 0.6 collective-permute-start.2
  10.0 2.6 %collective-permute-start.5 = (bf16[80,1024]{1,0:T(8,128)(2,1)S(1)}, bf16[80,1024]{1,0:T(8,128)(2,1)S(1)}, u32[]{:S(2)}, u32[]{:S(2)}) collective-permute-start(bf16[80,1024]{1,0:T(8,128)(2,1)S(1)} %shard_map.111), channel_id=1, source_target_pairs={{0,8},{1,9},{2,0},{3,1},{4,12},{5,13},{6,4},{7,5},{8,10},{9,11},{1... | collective-permute-start | bytes 491528 | tf_op jit(solution)/shard_map/ppermute | solution.py:296
  12.6 0.7 %collective-permute-start.3 = (bf16[80,1024]{1,0:T(8,128)(2,1)S(1)}, bf16[80,1024]{1,0:T(8,128)(2,1)S(1)}, u32[]{:S(2)}, u32[]{:S(2)}) collective-permute-start(bf16[80,1024]{1,0:T(8,128)(2,1)S(1)} %shard_map.111), channel_id=1, source_target_pairs={{0,0},{1,1},{2,8},{3,9},{4,4},{5,5},{6,12},{7,13},{8,2},{9,3},{10,... | collective-permute-start | bytes 491528 | tf_op jit(solution)/shard_map/ppermute | solution.py:296
  13.3 2.9 %collective-permute-done.5.b10_ref = bf16[80,1024]{1,0:T(8,128)(2,1)S(1)} collective-permute-done((bf16[80,1024]{1,0:T(8,128)(2,1)S(1)}, bf16[80,1024]{1,0:T(8,128)(2,1)S(1)}, u32[]{:S(2)}, u32[]{:S(2)}) %collective-permute-start.5) | collective-permute-done | bytes 163872 | tf_op jit(solution)/shard_map/ppermute | solution.py:296
  16.2 4.9 %collective-permute-start.6 = (bf16[80,1024]{1,0:T(8,128)(2,1)S(1)}, bf16[80,1024]{1,0:T(8,128)(2,1)S(1)}, u32[]{:S(2)}, u32[]{:S(2)}) collective-permute-start(bf16[80,1024]{1,0:T(8,128)(2,1)S(1)} %collective-permute-done.5.b10_ref), channel_id=1, source_target_pairs={{0,4},{4,0},{8,12},{12,8},{1,5},{5,1},{9,13},{13,9},{2,6},{6,2},{1... | collective-permute-start | bytes 491528 | tf_op jit(solution)/shard_map/ppermute | solution.py:297
  21.1 1.5 %collective-permute-start.15 = (bf16[80,1024]{1,0:T(8,128)(2,1)S(1)}, bf16[80,1024]{1,0:T(8,128)(2,1)S(1)}, u32[]{:S(2)}, u32[]{:S(2)}) collective-permute-start(bf16[80,1024]{1,0:T(8,128)(2,1)S(1)} %collective-permute-done.5.b10_ref), channel_id=1, source_target_pairs={{0,16},{16,0},{1,17},{17,1},{2,18},{18,2},{3,19},{19,3},{4,20},{20... | collective-permute-start | bytes 491528 | tf_op jit(solution)/shard_map/ppermute | solution.py:271
  22.6 0.5 collective-permute-start.13
  23.2 1.9 %shard_map.112 = (bf16[160,512]{1,0:T(8,128)(2,1)S(1)}, bf16[160,512]{1,0:T(8,128)(2,1)S(1)}, bf16[160,512]{1,0:T(8,128)(2,1)S(1)}, f32[4,160,160]{2,1,0:T(8,128)S(1)}, bf16[160,512]{1,0:T(8,128)(2,1)S(1)}) custom-call(s32[1,1]{1,0:T(1,128)S(6)} %copy.12.count_ref, f32[8]{0:T(128)S(1)} %copy-done.1, bf16[400,512]{1,0:T(8,128)(2,1)S(1)} %get-tuple-element.93.mine_ref, ...), custom_call_target="tpu_custom_call" | custom-call | tf_op jit(solution)/shard_map/pallas_call | solution.py:32
  25.1 2.0 %collective-permute-done.6.b11_ref = bf16[80,1024]{1,0:T(8,128)(2,1)S(1)} collective-permute-done((bf16[80,1024]{1,0:T(8,128)(2,1)S(1)}, bf16[80,1024]{1,0:T(8,128)(2,1)S(1)}, u32[]{:S(2)}, u32[]{:S(2)}) %collective-permute-start.6) | collective-permute-done | bytes 163872 | tf_op jit(solution)/shard_map/ppermute | solution.py:297
  27.0 3.5 %collective-permute-done.4.b01_ref = bf16[80,1024]{1,0:T(8,128)(2,1)S(1)} collective-permute-done((bf16[80,1024]{1,0:T(8,128)(2,1)S(1)}, bf16[80,1024]{1,0:T(8,128)(2,1)S(1)}, u32[]{:S(2)}, u32[]{:S(2)}) %collective-permute-start.4) | collective-permute-done | bytes 163872 | tf_op jit(solution)/shard_map/ppermute | solution.py:297
  30.5 1.0 %shard_map.113 = (f32[80,512]{1,0:T(8,128)S(1)}, bf16[80,512]{1,0:T(8,128)(2,1)S(1)}, bf16[80,512]{1,0:T(8,128)(2,1)S(1)}, bf16[80,512]{1,0:T(8,128)(2,1)S(1)}, ...) custom-call(bf16[80,1024]{1,0:T(8,128)(2,1)S(1)} %collective-permute-done.3.b00_ref, ...), custom_call_target="tpu_custom_call" | custom-call | tf_op jit(solution)/shard_map/pallas_call | solution.py:32
  31.8 1.5 %collective-permute-start.8 = (bf16[80,512]{1,0:T(8,128)(2,1)S(1)}, bf16[80,512]{1,0:T(8,128)(2,1)S(1)}, u32[]{:S(2)}, u32[]{:S(2)}) collective-permute-start(bf16[80,512]{1,0:T(8,128)(2,1)S(1)} %get-tuple-element.63), channel_id=1, source_target_pairs={{0,16},{16,0},{1,17},{17,1},{2,18},{18,2},{3,19},{19,3},{4,20},{20... | collective-permute-start | bytes 245768 | tf_op jit(solution)/shard_map/ppermute | solution.py:271
  33.3 0.5 collective-permute-start.10
  33.8 1.1 %collective-permute-start.16 = (bf16[80,1024]{1,0:T(8,128)(2,1)S(1)}, bf16[80,1024]{1,0:T(8,128)(2,1)S(1)}, u32[]{:S(2)}, u32[]{:S(2)}) collective-permute-start(bf16[80,1024]{1,0:T(8,128)(2,1)S(1)} %collective-permute-done.15.b10_ref), channel_id=1, source_target_pairs={{0,4},{4,0},{8,12},{12,8},{1,5},{5,1},{9,13},{13,9},{2,6},{6,2},{1... | collective-permute-start | bytes 491528 | tf_op jit(solution)/shard_map/ppermute | solution.py:297
  34.9 1.0 %collective-permute-start.14 = (bf16[80,1024]{1,0:T(8,128)(2,1)S(1)}, bf16[80,1024]{1,0:T(8,128)(2,1)S(1)}, u32[]{:S(2)}, u32[]{:S(2)}) collective-permute-start(bf16[80,1024]{1,0:T(8,128)(2,1)S(1)} %collective-permute-done.13.b00_ref), channel_id=1, source_target_pairs={{0,4},{4,0},{8,12},{12,8},{1,5},{5,1},{9,13},{13,9},{2,6},{6,2},{1... | collective-permute-start | bytes 491528 | tf_op jit(solution)/shard_map/ppermute | solution.py:297
  36.0 1.6 %collective-permute-start.18 = (bf16[160,512]{1,0:T(8,128)(2,1)S(1)}, bf16[160,512]{1,0:T(8,128)(2,1)S(1)}, u32[]{:S(2)}, u32[]{:S(2)}) collective-permute-start(bf16[160,512]{1,0:T(8,128)(2,1)S(1)} %get-tuple-element.55.output_ref.mine_ref), channel_id=1, source_target_pairs={{0,2},{1,3},{2,0},{3,1},{4,6},{5,7},{6,4},{7,5},{8,10},{9,11},{10,... | collective-permute-start | bytes 491528 | tf_op jit(solution)/shard_map/ppermute | solution.py:272
  37.7 2.3 %collective-permute-start.9 = (bf16[80,512]{1,0:T(8,128)(2,1)S(1)}, bf16[80,512]{1,0:T(8,128)(2,1)S(1)}, u32[]{:S(2)}, u32[]{:S(2)}) collective-permute-start(bf16[80,512]{1,0:T(8,128)(2,1)S(1)} %get-tuple-element.64), channel_id=1, source_target_pairs={{0,18},{1,19},{2,16},{3,17},{16,2},{17,3},{18,0},{19,1},{4,22},{5,... | collective-permute-start | bytes 245768 | tf_op jit(solution)/shard_map/ppermute | solution.py:327
  39.9 3.8 %collective-permute-done.9.from_xy_ref = bf16[80,512]{1,0:T(8,128)(2,1)S(1)} collective-permute-done((bf16[80,512]{1,0:T(8,128)(2,1)S(1)}, bf16[80,512]{1,0:T(8,128)(2,1)S(1)}, u32[]{:S(2)}, u32[]{:S(2)}) %collective-permute-start.9) | collective-permute-done | bytes 81952 | tf_op jit(solution)/shard_map/ppermute | solution.py:327
  43.7 1.4 %collective-permute-start.11 = (bf16[160,512]{1,0:T(8,128)(2,1)S(1)}, bf16[160,512]{1,0:T(8,128)(2,1)S(1)}, u32[]{:S(2)}, u32[]{:S(2)}) collective-permute-start(bf16[160,512]{1,0:T(8,128)(2,1)S(1)} %collective-permute-done.10.away_ref), channel_id=1, source_target_pairs={{0,2},{1,3},{2,0},{3,1},{4,6},{5,7},{6,4},{7,5},{8,10},{9,11},{10,... | collective-permute-start | bytes 491528 | tf_op jit(solution)/shard_map/ppermute | solution.py:272
  45.1 1.5 %shard_map.114 = (bf16[384,512]{1,0:T(8,128)(2,1)S(1)}, bf16[384,512]{1,0:T(8,128)(2,1)S(1)}) custom-call(s32[1,1]{1,0:T(1,128)S(6)} %copy.12.count_ref, bf16[160,512]{1,0:T(8,128)(2,1)S(1)} %get-tuple-element.49.q_ref, bf16[160,512]{1,0:T(8,128)(2,1)S(1)} %get-tuple-element.50.k_ref, bf16[160,512]{1,0:T(8,128)(2,1)S(1)} %get-tuple-element.51.v_ref, ...), custom_call_target="tpu_custom_call" | custom-call | tf_op jit(solution)/shard_map/pallas_call | solution.py:32
  46.6 0.7 %collective-permute-start.21 = (bf16[384,512]{1,0:T(8,128)(2,1)S(1)}, bf16[384,512]{1,0:T(8,128)(2,1)S(1)}, u32[]{:S(2)}, u32[]{:S(2)}) collective-permute-start(bf16[384,512]{1,0:T(8,128)(2,1)S(1)} %get-tuple-element.68), channel_id=1, source_target_pairs={{0,16},{16,0},{1,17},{17,1},{2,18},{18,2},{3,19},{19,3},{4,20},{20... | collective-permute-start | bytes 1179656 | tf_op jit(solution)/shard_map/ppermute | solution.py:271
  48.1 0.9 %collective-permute-done.11.away_x_ref = bf16[160,512]{1,0:T(8,128)(2,1)S(1)} collective-permute-done((bf16[160,512]{1,0:T(8,128)(2,1)S(1)}, bf16[160,512]{1,0:T(8,128)(2,1)S(1)}, u32[]{:S(2)}, u32[]{:S(2)}) %collective-permute-start.11) | collective-permute-done | bytes 163872 | tf_op jit(solution)/shard_map/ppermute | solution.py:272
  49.6 1.2 %collective-permute-done.20.away_core_ref = bf16[320,512]{1,0:T(8,128)(2,1)S(1)} collective-permute-done((bf16[320,512]{1,0:T(8,128)(2,1)S(1)}, bf16[320,512]{1,0:T(8,128)(2,1)S(1)}, u32[]{:S(2)}, u32[]{:S(2)}) %collective-permute-start.20) | collective-permute-done | bytes 327712 | tf_op jit(solution)/shard_map/ppermute | solution.py:273
  50.8 4.1 %shard_map.116 = f32[1024,1024]{1,0:T(8,128)} custom-call(bf16[160,1024]{1,0:T(8,128)(2,1)S(1)} %get-tuple-element.71.own_g_ref, bf16[160,1024]{1,0:T(8,128)(2,1)S(1)} %collective-permute-done.12.near_g_ref, bf16[160,1024]{1,0:T(8,128)(2,1)S(1)} %get-tuple-element.77.own_p_ref, bf16[160,1024]{1,0:T(8,128)(2,1)S(1)} %collective-permute-done.17.near_p_ref, ...), custom_call_target="tpu_custom_call" | custom-call | tf_op jit(solution)/shard_map/pallas_call | solution.py:243
  54.8 3.4 %collective-permute-done.21.peer_ref = bf16[384,512]{1,0:T(8,128)(2,1)S(1)} collective-permute-done((bf16[384,512]{1,0:T(8,128)(2,1)S(1)}, bf16[384,512]{1,0:T(8,128)(2,1)S(1)}, u32[]{:S(2)}, u32[]{:S(2)}) %collective-permute-start.21) | collective-permute-done | bytes 393248 | tf_op jit(solution)/shard_map/ppermute | solution.py:271
  58.2 0.9 %shard_map.117 = (bf16[128,1024]{1,0:T(8,128)(2,1)}, bf16[128,1024]{1,0:T(8,128)(2,1)}, bf16[128,1024]{1,0:T(8,128)(2,1)}) custom-call(bf16[384,512]{1,0:T(8,128)(2,1)S(1)} %get-tuple-element.81.own_ref, bf16[384,512]{1,0:T(8,128)(2,1)S(1)} %collective-permute-done.21.peer_ref), custom_call_target="tpu_custom_call" | custom-call | tf_op jit(solution)/shard_map/pallas_call | solution.py:32
  (32 shorter events, 2.5 us)
Async XLA Ops:
  0.6 22.5 %copy-start.1 = (f32[8]{0:T(128)S(1)}, f32[8]{0:T(128)}, u32[]{:S(2)}) copy-start(f32[8]{0:T(128)} %slopes_ref.1) | copy-start | bytes 100
  1.5 7.9 %collective-permute-start.1 = (bf16[1024,1024]{1,0:T(8,128)(2,1)}, bf16[1024,1024]{1,0:T(8,128)(2,1)S(1)}, u32[]{:S(2)}, u32[]{:S(2)}) collective-permute-start(bf16[1024,1024]{1,0:T(8,128)(2,1)} %own_w_ref.1), channel_id=1, source_target_pairs={{0,1},{1,0},{2,3},{3,2},{4,5},{5,4},{6,7},{7,6},{8,9},{9,8},{10,11... | collective-permute-start | bytes 6291464 | tf_op jit(solution)/shard_map/ppermute | solution.py:273
  2.0 7.2 %collective-permute-start = (bf16[48,1024]{1,0:T(8,128)(2,1)S(1)}, bf16[48,1024]{1,0:T(8,128)(2,1)S(1)}, u32[]{:S(2)}, u32[]{:S(2)}) collective-permute-start(bf16[48,1024]{1,0:T(8,128)(2,1)S(1)} %slice_bitcast_fusion.1), channel_id=1, source_target_pairs={{0,16},{16,0},{1,17},{17,1},{2,18},{18,2},{3,19},{19,3},{4,20},{20... | collective-permute-start | bytes 294920 | tf_op jit(solution)/shard_map/ppermute | solution.py:271
  6.2 24.3 %copy-start = (bf16[1024,1024]{1,0:T(8,128)(2,1)S(1)}, bf16[1024,1024]{1,0:T(8,128)(2,1)}, u32[]{:S(2)}) copy-start(bf16[1024,1024]{1,0:T(8,128)(2,1)} %own_w_ref.1) | copy-start | bytes 6291460
  9.4 13.7 %collective-permute-start.2 = (bf16[400,512]{1,0:T(8,128)(2,1)S(1)}, bf16[400,512]{1,0:T(8,128)(2,1)S(1)}, u32[]{:S(2)}, u32[]{:S(2)}) collective-permute-start(bf16[400,512]{1,0:T(8,128)(2,1)S(1)} %get-tuple-element.48), channel_id=1, source_target_pairs={{0,16},{16,0},{1,17},{17,1},{2,18},{18,2},{3,19},{19,3},{4,20},{20... | collective-permute-start | bytes 1228808 | tf_op jit(solution)/shard_map/ppermute | solution.py:271
  10.0 6.1 %collective-permute-start.5 = (bf16[80,1024]{1,0:T(8,128)(2,1)S(1)}, bf16[80,1024]{1,0:T(8,128)(2,1)S(1)}, u32[]{:S(2)}, u32[]{:S(2)}) collective-permute-start(bf16[80,1024]{1,0:T(8,128)(2,1)S(1)} %shard_map.111), channel_id=1, source_target_pairs={{0,8},{1,9},{2,0},{3,1},{4,12},{5,13},{6,4},{7,5},{8,10},{9,11},{1... | collective-permute-start | bytes 491528 | tf_op jit(solution)/shard_map/ppermute | solution.py:296
  12.6 8.5 %collective-permute-start.3 = (bf16[80,1024]{1,0:T(8,128)(2,1)S(1)}, bf16[80,1024]{1,0:T(8,128)(2,1)S(1)}, u32[]{:S(2)}, u32[]{:S(2)}) collective-permute-start(bf16[80,1024]{1,0:T(8,128)(2,1)S(1)} %shard_map.111), channel_id=1, source_target_pairs={{0,0},{1,1},{2,8},{3,9},{4,4},{5,5},{6,12},{7,13},{8,2},{9,3},{10,... | collective-permute-start | bytes 491528 | tf_op jit(solution)/shard_map/ppermute | solution.py:296
  16.2 10.9 %collective-permute-start.6 = (bf16[80,1024]{1,0:T(8,128)(2,1)S(1)}, bf16[80,1024]{1,0:T(8,128)(2,1)S(1)}, u32[]{:S(2)}, u32[]{:S(2)}) collective-permute-start(bf16[80,1024]{1,0:T(8,128)(2,1)S(1)} %collective-permute-done.5.b10_ref), channel_id=1, source_target_pairs={{0,4},{4,0},{8,12},{12,8},{1,5},{5,1},{9,13},{13,9},{2,6},{6,2},{1... | collective-permute-start | bytes 491528 | tf_op jit(solution)/shard_map/ppermute | solution.py:297
  21.1 9.4 %collective-permute-start.4 = (bf16[80,1024]{1,0:T(8,128)(2,1)S(1)}, bf16[80,1024]{1,0:T(8,128)(2,1)S(1)}, u32[]{:S(2)}, u32[]{:S(2)}) collective-permute-start(bf16[80,1024]{1,0:T(8,128)(2,1)S(1)} %collective-permute-done.3.b00_ref), channel_id=1, source_target_pairs={{0,4},{4,0},{8,12},{12,8},{1,5},{5,1},{9,13},{13,9},{2,6},{6,2},{1... | collective-permute-start | bytes 491528 | tf_op jit(solution)/shard_map/ppermute | solution.py:297
  21.1 12.7 %collective-permute-start.15 = (bf16[80,1024]{1,0:T(8,128)(2,1)S(1)}, bf16[80,1024]{1,0:T(8,128)(2,1)S(1)}, u32[]{:S(2)}, u32[]{:S(2)}) collective-permute-start(bf16[80,1024]{1,0:T(8,128)(2,1)S(1)} %collective-permute-done.5.b10_ref), channel_id=1, source_target_pairs={{0,16},{16,0},{1,17},{17,1},{2,18},{18,2},{3,19},{19,3},{4,20},{20... | collective-permute-start | bytes 491528 | tf_op jit(solution)/shard_map/ppermute | solution.py:271
  22.6 12.3 %collective-permute-start.13 = (bf16[80,1024]{1,0:T(8,128)(2,1)S(1)}, bf16[80,1024]{1,0:T(8,128)(2,1)S(1)}, u32[]{:S(2)}, u32[]{:S(2)}) collective-permute-start(bf16[80,1024]{1,0:T(8,128)(2,1)S(1)} %collective-permute-done.3.b00_ref), channel_id=1, source_target_pairs={{0,16},{16,0},{1,17},{17,1},{2,18},{18,2},{3,19},{19,3},{4,20},{20... | collective-permute-start | bytes 491528 | tf_op jit(solution)/shard_map/ppermute | solution.py:271
  31.5 4.5 %collective-permute-start.7 = (bf16[80,512]{1,0:T(8,128)(2,1)S(1)}, bf16[80,512]{1,0:T(8,128)(2,1)S(1)}, u32[]{:S(2)}, u32[]{:S(2)}) collective-permute-start(bf16[80,512]{1,0:T(8,128)(2,1)S(1)} %get-tuple-element.62), channel_id=1, source_target_pairs={{0,2},{1,3},{2,0},{3,1},{4,6},{5,7},{6,4},{7,5},{8,10},{9,11},{10,... | collective-permute-start | bytes 245768 | tf_op jit(solution)/shard_map/ppermute | solution.py:272
  31.8 5.8 %collective-permute-start.8 = (bf16[80,512]{1,0:T(8,128)(2,1)S(1)}, bf16[80,512]{1,0:T(8,128)(2,1)S(1)}, u32[]{:S(2)}, u32[]{:S(2)}) collective-permute-start(bf16[80,512]{1,0:T(8,128)(2,1)S(1)} %get-tuple-element.63), channel_id=1, source_target_pairs={{0,16},{16,0},{1,17},{17,1},{2,18},{18,2},{3,19},{19,3},{4,20},{20... | collective-permute-start | bytes 245768 | tf_op jit(solution)/shard_map/ppermute | solution.py:271
  33.3 10.4 %collective-permute-start.10 = (bf16[160,512]{1,0:T(8,128)(2,1)S(1)}, bf16[160,512]{1,0:T(8,128)(2,1)S(1)}, u32[]{:S(2)}, u32[]{:S(2)}) collective-permute-start(bf16[160,512]{1,0:T(8,128)(2,1)S(1)} %get-tuple-element.55.output_ref.mine_ref), channel_id=1, source_target_pairs={{0,16},{16,0},{1,17},{17,1},{2,18},{18,2},{3,19},{19,3},{4,20},{20... | collective-permute-start | bytes 491528 | tf_op jit(solution)/shard_map/ppermute | solution.py:271
  33.8 12.8 %collective-permute-start.16 = (bf16[80,1024]{1,0:T(8,128)(2,1)S(1)}, bf16[80,1024]{1,0:T(8,128)(2,1)S(1)}, u32[]{:S(2)}, u32[]{:S(2)}) collective-permute-start(bf16[80,1024]{1,0:T(8,128)(2,1)S(1)} %collective-permute-done.15.b10_ref), channel_id=1, source_target_pairs={{0,4},{4,0},{8,12},{12,8},{1,5},{5,1},{9,13},{13,9},{2,6},{6,2},{1... | collective-permute-start | bytes 491528 | tf_op jit(solution)/shard_map/ppermute | solution.py:297
  34.9 12.5 %collective-permute-start.14 = (bf16[80,1024]{1,0:T(8,128)(2,1)S(1)}, bf16[80,1024]{1,0:T(8,128)(2,1)S(1)}, u32[]{:S(2)}, u32[]{:S(2)}) collective-permute-start(bf16[80,1024]{1,0:T(8,128)(2,1)S(1)} %collective-permute-done.13.b00_ref), channel_id=1, source_target_pairs={{0,4},{4,0},{8,12},{12,8},{1,5},{5,1},{9,13},{13,9},{2,6},{6,2},{1... | collective-permute-start | bytes 491528 | tf_op jit(solution)/shard_map/ppermute | solution.py:297
  36.0 11.4 %collective-permute-start.18 = (bf16[160,512]{1,0:T(8,128)(2,1)S(1)}, bf16[160,512]{1,0:T(8,128)(2,1)S(1)}, u32[]{:S(2)}, u32[]{:S(2)}) collective-permute-start(bf16[160,512]{1,0:T(8,128)(2,1)S(1)} %get-tuple-element.55.output_ref.mine_ref), channel_id=1, source_target_pairs={{0,2},{1,3},{2,0},{3,1},{4,6},{5,7},{6,4},{7,5},{8,10},{9,11},{10,... | collective-permute-start | bytes 491528 | tf_op jit(solution)/shard_map/ppermute | solution.py:272
  37.7 6.1 %collective-permute-start.9 = (bf16[80,512]{1,0:T(8,128)(2,1)S(1)}, bf16[80,512]{1,0:T(8,128)(2,1)S(1)}, u32[]{:S(2)}, u32[]{:S(2)}) collective-permute-start(bf16[80,512]{1,0:T(8,128)(2,1)S(1)} %get-tuple-element.64), channel_id=1, source_target_pairs={{0,18},{1,19},{2,16},{3,17},{16,2},{17,3},{18,0},{19,1},{4,22},{5,... | collective-permute-start | bytes 245768 | tf_op jit(solution)/shard_map/ppermute | solution.py:327
  43.7 5.3 %collective-permute-start.11 = (bf16[160,512]{1,0:T(8,128)(2,1)S(1)}, bf16[160,512]{1,0:T(8,128)(2,1)S(1)}, u32[]{:S(2)}, u32[]{:S(2)}) collective-permute-start(bf16[160,512]{1,0:T(8,128)(2,1)S(1)} %collective-permute-done.10.away_ref), channel_id=1, source_target_pairs={{0,2},{1,3},{2,0},{3,1},{4,6},{5,7},{6,4},{7,5},{8,10},{9,11},{10,... | collective-permute-start | bytes 491528 | tf_op jit(solution)/shard_map/ppermute | solution.py:272
  45.1 4.0 %collective-permute-start.12 = (bf16[160,1024]{1,0:T(8,128)(2,1)S(1)}, bf16[160,1024]{1,0:T(8,128)(2,1)S(1)}, u32[]{:S(2)}, u32[]{:S(2)}) collective-permute-start(bf16[160,1024]{1,0:T(8,128)(2,1)S(1)} %get-tuple-element.72), channel_id=1, source_target_pairs={{0,1},{1,0},{2,3},{3,2},{4,5},{5,4},{6,7},{7,6},{8,9},{9,8},{10,11... | collective-permute-start | bytes 983048 | tf_op jit(solution)/shard_map/ppermute | solution.py:273
  46.6 11.6 %collective-permute-start.21 = (bf16[384,512]{1,0:T(8,128)(2,1)S(1)}, bf16[384,512]{1,0:T(8,128)(2,1)S(1)}, u32[]{:S(2)}, u32[]{:S(2)}) collective-permute-start(bf16[384,512]{1,0:T(8,128)(2,1)S(1)} %get-tuple-element.68), channel_id=1, source_target_pairs={{0,16},{16,0},{1,17},{17,1},{2,18},{18,2},{3,19},{19,3},{4,20},{20... | collective-permute-start | bytes 1179656 | tf_op jit(solution)/shard_map/ppermute | solution.py:271
  47.4 1.8 %collective-permute-start.19 = (bf16[320,512]{1,0:T(8,128)(2,1)S(1)}, bf16[320,512]{1,0:T(8,128)(2,1)S(1)}, u32[]{:S(2)}, u32[]{:S(2)}) collective-permute-start(bf16[320,512]{1,0:T(8,128)(2,1)S(1)} %pad_maximum_fusion.1), channel_id=1, source_target_pairs={{0,1},{1,0},{2,3},{3,2},{4,5},{5,4},{6,7},{7,6},{8,9},{9,8},{10,11... | collective-permute-start | bytes 983048 | tf_op jit(solution)/shard_map/ppermute | solution.py:273
  47.8 1.8 %collective-permute-start.17 = (bf16[160,1024]{1,0:T(8,128)(2,1)S(1)}, bf16[160,1024]{1,0:T(8,128)(2,1)S(1)}, u32[]{:S(2)}, u32[]{:S(2)}) collective-permute-start(bf16[160,1024]{1,0:T(8,128)(2,1)S(1)} %get-tuple-element.78), channel_id=1, source_target_pairs={{0,1},{1,0},{2,3},{3,2},{4,5},{5,4},{6,7},{7,6},{8,9},{9,8},{10,11... | collective-permute-start | bytes 983048 | tf_op jit(solution)/shard_map/ppermute | solution.py:273
  49.1 1.7 %collective-permute-start.20 = (bf16[320,512]{1,0:T(8,128)(2,1)S(1)}, bf16[320,512]{1,0:T(8,128)(2,1)S(1)}, u32[]{:S(2)}, u32[]{:S(2)}) collective-permute-start(bf16[320,512]{1,0:T(8,128)(2,1)S(1)} %pad_maximum_fusion.2), channel_id=1, source_target_pairs={{0,1},{1,0},{2,3},{3,2},{4,5},{5,4},{6,7},{7,6},{8,9},{9,8},{10,11... | collective-permute-start | bytes 983048 | tf_op jit(solution)/shard_map/ppermute | solution.py:273

commit v3 on v2

--- a/solution.py
+++ b/solution.py
@@ -27,13 +27,15 @@
     return jnp.where(mask, 1.0, 0.0).astype(BF16)
 
 
-def call(body, outs, args, smem=(), hbm=(), scratch=(), vmem=8):
-    where = {i: pltpu.SMEM for i in smem} | {i: pltpu.HBM for i in hbm}
+def call(body, outs, args, smem=(), out=pltpu.VMEM, scratch=(), vmem=8):
     return pl.pallas_call(
         body,
         out_shape=outs,
-        in_specs=[pl.BlockSpec(memory_space=where.get(i, pltpu.VMEM)) for i in range(len(args))],
-        out_specs=jax.tree.map(lambda _: pl.BlockSpec(memory_space=pltpu.VMEM), outs),
+        in_specs=[
+            pl.BlockSpec(memory_space=pltpu.SMEM if i in smem else pltpu.VMEM)
+            for i in range(len(args))
+        ],
+        out_specs=jax.tree.map(lambda _: pl.BlockSpec(memory_space=out), outs),
         scratch_shapes=list(scratch),
         compiler_params=pltpu.CompilerParams(vmem_limit_bytes=vmem * 2**20),
     )(*args)
@@ -44,33 +46,6 @@
     other = index - half
     own1 = jnp.where(other < count1, rows + other, half + other - count1)
     return jnp.where(index < half, own0, own1)
-
-
-def pack_message_kernel(
-    q_ref, k_ref, v_ref, grad_ref, weight_ref, gaps_ref,
-    mine_ref, away_ref, grad_here, weight_here, gaps_here, sems, others,
-):
-    rows, width = q_ref.shape
-    part = width // 2
-    c = lax.axis_index("context")
-    copies = [
-        pltpu.make_async_copy(gaps_ref, gaps_here, others.at[0]),
-        pltpu.make_async_copy(grad_ref.at[: grad_here.shape[0], :], grad_here, others.at[1]),
-        pltpu.make_async_copy(weight_ref, weight_here, others.at[2]),
-    ]
-    for side, out in enumerate((mine_ref, away_ref)):
-        at = pl.ds(pl.multiple_of((c if side == 0 else 1 - c) * part, part), part)
-        for n, ref in enumerate((q_ref, k_ref, v_ref)):
-            to = out.at[n * rows : (n + 1) * rows, :]
-            copies.append(pltpu.make_async_copy(ref.at[:, at], to, sems.at[side, n]))
-    for copy in copies:
-        copy.start()
-    for copy in copies:
-        copy.wait()
-    line = jnp.broadcast_to(gaps_here[...].astype(F32), (16, rows)).astype(BF16)
-    for out in (mine_ref, away_ref):
-        out[3 * rows :, :] = jnp.zeros((16, part), BF16)
-        out[3 * rows :, :rows] = line
 
 
 def pack_rows_kernel(count_ref, own_ref, extra_ref, out_ref):
@@ -144,8 +119,17 @@
                     near_ref[at, :] = blocks[n ^ seq][1 - chunk][...]
 
 
-def place_kernel(b00_ref, b01_ref, b10_ref, b11_ref, own_ref, near_ref):
-    place(((b00_ref, b01_ref), (b10_ref, b11_ref)), own_ref, near_ref)
+def bundle_kernel(
+    p00_ref, p01_ref, p10_ref, p11_ref, mine_ref, mine_x_ref, away_ref, away_x_ref,
+    own_p_ref, bundle_ref,
+):
+    pair, part = mine_ref.shape
+    blocks = (p00_ref, p01_ref), (p10_ref, p11_ref)
+    place(blocks, own_p_ref, bundle_ref.at[:pair])
+    bundle_ref[pair : 2 * pair, :part] = mine_ref[...]
+    bundle_ref[pair : 2 * pair, part:] = mine_x_ref[...]
+    bundle_ref[2 * pair :, :part] = away_ref[...]
+    bundle_ref[2 * pair :, part:] = away_x_ref[...]
 
 
 def partial_kernel(
@@ -166,7 +150,7 @@
 
 def backward_kernel(
     count_ref, q_ref, k_ref, v_ref, probs_ref, output_ref, keep_ref, from_x_ref, from_y_ref, from_xy_ref,
-    own_ref, send_ref, g_ref, grads_ref,
+    own_ref, send_ref, send_q_ref, g_ref, grads_ref,
 ):
     total, part = q_ref.shape
     half = total // 2
@@ -192,64 +176,62 @@
     slot = packed_slot(iota((rows, total), 1), half, rows, count0, total - count0)
     row = iota((rows, total), 0)
     own_pick, peer_pick = onehot(slot == c * rows + row), onehot(slot == (1 - c) * rows + row)
+    send_q_ref[...] = dot(peer_pick, grads_ref[0]).astype(BF16)
+    for n in range(1, 3):
+        send_ref[(n - 1) * rows : n * rows, :] = dot(peer_pick, grads_ref[n]).astype(BF16)
     for n in range(3):
-        send_ref[n * rows : (n + 1) * rows, :] = dot(peer_pick, grads_ref[n]).astype(BF16)
         own_ref[n * rows : (n + 1) * rows, :] = dot(own_pick, grads_ref[n]).astype(BF16)
 
 
-def finish_kernel(own_ref, peer_ref, q_ref, k_ref, v_ref):
+def finish_kernel(own_ref, peer_ref, peer_q_ref, q_ref, k_ref, v_ref, sems):
     rows, width = q_ref.shape
     part = width // 2
     c = lax.axis_index("context")
-    mine = pl.ds(pl.multiple_of(c * part, part), part)
-    away = pl.ds(pl.multiple_of((1 - c) * part, part), part)
-    for n, ref in enumerate((q_ref, k_ref, v_ref)):
-        ref[:, mine] = own_ref[n * rows : (n + 1) * rows, :]
-        ref[:, away] = peer_ref[n * rows : (n + 1) * rows, :]
+    copies = []
+    own = [own_ref.at[n * rows : (n + 1) * rows, :] for n in range(3)]
+    peer = [peer_q_ref, peer_ref.at[:rows, :], peer_ref.at[rows:, :]]
+    for side, sources in enumerate((own, peer)):
+        at = pl.ds(pl.multiple_of((c if side == 0 else 1 - c) * part, part), part)
+        for n, ref in enumerate((q_ref, k_ref, v_ref)):
+            copies.append(pltpu.make_async_copy(sources[n], ref.at[:, at], sems.at[side, n]))
+    for copy in copies:
+        copy.start()
+    for copy in copies:
+        copy.wait()
 
 
 def weight_kernel(
-    own_g_ref, near_g_ref, own_p_ref, near_p_ref, mine_ref, mine_x_ref, mine_core_ref,
-    away_ref, away_x_ref, away_core_ref, out_ref, right_ref, left_ref,
+    own_g_ref, near_g_ref, own_p_ref, bundle_ref, mine_ref, mine_x_ref, away_ref, away_x_ref,
+    weight_ref, left_ref, right_ref, done_ref, sems,
 ):
-    pair = own_g_ref.shape[0]
-    half = pair // 2
-    part = right_ref.shape[1] // 2
-
-    @pl.when(pl.program_id(0) == 0)
-    def _():
-        c = lax.axis_index("context")
-        sides = (mine_ref, mine_x_ref, mine_core_ref), (away_ref, away_x_ref, away_core_ref)
-        for side, refs in enumerate(sides):
-            at = pl.ds(pl.multiple_of((c if side == 0 else 1 - c) * part, part), part)
-            for s in range(4):
-                source, base = refs[min(s, 2)], 2 * half * max(s - 2, 0)
-                for which in range(2):
-                    rows = (c if which == 0 else 1 - c) * half + base
-                    to = (which * 4 + s) * half
-                    right_ref[to : to + half, at] = source[
-                        pl.ds(pl.multiple_of(rows, half), half), :
-                    ]
-
-    for n, ref in enumerate((own_g_ref, near_g_ref, own_p_ref, near_p_ref)):
-        left_ref[n * pair : (n + 1) * pair, :] = ref[...]
-    out_ref[...] = dot(left_ref[...], right_ref[...], TN)
-
-
-def weight_gradient(grads, outputs, blocks=4):
-    pair, features = grads[0].shape
-    width = 2 * outputs[0].shape[1]
-    block = features // blocks
-    return pl.pallas_call(
-        weight_kernel,
-        grid=(blocks,),
-        out_shape=jax.ShapeDtypeStruct((features, width), F32),
-        in_specs=[pl.BlockSpec((pair, block), lambda i: (0, i)) for _ in grads]
-        + [pl.BlockSpec(a.shape, lambda i: (0, 0)) for a in outputs],
-        out_specs=pl.BlockSpec((block, width), lambda i: (i, 0)),
-        scratch_shapes=[pltpu.VMEM((4 * pair, width), BF16), pltpu.VMEM((4 * pair, block), BF16)],
-        compiler_params=pltpu.CompilerParams(vmem_limit_bytes=16 * 2**20),
-    )(*grads, *outputs)
+    pair, width = own_g_ref.shape
+    half, part = pair // 2, width // 2
+    blocks, block = done_ref.shape[:2]
+    c = lax.axis_index("context")
+    pieces = (own_g_ref, near_g_ref), (own_p_ref, bundle_ref.at[:pair])
+    for which, refs in enumerate(pieces):
+        for n, ref in enumerate(refs):
+            for s in range(2):
+                row = (2 * n + s) * pair + (c if which == 0 else 1 - c) * half
+                left_ref[pl.ds(pl.multiple_of(row, half), half), :] = ref[
+                    s * half : (s + 1) * half, :
+                ]
+    sides = (mine_ref, mine_x_ref), (away_ref, away_x_ref)
+    for side, refs in enumerate(sides):
+        at = pl.ds(pl.multiple_of((c if side == 0 else 1 - c) * part, part), part)
+        near = (side + 1) * pair
+        for s in range(2):
+            cols = slice(s * part, (s + 1) * part)
+            right_ref[s * pair : (s + 1) * pair, at] = refs[s][...]
+            right_ref[(s + 2) * pair : (s + 3) * pair, at] = bundle_ref[near : near + pair, cols]
+    copies = []
+    for n in range(blocks):
+        rows = slice(n * block, (n + 1) * block)
+        done_ref[n] = dot(left_ref[:, rows], right_ref[...], TN)
+        copies.append(pltpu.make_async_copy(done_ref.at[n], weight_ref.at[rows, :], sems.at[n]))
+        copies[-1].start()
+    for copy in copies:
+        copy.wait()
 
 
 def spread(flip):
@@ -274,25 +256,26 @@
     after = lax.optimization_barrier
 
     grad = out_grad[0]
-    extra = grad[half:]
-    extra, q0, near_weight = after((extra, queries, out_weight))
+    c = lax.axis_index("context")
+
+    def side(which, q, k, v):
+        cut = lambda a: lax.dynamic_slice_in_dim(a[0], which * part, part, 1)
+        return jnp.concatenate([cut(q), cut(k), cut(v), tail], axis=0)
+
+    extra, gaps, near_weight, *source = after(
+        (grad[half:], gaps, out_weight, queries, keys, values)
+    )
     near_weight = over_core(near_weight)
     extra = over_y(extra)
-    own_weight, grad_here = out_weight, grad[:half]
-    c = lax.axis_index("context")
     tail = jnp.broadcast_to(gaps.astype(BF16), (16, rows))
     tail = jnp.concatenate([tail] * (part // rows), axis=1)
-
-    def side(which):
-        cut = lambda a: lax.dynamic_slice_in_dim(a, which * part, part, 1)
-        return jnp.concatenate([cut(q0[0]), cut(keys[0]), cut(values[0]), tail], axis=0)
-
-    mine, message = side(c), side(1 - c)
+    message = side(1 - c, *source)
     packed = call(
-        pack_rows_kernel, shape((half, width), BF16), (counts, grad_here, extra), smem=(0,)
-    )
-    packed, near_weight, message = after((packed, near_weight, message))
+        pack_rows_kernel, shape((half, width), BF16), (counts, grad[:half], extra), smem=(0,)
+    )
     message = over_y(message)
+    packed, near_weight, *source = after((packed, near_weight, *source))
+    mine = side(c, *source)
     first, second = [lax.ppermute(packed, ("tensor", "fsdp"), spread(a)) for a in (0, 1)]
     over_z = lambda a: lax.ppermute(a, "tensor", [(i, i ^ 1) for i in range(4)])
     blocks = [first, over_z(first), second, over_z(second)]
@@ -308,9 +291,11 @@
         (counts, slopes, mine, message),
         smem=(0, 1),
     )
+    out_x = over_x(output)
     peer_output = over_y(output)
-    peer_first, peer_second = over_y(blocks[0]), over_y(blocks[2])
-    *blocks, output = after((*blocks, output))
+    peer_first, peer_second = over_y(first), over_y(second)
+    peer_first_z = over_z(peer_first)
+    *blocks, output, peer_first, peer_second = after((*blocks, output, peer_first, peer_second))
     keep, send_x, send_y, send_xy, own_g, near_g = call(
         partial_kernel,
         (
@@ -321,7 +306,7 @@
             shape((total, width), BF16),
             shape((total, width), BF16),
         ),
-        (*blocks, own_weight, near_weight),
+        (*blocks, out_weight, near_weight),
         scratch=(pltpu.VMEM((total, width), F32),),
     )
     from_xy = lax.ppermute(
@@ -330,33 +315,55 @@
         [(c * 4 + f, (1 - c) * 4 + (f ^ 2)) for c in range(2) for f in range(4)],
     )
     from_x, from_y = over_x(send_x), over_y(send_y)
-    near_g = over_core(near_g)
-    mine_x = over_x(output)
-    mine_core = over_core(jnp.concatenate([output, mine_x], axis=0))
     from_x, from_y, from_xy, peer_output = after((from_x, from_y, from_xy, peer_output))
-    away_x = over_x(peer_output)
-    peer_blocks = [peer_first, over_z(peer_first), peer_second, over_z(peer_second)]
-    own, send = call(
+    own, send, send_q = call(
         backward_kernel,
-        (shape((3 * rows, part), BF16), shape((3 * rows, part), BF16)),
+        (
+            shape((3 * rows, part), BF16),
+            shape((2 * rows, part), BF16),
+            shape((rows, part), BF16),
+        ),
         (counts, q, k, v, probs, output, keep, from_x, from_y, from_xy),
         smem=(0,),
         scratch=(pltpu.VMEM((total, part), BF16), pltpu.VMEM((3, total, part), BF16)),
     )
     peer = over_y(send)
-    peer_blocks = after((send, *peer_blocks))[1:]
-    own_p, near_p = call(
-        place_kernel, (shape((total, width), BF16), shape((total, width), BF16)), peer_blocks
-    )
-    near_p = over_core(near_p)
-    own_g, away_x = after((send, own_g, away_x))[1:]
-    away_core = over_core(jnp.concatenate([peer_output, away_x], axis=0))
-    weight_grad = weight_gradient(
-        (own_g, near_g, own_p, near_p),
-        (output, mine_x, mine_core, peer_output, away_x, away_core),
+    near_g, peer_second, peer_output = after((near_g, peer_second, peer_output, send))[:3]
+    near_g = over_core(near_g)
+    peer_second_z = over_z(peer_second)
+    peer_x = over_x(peer_output)
+    bundled = (
+        peer_first, peer_first_z, peer_second, peer_second_z, output, out_x, peer_output, peer_x
+    )
+    *bundled, peer, send_q = after((*bundled, peer, send_q))
+    peer_q = over_y(send_q)
+    own_p, bundle = call(
+        bundle_kernel,
+        (shape((total, width), BF16), shape((3 * total, width), BF16)),
+        bundled,
+    )
+    bundle = over_core(bundle)
+    weight_grad = call(
+        weight_kernel,
+        shape(out_weight.shape, F32),
+        (own_g, near_g, own_p, bundle, output, out_x, peer_output, peer_x),
+        out=pl.ANY,
+        scratch=(
+            pltpu.VMEM((4 * total, width), BF16),
+            pltpu.VMEM((4 * total, width), BF16),
+            pltpu.VMEM((4, width // 4, width), F32),
+            pltpu.SemaphoreType.DMA((4,)),
+        ),
+        vmem=16,
     )
     weight_grad, own = after((weight_grad, own))
-    grads = call(finish_kernel, tuple(shape((rows, width), BF16) for _ in range(3)), (own, peer))
+    grads = call(
+        finish_kernel,
+        tuple(shape((rows, width), BF16) for _ in range(3)),
+        (own, peer, peer_q),
+        out=pl.ANY,
+        scratch=(pltpu.SemaphoreType.DMA((2, 3)),),
+    )
     return (grads[0][None], grads[1][None], grads[2][None], weight_grad)
 
 

time: 59.4 us -> 57.3 us (0.965)
  waiting for transfers between devices: 18.2 us -> 16.9 us
  starting transfers between devices: 25 us -> 26 us
  local copies, waits for them, and re-layouts: 4.12 us -> 3.14 us
  Pallas kernels: 9.63 us -> 8.9 us
    pallas_call x1 -> x0, Pallas kernels: 4.05 us -> none  [weight_gradient(): pl.pallas_call(weight_kernel, grid=(blocks,), out_shape=jax.ShapeDtypeStr...]
    pallas_call x6 -> x7, Pallas kernels: 5.57 us -> 8.9 us  [call(): pl.pallas_call(body, out_shape=outs, in_specs=[pl.BlockSpec(memory_space=...]
    ppermute x7 -> x8, starting transfers between devices: 7.97 us -> 10.4 us  [packed_device(): over_y = lambda a: lax.ppermute(a, 'context', [(0, 1), (1, 0)])]
    ppermute x1, waiting for transfers between devices: 3.83 us -> 1.58 us  [packed_device(): lax.ppermute(send_xy, ('context', 'fsdp'), [(c * 4 + f, (1 - c) * 4 + (f...]
    ppermute x3, waiting for transfers between devices: 1.07 us -> 2.85 us  [packed_device(): over_x = lambda a: lax.ppermute(a, 'fsdp', [(i, i ^ 2) for i in range(4)])]
    ppermute x7 -> x8, waiting for transfers between devices: 3.42 us -> 1.99 us  [packed_device(): over_y = lambda a: lax.ppermute(a, 'context', [(0, 1), (1, 0)])]
    dynamic_slice x2 -> x4, local copies, waits for them, and re-layouts: 2.28 us -> 1.06 us  [side(): cut = lambda a: lax.dynamic_slice_in_dim(a[0], which * part, part, 1)]
    ppermute x4, waiting for transfers between devices: 5.44 us -> 6.53 us  [packed_device(): over_z = lambda a: lax.ppermute(a, 'tensor', [(i, i ^ 1) for i in range(4)])]
  transfers between devices with their start and end apart: 22 -> 21, of which waited for: 9 -> 12; matrix products, arithmetic and copies ran while one was open for 7% -> 5% of each run, Pallas kernels for 15% -> 11%
where the time goes in v3:
time: 57.3 us; the launch traced here: 57.1 us
  starting transfers between devices  26 us (45%)
  waiting for transfers between devices  16.9 us (29%)
  Pallas kernels  8.9 us (16%)
  local copies, waits for them, and re-layouts  3.14 us (5%)
  between operations  1.49 us (3%)
  other arithmetic  0.72 us (1%)
    ppermute x8, starting transfers between devices, packed_device(): over_y = lambda a: lax.ppermute(a, 'context', [(0, 1), (1, 0)])  10.4 us
    pallas_call x7, Pallas kernels, call(): pl.pallas_call(body, out_shape=outs, in_specs=[pl.BlockSpec(memory_space=...  8.9 us
    ppermute x4, starting transfers between devices, packed_device(): over_z = lambda a: lax.ppermute(a, 'tensor', [(i, i ^ 1) for i in range(4)])  6.99 us
    ppermute x4, waiting for transfers between devices, packed_device(): over_z = lambda a: lax.ppermute(a, 'tensor', [(i, i ^ 1) for i in range(4)])  6.53 us
    ppermute x2, starting transfers between devices, packed_device(): lax.ppermute(packed, ('tensor', 'fsdp'), spread(a))  3.25 us
    ppermute x3, starting transfers between devices, packed_device(): over_x = lambda a: lax.ppermute(a, 'fsdp', [(i, i ^ 2) for i in range(4)])  3.11 us
    ppermute x3, waiting for transfers between devices, packed_device(): over_x = lambda a: lax.ppermute(a, 'fsdp', [(i, i ^ 2) for i in range(4)])  2.85 us
    ppermute x2, waiting for transfers between devices, packed_device(): lax.ppermute(packed, ('tensor', 'fsdp'), spread(a))  2.38 us
  transfers between devices with their start and end apart: 21, of which 12 were waited for; matrix products, arithmetic and copies ran while one was open for 5% of the time, Pallas kernels for 11%

profile of v3, /device:TPU:0, one launch (start us, length us, event | category | flops | bytes accessed | tf_op | source)
XLA Modules:
  0.0 57.1 jit_solution(9996137679838525550)
XLA Ops:
  0.7 1.0 %slice_bitcast_fusion.1 = bf16[48,1024]{1,0:T(8,128)(2,1)S(1)} fusion(bf16[1,128,1024]{2,1,0:T(8,128)(2,1)} %param.11), kind=kLoop, calls=%fused_computation.10 | loop fusion | bytes 196608 | tf_op jit(solution)/shard_map/slice | solution.py:266
  2.1 2.6 %collective-permute-start = (bf16[48,1024]{1,0:T(8,128)(2,1)S(1)}, bf16[48,1024]{1,0:T(8,128)(2,1)S(1)}, u32[]{:S(2)}, u32[]{:S(2)}) collective-permute-start(bf16[48,1024]{1,0:T(8,128)(2,1)S(1)} %slice_bitcast_fusion.1), channel_id=1, source_target_pairs={{0,16},{16,0},{1,17},{17,1},{2,18},{18,2},{3,19},{19,3},{4,20},{20... | collective-permute-start | bytes 294920 | tf_op jit(solution)/shard_map/ppermute | solution.py:253
  5.3 1.0 %dynamic-slice_bitcast_fusion = (bf16[128,512]{1,0:T(8,128)(2,1)S(1)}, bf16[128,512]{1,0:T(8,128)(2,1)S(1)}) fusion(bf16[1,128,1024]{2,1,0:T(8,128)(2,1)} %param.10, s32[]{:T(128)S(6)} %select_n.5, bf16[1,128,1024]{2,1,0:T(8,128)(2,1)} %param.9), kind=kLoop, calls=%fused_computation.4 | loop fusion | bytes 524292 | tf_op jit(solution)/shard_map/dynamic_slice | solution.py:262
  7.0 1.1 %slice_bitcast_fusion.own_ref = bf16[80,1024]{1,0:T(8,128)(2,1)S(1)} fusion(bf16[1,128,1024]{2,1,0:T(8,128)(2,1)} %param.11), kind=kLoop, calls=%fused_computation.3 | loop fusion | bytes 327680 | tf_op jit(solution)/shard_map/slice | solution.py:274
  8.5 1.8 %collective-permute-start.6 = (bf16[400,512]{1,0:T(8,128)(2,1)S(1)}, bf16[400,512]{1,0:T(8,128)(2,1)S(1)}, u32[]{:S(2)}, u32[]{:S(2)}) collective-permute-start(bf16[400,512]{1,0:T(8,128)(2,1)S(1)} %get-tuple-element.116), channel_id=1, source_target_pairs={{0,16},{16,0},{1,17},{17,1},{2,18},{18,2},{3,19},{19,3},{4,20},{20... | collective-permute-start | bytes 1228808 | tf_op jit(solution)/shard_map/ppermute | solution.py:253
  10.3 2.6 %collective-permute-start.4 = (bf16[80,1024]{1,0:T(8,128)(2,1)S(1)}, bf16[80,1024]{1,0:T(8,128)(2,1)S(1)}, u32[]{:S(2)}, u32[]{:S(2)}) collective-permute-start(bf16[80,1024]{1,0:T(8,128)(2,1)S(1)} %shard_map.111), channel_id=1, source_target_pairs={{0,8},{1,9},{2,0},{3,1},{4,12},{5,13},{6,4},{7,5},{8,10},{9,11},{1... | collective-permute-start | bytes 491528 | tf_op jit(solution)/shard_map/ppermute | solution.py:279
  13.6 2.4 %collective-permute-done.4.b10_ref = bf16[80,1024]{1,0:T(8,128)(2,1)S(1)} collective-permute-done((bf16[80,1024]{1,0:T(8,128)(2,1)S(1)}, bf16[80,1024]{1,0:T(8,128)(2,1)S(1)}, u32[]{:S(2)}, u32[]{:S(2)}) %collective-permute-start.4) | collective-permute-done | bytes 163872 | tf_op jit(solution)/shard_map/ppermute | solution.py:279
  16.8 4.9 %collective-permute-start.5 = (bf16[80,1024]{1,0:T(8,128)(2,1)S(1)}, bf16[80,1024]{1,0:T(8,128)(2,1)S(1)}, u32[]{:S(2)}, u32[]{:S(2)}) collective-permute-start(bf16[80,1024]{1,0:T(8,128)(2,1)S(1)} %collective-permute-done.4.b10_ref), channel_id=1, source_target_pairs={{0,4},{4,0},{8,12},{12,8},{1,5},{5,1},{9,13},{13,9},{2,6},{6,2},{1... | collective-permute-start | bytes 491528 | tf_op jit(solution)/shard_map/ppermute | solution.py:280
  21.7 1.2 %collective-permute-start.7 = (bf16[80,1024]{1,0:T(8,128)(2,1)S(1)}, bf16[80,1024]{1,0:T(8,128)(2,1)S(1)}, u32[]{:S(2)}, u32[]{:S(2)}) collective-permute-start(bf16[80,1024]{1,0:T(8,128)(2,1)S(1)} %collective-permute-done.2.b00_ref), channel_id=1, source_target_pairs={{0,16},{16,0},{1,17},{17,1},{2,18},{18,2},{3,19},{19,3},{4,20},{20... | collective-permute-start | bytes 491528 | tf_op jit(solution)/shard_map/ppermute | solution.py:253
  22.9 1.9 %shard_map.112 = (bf16[160,512]{1,0:T(8,128)(2,1)S(1)}, bf16[160,512]{1,0:T(8,128)(2,1)S(1)}, bf16[160,512]{1,0:T(8,128)(2,1)S(1)}, f32[4,160,160]{2,1,0:T(8,128)S(1)}, bf16[160,512]{1,0:T(8,128)(2,1)S(1)}) custom-call(s32[1,1]{1,0:T(1,128)S(6)} %copy.12.count_ref, f32[8]{0:T(128)S(1)} %copy-done.2, bf16[400,512]{1,0:T(8,128)(2,1)S(1)} %get-tuple-element.117.mine_ref, ...), custom_call_target="tpu_custom_call" | custom-call | tf_op jit(solution)/shard_map/pallas_call | solution.py:31
  24.8 0.9 %collective-permute-start.12 = (bf16[160,512]{1,0:T(8,128)(2,1)S(1)}, bf16[160,512]{1,0:T(8,128)(2,1)S(1)}, u32[]{:S(2)}, u32[]{:S(2)}) collective-permute-start(bf16[160,512]{1,0:T(8,128)(2,1)S(1)} %get-tuple-element.102.output_ref.mine_ref), channel_id=1, source_target_pairs={{0,16},{16,0},{1,17},{17,1},{2,18},{18,2},{3,19},{19,3},{4,20},{20... | collective-permute-start | bytes 491528 | tf_op jit(solution)/shard_map/ppermute | solution.py:253
  25.7 1.2 %collective-permute-done.5.b11_ref = bf16[80,1024]{1,0:T(8,128)(2,1)S(1)} collective-permute-done((bf16[80,1024]{1,0:T(8,128)(2,1)S(1)}, bf16[80,1024]{1,0:T(8,128)(2,1)S(1)}, u32[]{:S(2)}, u32[]{:S(2)}) %collective-permute-start.5) | collective-permute-done | bytes 163872 | tf_op jit(solution)/shard_map/ppermute | solution.py:280
  26.9 1.0 %collective-permute-done.7.p00_ref = bf16[80,1024]{1,0:T(8,128)(2,1)S(1)} collective-permute-done((bf16[80,1024]{1,0:T(8,128)(2,1)S(1)}, bf16[80,1024]{1,0:T(8,128)(2,1)S(1)}, u32[]{:S(2)}, u32[]{:S(2)}) %collective-permute-start.7) | collective-permute-done | bytes 163872 | tf_op jit(solution)/shard_map/ppermute | solution.py:253
  27.8 2.5 %collective-permute-done.3.b01_ref = bf16[80,1024]{1,0:T(8,128)(2,1)S(1)} collective-permute-done((bf16[80,1024]{1,0:T(8,128)(2,1)S(1)}, bf16[80,1024]{1,0:T(8,128)(2,1)S(1)}, u32[]{:S(2)}, u32[]{:S(2)}) %collective-permute-start.3) | collective-permute-done | bytes 163872 | tf_op jit(solution)/shard_map/ppermute | solution.py:280
  30.3 1.0 %shard_map.113 = (f32[80,512]{1,0:T(8,128)S(1)}, bf16[80,512]{1,0:T(8,128)(2,1)S(1)}, bf16[80,512]{1,0:T(8,128)(2,1)S(1)}, bf16[80,512]{1,0:T(8,128)(2,1)S(1)}, ...) custom-call(bf16[80,1024]{1,0:T(8,128)(2,1)S(1)} %collective-permute-done.2.b00_ref, ...), custom_call_target="tpu_custom_call" | custom-call | tf_op jit(solution)/shard_map/pallas_call | solution.py:31
  31.3 1.1 %collective-permute-start.9 = (bf16[80,512]{1,0:T(8,128)(2,1)S(1)}, bf16[80,512]{1,0:T(8,128)(2,1)S(1)}, u32[]{:S(2)}, u32[]{:S(2)}) collective-permute-start(bf16[80,512]{1,0:T(8,128)(2,1)S(1)} %get-tuple-element.79), channel_id=1, source_target_pairs={{0,2},{1,3},{2,0},{3,1},{4,6},{5,7},{6,4},{7,5},{8,10},{9,11},{10,... | collective-permute-start | bytes 245768 | tf_op jit(solution)/shard_map/ppermute | solution.py:254
  32.4 1.2 %collective-permute-start.10 = (bf16[80,512]{1,0:T(8,128)(2,1)S(1)}, bf16[80,512]{1,0:T(8,128)(2,1)S(1)}, u32[]{:S(2)}, u32[]{:S(2)}) collective-permute-start(bf16[80,512]{1,0:T(8,128)(2,1)S(1)} %get-tuple-element.80), channel_id=1, source_target_pairs={{0,16},{16,0},{1,17},{17,1},{2,18},{18,2},{3,19},{19,3},{4,20},{20... | collective-permute-start | bytes 245768 | tf_op jit(solution)/shard_map/ppermute | solution.py:253
  33.6 1.2 %collective-permute-start.11 = (bf16[80,512]{1,0:T(8,128)(2,1)S(1)}, bf16[80,512]{1,0:T(8,128)(2,1)S(1)}, u32[]{:S(2)}, u32[]{:S(2)}) collective-permute-start(bf16[80,512]{1,0:T(8,128)(2,1)S(1)} %get-tuple-element.81), channel_id=1, source_target_pairs={{0,18},{1,19},{2,16},{3,17},{16,2},{17,3},{18,0},{19,1},{4,22},{5,... | collective-permute-start | bytes 245768 | tf_op jit(solution)/shard_map/ppermute | solution.py:312
  34.8 1.5 %collective-permute-done.9.from_x_ref = bf16[80,512]{1,0:T(8,128)(2,1)S(1)} collective-permute-done((bf16[80,512]{1,0:T(8,128)(2,1)S(1)}, bf16[80,512]{1,0:T(8,128)(2,1)S(1)}, u32[]{:S(2)}, u32[]{:S(2)}) %collective-permute-start.9) | collective-permute-done | bytes 81952 | tf_op jit(solution)/shard_map/ppermute | solution.py:254
  36.3 1.0 %collective-permute-done.10.from_y_ref = bf16[80,512]{1,0:T(8,128)(2,1)S(1)} collective-permute-done((bf16[80,512]{1,0:T(8,128)(2,1)S(1)}, bf16[80,512]{1,0:T(8,128)(2,1)S(1)}, u32[]{:S(2)}, u32[]{:S(2)}) %collective-permute-start.10) | collective-permute-done | bytes 81952 | tf_op jit(solution)/shard_map/ppermute | solution.py:253
  37.3 1.6 %collective-permute-done.11.from_xy_ref = bf16[80,512]{1,0:T(8,128)(2,1)S(1)} collective-permute-done((bf16[80,512]{1,0:T(8,128)(2,1)S(1)}, bf16[80,512]{1,0:T(8,128)(2,1)S(1)}, u32[]{:S(2)}, u32[]{:S(2)}) %collective-permute-start.11) | collective-permute-done | bytes 81952 | tf_op jit(solution)/shard_map/ppermute | solution.py:312
  38.9 1.5 %shard_map.114 = (bf16[384,512]{1,0:T(8,128)(2,1)S(1)}, bf16[256,512]{1,0:T(8,128)(2,1)S(1)}, bf16[128,512]{1,0:T(8,128)(2,1)S(1)}) custom-call(s32[1,1]{1,0:T(1,128)S(6)} %copy.12.count_ref, bf16[160,512]{1,0:T(8,128)(2,1)S(1)} %get-tuple-element.83.q_ref, bf16[160,512]{1,0:T(8,128)(2,1)S(1)} %get-tuple-element.84.k_ref, ...), custom_call_target="tpu_custom_call" | custom-call | tf_op jit(solution)/shard_map/pallas_call | solution.py:31
  40.5 0.9 %collective-permute-start.18 = (bf16[256,512]{1,0:T(8,128)(2,1)S(1)}, bf16[256,512]{1,0:T(8,128)(2,1)S(1)}, u32[]{:S(2)}, u32[]{:S(2)}) collective-permute-start(bf16[256,512]{1,0:T(8,128)(2,1)S(1)} %get-tuple-element.92), channel_id=1, source_target_pairs={{0,16},{16,0},{1,17},{17,1},{2,18},{18,2},{3,19},{19,3},{4,20},{20... | collective-permute-start | bytes 786440 | tf_op jit(solution)/shard_map/ppermute | solution.py:253
  41.4 1.2 %collective-permute-start.14 = (bf16[80,1024]{1,0:T(8,128)(2,1)S(1)}, bf16[80,1024]{1,0:T(8,128)(2,1)S(1)}, u32[]{:S(2)}, u32[]{:S(2)}) collective-permute-start(bf16[80,1024]{1,0:T(8,128)(2,1)S(1)} %collective-permute-done.7.p00_ref), channel_id=1, source_target_pairs={{0,4},{4,0},{8,12},{12,8},{1,5},{5,1},{9,13},{13,9},{2,6},{6,2},{1... | collective-permute-start | bytes 491528 | tf_op jit(solution)/shard_map/ppermute | solution.py:280
  42.5 0.9 %collective-permute-start.16 = (bf16[160,512]{1,0:T(8,128)(2,1)S(1)}, bf16[160,512]{1,0:T(8,128)(2,1)S(1)}, u32[]{:S(2)}, u32[]{:S(2)}) collective-permute-start(bf16[160,512]{1,0:T(8,128)(2,1)S(1)} %get-tuple-element.102.output_ref.mine_ref), channel_id=1, source_target_pairs={{0,2},{1,3},{2,0},{3,1},{4,6},{5,7},{6,4},{7,5},{8,10},{9,11},{10,... | collective-permute-start | bytes 491528 | tf_op jit(solution)/shard_map/ppermute | solution.py:254
  44.4 1.1 %collective-permute-start.17 = (bf16[160,512]{1,0:T(8,128)(2,1)S(1)}, bf16[160,512]{1,0:T(8,128)(2,1)S(1)}, u32[]{:S(2)}, u32[]{:S(2)}) collective-permute-start(bf16[160,512]{1,0:T(8,128)(2,1)S(1)} %collective-permute-done.12.away_ref), channel_id=1, source_target_pairs={{0,2},{1,3},{2,0},{3,1},{4,6},{5,7},{6,4},{7,5},{8,10},{9,11},{10,... | collective-permute-start | bytes 491528 | tf_op jit(solution)/shard_map/ppermute | solution.py:254
  45.4 1.8 %collective-permute-done.14.p01_ref = bf16[80,1024]{1,0:T(8,128)(2,1)S(1)} collective-permute-done((bf16[80,1024]{1,0:T(8,128)(2,1)S(1)}, bf16[80,1024]{1,0:T(8,128)(2,1)S(1)}, u32[]{:S(2)}, u32[]{:S(2)}) %collective-permute-start.14) | collective-permute-done | bytes 163872 | tf_op jit(solution)/shard_map/ppermute | solution.py:280
  47.9 1.1 %collective-permute-done.15.p11_ref = bf16[80,1024]{1,0:T(8,128)(2,1)S(1)} collective-permute-done((bf16[80,1024]{1,0:T(8,128)(2,1)S(1)}, bf16[80,1024]{1,0:T(8,128)(2,1)S(1)}, u32[]{:S(2)}, u32[]{:S(2)}) %collective-permute-start.15) | collective-permute-done | bytes 163872 | tf_op jit(solution)/shard_map/ppermute | solution.py:280
  50.4 1.0 %collective-permute-start.20 = (bf16[128,512]{1,0:T(8,128)(2,1)S(1)}, bf16[128,512]{1,0:T(8,128)(2,1)S(1)}, u32[]{:S(2)}, u32[]{:S(2)}) collective-permute-start(bf16[128,512]{1,0:T(8,128)(2,1)S(1)} %get-tuple-element.111), channel_id=1, source_target_pairs={{0,16},{16,0},{1,17},{17,1},{2,18},{18,2},{3,19},{19,3},{4,20},{20... | collective-permute-start | bytes 393224 | tf_op jit(solution)/shard_map/ppermute | solution.py:253
  51.3 1.5 %collective-permute-done.13.near_g_ref = bf16[160,1024]{1,0:T(8,128)(2,1)S(1)} collective-permute-done((bf16[160,1024]{1,0:T(8,128)(2,1)S(1)}, bf16[160,1024]{1,0:T(8,128)(2,1)S(1)}, u32[]{:S(2)}, u32[]{:S(2)}) %collective-permute-start.13) | collective-permute-done | bytes 327712 | tf_op jit(solution)/shard_map/ppermute | solution.py:255
  52.9 3.3 %shard_map.116 = f32[1024,1024]{1,0:T(8,128)} custom-call(bf16[160,1024]{1,0:T(8,128)(2,1)S(1)} %get-tuple-element.76.own_g_ref, bf16[160,1024]{1,0:T(8,128)(2,1)S(1)} %collective-permute-done.13.near_g_ref, bf16[160,1024]{1,0:T(8,128)(2,1)S(1)} %get-tuple-element.106.own_p_ref, bf16[480,1024]{1,0:T(8,128)(2,1)S(1)} %collective-permute-done.19.bundle_ref, ...), custom_call_target="tpu_custom_call" | custom-call | tf_op jit(solution)/shard_map/pallas_call | solution.py:31
  56.2 0.9 %shard_map.117 = (bf16[128,1024]{1,0:T(8,128)(2,1)}, bf16[128,1024]{1,0:T(8,128)(2,1)}, bf16[128,1024]{1,0:T(8,128)(2,1)}) custom-call(bf16[384,512]{1,0:T(8,128)(2,1)S(1)} %get-tuple-element.109.own_ref, bf16[256,512]{1,0:T(8,128)(2,1)S(1)} %collective-permute-done.18.peer_ref, bf16[128,512]{1,0:T(8,128)(2,1)S(1)} %collective-permute-done.20.peer_q_ref), custom_call_target="tpu_custom_call" | custom-call | tf_op jit(solution)/shard_map/pallas_call | solution.py:31
  (36 shorter events, 5.9 us)
Async XLA Ops:
  0.6 7.5 %copy-start = (bf16[1,128,1024]{2,1,0:T(8,128)(2,1)S(1)}, bf16[1,128,1024]{2,1,0:T(8,128)(2,1)}, u32[]{:S(2)}) copy-start(bf16[1,128,1024]{2,1,0:T(8,128)(2,1)} %param.8) | copy-start | bytes 786436
  0.6 7.8 %copy-start.3 = (bf16[1,128,1024]{2,1,0:T(8,128)(2,1)S(1)}, bf16[1,128,1024]{2,1,0:T(8,128)(2,1)}, u32[]{:S(2)}) copy-start(bf16[1,128,1024]{2,1,0:T(8,128)(2,1)} %param.10) | copy-start | bytes 786436
  0.7 7.8 %copy-start.4 = (bf16[1,128,1024]{2,1,0:T(8,128)(2,1)S(1)}, bf16[1,128,1024]{2,1,0:T(8,128)(2,1)}, u32[]{:S(2)}) copy-start(bf16[1,128,1024]{2,1,0:T(8,128)(2,1)} %param.9) | copy-start | bytes 786436
  0.7 22.2 %copy-start.2 = (f32[8]{0:T(128)S(1)}, f32[8]{0:T(128)}, u32[]{:S(2)}) copy-start(f32[8]{0:T(128)} %slopes_ref.1) | copy-start | bytes 100
  1.6 6.7 %collective-permute-start.1 = (bf16[1024,1024]{1,0:T(8,128)(2,1)}, bf16[1024,1024]{1,0:T(8,128)(2,1)S(1)}, u32[]{:S(2)}, u32[]{:S(2)}) collective-permute-start(bf16[1024,1024]{1,0:T(8,128)(2,1)} %own_w_ref.1), channel_id=1, source_target_pairs={{0,1},{1,0},{2,3},{3,2},{4,5},{5,4},{6,7},{7,6},{8,9},{9,8},{10,11... | collective-permute-start | bytes 6291464 | tf_op jit(solution)/shard_map/ppermute | solution.py:255
  2.1 6.0 %collective-permute-start = (bf16[48,1024]{1,0:T(8,128)(2,1)S(1)}, bf16[48,1024]{1,0:T(8,128)(2,1)S(1)}, u32[]{:S(2)}, u32[]{:S(2)}) collective-permute-start(bf16[48,1024]{1,0:T(8,128)(2,1)S(1)} %slice_bitcast_fusion.1), channel_id=1, source_target_pairs={{0,16},{16,0},{1,17},{17,1},{2,18},{18,2},{3,19},{19,3},{4,20},{20... | collective-permute-start | bytes 294920 | tf_op jit(solution)/shard_map/ppermute | solution.py:253
  7.0 23.3 %copy-start.1 = (bf16[1024,1024]{1,0:T(8,128)(2,1)S(1)}, bf16[1024,1024]{1,0:T(8,128)(2,1)}, u32[]{:S(2)}) copy-start(bf16[1024,1024]{1,0:T(8,128)(2,1)} %own_w_ref.1) | copy-start | bytes 6291460
  8.5 14.4 %collective-permute-start.6 = (bf16[400,512]{1,0:T(8,128)(2,1)S(1)}, bf16[400,512]{1,0:T(8,128)(2,1)S(1)}, u32[]{:S(2)}, u32[]{:S(2)}) collective-permute-start(bf16[400,512]{1,0:T(8,128)(2,1)S(1)} %get-tuple-element.116), channel_id=1, source_target_pairs={{0,16},{16,0},{1,17},{17,1},{2,18},{18,2},{3,19},{19,3},{4,20},{20... | collective-permute-start | bytes 1228808 | tf_op jit(solution)/shard_map/ppermute | solution.py:253
  10.3 5.6 %collective-permute-start.4 = (bf16[80,1024]{1,0:T(8,128)(2,1)S(1)}, bf16[80,1024]{1,0:T(8,128)(2,1)S(1)}, u32[]{:S(2)}, u32[]{:S(2)}) collective-permute-start(bf16[80,1024]{1,0:T(8,128)(2,1)S(1)} %shard_map.111), channel_id=1, source_target_pairs={{0,8},{1,9},{2,0},{3,1},{4,12},{5,13},{6,4},{7,5},{8,10},{9,11},{1... | collective-permute-start | bytes 491528 | tf_op jit(solution)/shard_map/ppermute | solution.py:279
  12.9 8.8 %collective-permute-start.2 = (bf16[80,1024]{1,0:T(8,128)(2,1)S(1)}, bf16[80,1024]{1,0:T(8,128)(2,1)S(1)}, u32[]{:S(2)}, u32[]{:S(2)}) collective-permute-start(bf16[80,1024]{1,0:T(8,128)(2,1)S(1)} %shard_map.111), channel_id=1, source_target_pairs={{0,0},{1,1},{2,8},{3,9},{4,4},{5,5},{6,12},{7,13},{8,2},{9,3},{10,... | collective-permute-start | bytes 491528 | tf_op jit(solution)/shard_map/ppermute | solution.py:279
  15.9 9.8 %collective-permute-start.8 = (bf16[80,1024]{1,0:T(8,128)(2,1)S(1)}, bf16[80,1024]{1,0:T(8,128)(2,1)S(1)}, u32[]{:S(2)}, u32[]{:S(2)}) collective-permute-start(bf16[80,1024]{1,0:T(8,128)(2,1)S(1)} %collective-permute-done.4.b10_ref), channel_id=1, source_target_pairs={{0,16},{16,0},{1,17},{17,1},{2,18},{18,2},{3,19},{19,3},{4,20},{20... | collective-permute-start | bytes 491528 | tf_op jit(solution)/shard_map/ppermute | solution.py:253
  16.8 10.1 %collective-permute-start.5 = (bf16[80,1024]{1,0:T(8,128)(2,1)S(1)}, bf16[80,1024]{1,0:T(8,128)(2,1)S(1)}, u32[]{:S(2)}, u32[]{:S(2)}) collective-permute-start(bf16[80,1024]{1,0:T(8,128)(2,1)S(1)} %collective-permute-done.4.b10_ref), channel_id=1, source_target_pairs={{0,4},{4,0},{8,12},{12,8},{1,5},{5,1},{9,13},{13,9},{2,6},{6,2},{1... | collective-permute-start | bytes 491528 | tf_op jit(solution)/shard_map/ppermute | solution.py:280
  21.7 6.1 %collective-permute-start.7 = (bf16[80,1024]{1,0:T(8,128)(2,1)S(1)}, bf16[80,1024]{1,0:T(8,128)(2,1)S(1)}, u32[]{:S(2)}, u32[]{:S(2)}) collective-permute-start(bf16[80,1024]{1,0:T(8,128)(2,1)S(1)} %collective-permute-done.2.b00_ref), channel_id=1, source_target_pairs={{0,16},{16,0},{1,17},{17,1},{2,18},{18,2},{3,19},{19,3},{4,20},{20... | collective-permute-start | bytes 491528 | tf_op jit(solution)/shard_map/ppermute | solution.py:253
  22.9 7.4 %collective-permute-start.3 = (bf16[80,1024]{1,0:T(8,128)(2,1)S(1)}, bf16[80,1024]{1,0:T(8,128)(2,1)S(1)}, u32[]{:S(2)}, u32[]{:S(2)}) collective-permute-start(bf16[80,1024]{1,0:T(8,128)(2,1)S(1)} %collective-permute-done.2.b00_ref), channel_id=1, source_target_pairs={{0,4},{4,0},{8,12},{12,8},{1,5},{5,1},{9,13},{13,9},{2,6},{6,2},{1... | collective-permute-start | bytes 491528 | tf_op jit(solution)/shard_map/ppermute | solution.py:280
  24.8 14.1 %collective-permute-start.12 = (bf16[160,512]{1,0:T(8,128)(2,1)S(1)}, bf16[160,512]{1,0:T(8,128)(2,1)S(1)}, u32[]{:S(2)}, u32[]{:S(2)}) collective-permute-start(bf16[160,512]{1,0:T(8,128)(2,1)S(1)} %get-tuple-element.102.output_ref.mine_ref), channel_id=1, source_target_pairs={{0,16},{16,0},{1,17},{17,1},{2,18},{18,2},{3,19},{19,3},{4,20},{20... | collective-permute-start | bytes 491528 | tf_op jit(solution)/shard_map/ppermute | solution.py:253
  31.3 5.1 %collective-permute-start.9 = (bf16[80,512]{1,0:T(8,128)(2,1)S(1)}, bf16[80,512]{1,0:T(8,128)(2,1)S(1)}, u32[]{:S(2)}, u32[]{:S(2)}) collective-permute-start(bf16[80,512]{1,0:T(8,128)(2,1)S(1)} %get-tuple-element.79), channel_id=1, source_target_pairs={{0,2},{1,3},{2,0},{3,1},{4,6},{5,7},{6,4},{7,5},{8,10},{9,11},{10,... | collective-permute-start | bytes 245768 | tf_op jit(solution)/shard_map/ppermute | solution.py:254
  32.4 5.0 %collective-permute-start.10 = (bf16[80,512]{1,0:T(8,128)(2,1)S(1)}, bf16[80,512]{1,0:T(8,128)(2,1)S(1)}, u32[]{:S(2)}, u32[]{:S(2)}) collective-permute-start(bf16[80,512]{1,0:T(8,128)(2,1)S(1)} %get-tuple-element.80), channel_id=1, source_target_pairs={{0,16},{16,0},{1,17},{17,1},{2,18},{18,2},{3,19},{19,3},{4,20},{20... | collective-permute-start | bytes 245768 | tf_op jit(solution)/shard_map/ppermute | solution.py:253
  33.6 5.3 %collective-permute-start.11 = (bf16[80,512]{1,0:T(8,128)(2,1)S(1)}, bf16[80,512]{1,0:T(8,128)(2,1)S(1)}, u32[]{:S(2)}, u32[]{:S(2)}) collective-permute-start(bf16[80,512]{1,0:T(8,128)(2,1)S(1)} %get-tuple-element.81), channel_id=1, source_target_pairs={{0,18},{1,19},{2,16},{3,17},{16,2},{17,3},{18,0},{19,1},{4,22},{5,... | collective-permute-start | bytes 245768 | tf_op jit(solution)/shard_map/ppermute | solution.py:312
  40.5 9.2 %collective-permute-start.18 = (bf16[256,512]{1,0:T(8,128)(2,1)S(1)}, bf16[256,512]{1,0:T(8,128)(2,1)S(1)}, u32[]{:S(2)}, u32[]{:S(2)}) collective-permute-start(bf16[256,512]{1,0:T(8,128)(2,1)S(1)} %get-tuple-element.92), channel_id=1, source_target_pairs={{0,16},{16,0},{1,17},{17,1},{2,18},{18,2},{3,19},{19,3},{4,20},{20... | collective-permute-start | bytes 786440 | tf_op jit(solution)/shard_map/ppermute | solution.py:253
  41.4 5.9 %collective-permute-start.14 = (bf16[80,1024]{1,0:T(8,128)(2,1)S(1)}, bf16[80,1024]{1,0:T(8,128)(2,1)S(1)}, u32[]{:S(2)}, u32[]{:S(2)}) collective-permute-start(bf16[80,1024]{1,0:T(8,128)(2,1)S(1)} %collective-permute-done.7.p00_ref), channel_id=1, source_target_pairs={{0,4},{4,0},{8,12},{12,8},{1,5},{5,1},{9,13},{13,9},{2,6},{6,2},{1... | collective-permute-start | bytes 491528 | tf_op jit(solution)/shard_map/ppermute | solution.py:280
  42.5 5.3 %collective-permute-start.16 = (bf16[160,512]{1,0:T(8,128)(2,1)S(1)}, bf16[160,512]{1,0:T(8,128)(2,1)S(1)}, u32[]{:S(2)}, u32[]{:S(2)}) collective-permute-start(bf16[160,512]{1,0:T(8,128)(2,1)S(1)} %get-tuple-element.102.output_ref.mine_ref), channel_id=1, source_target_pairs={{0,2},{1,3},{2,0},{3,1},{4,6},{5,7},{6,4},{7,5},{8,10},{9,11},{10,... | collective-permute-start | bytes 491528 | tf_op jit(solution)/shard_map/ppermute | solution.py:254
  43.5 5.5 %collective-permute-start.15 = (bf16[80,1024]{1,0:T(8,128)(2,1)S(1)}, bf16[80,1024]{1,0:T(8,128)(2,1)S(1)}, u32[]{:S(2)}, u32[]{:S(2)}) collective-permute-start(bf16[80,1024]{1,0:T(8,128)(2,1)S(1)} %collective-permute-done.8.p10_ref), channel_id=1, source_target_pairs={{0,4},{4,0},{8,12},{12,8},{1,5},{5,1},{9,13},{13,9},{2,6},{6,2},{1... | collective-permute-start | bytes 491528 | tf_op jit(solution)/shard_map/ppermute | solution.py:280
  44.4 5.3 %collective-permute-start.17 = (bf16[160,512]{1,0:T(8,128)(2,1)S(1)}, bf16[160,512]{1,0:T(8,128)(2,1)S(1)}, u32[]{:S(2)}, u32[]{:S(2)}) collective-permute-start(bf16[160,512]{1,0:T(8,128)(2,1)S(1)} %collective-permute-done.12.away_ref), channel_id=1, source_target_pairs={{0,2},{1,3},{2,0},{3,1},{4,6},{5,7},{6,4},{7,5},{8,10},{9,11},{10,... | collective-permute-start | bytes 491528 | tf_op jit(solution)/shard_map/ppermute | solution.py:254
  49.8 3.1 %collective-permute-start.19 = (bf16[480,1024]{1,0:T(8,128)(2,1)S(1)}, bf16[480,1024]{1,0:T(8,128)(2,1)S(1)}, u32[]{:S(2)}, u32[]{:S(2)}) collective-permute-start(bf16[480,1024]{1,0:T(8,128)(2,1)S(1)} %get-tuple-element.107), channel_id=1, source_target_pairs={{0,1},{1,0},{2,3},{3,2},{4,5},{5,4},{6,7},{7,6},{8,9},{9,8},{10,11... | collective-permute-start | bytes 2949128 | tf_op jit(solution)/shard_map/ppermute | solution.py:255
  49.9 3.0 %collective-permute-start.13 = (bf16[160,1024]{1,0:T(8,128)(2,1)S(1)}, bf16[160,1024]{1,0:T(8,128)(2,1)S(1)}, u32[]{:S(2)}, u32[]{:S(2)}) collective-permute-start(bf16[160,1024]{1,0:T(8,128)(2,1)S(1)} %get-tuple-element.93), channel_id=1, source_target_pairs={{0,1},{1,0},{2,3},{3,2},{4,5},{5,4},{6,7},{7,6},{8,9},{9,8},{10,11... | collective-permute-start | bytes 983048 | tf_op jit(solution)/shard_map/ppermute | solution.py:255
  50.4 5.8 %collective-permute-start.20 = (bf16[128,512]{1,0:T(8,128)(2,1)S(1)}, bf16[128,512]{1,0:T(8,128)(2,1)S(1)}, u32[]{:S(2)}, u32[]{:S(2)}) collective-permute-start(bf16[128,512]{1,0:T(8,128)(2,1)S(1)} %get-tuple-element.111), channel_id=1, source_target_pairs={{0,16},{16,0},{1,17},{17,1},{2,18},{18,2},{3,19},{19,3},{4,20},{20... | collective-permute-start | bytes 393224 | tf_op jit(solution)/shard_map/ppermute | solution.py:253

commit v4 on v3

--- a/solution.py
+++ b/solution.py
@@ -176,7 +176,10 @@
     slot = packed_slot(iota((rows, total), 1), half, rows, count0, total - count0)
     row = iota((rows, total), 0)
     own_pick, peer_pick = onehot(slot == c * rows + row), onehot(slot == (1 - c) * rows + row)
-    send_q_ref[...] = dot(peer_pick, grads_ref[0]).astype(BF16)
+    cut = send_q_ref.shape[0]
+    picked = dot(peer_pick, grads_ref[0]).astype(BF16)
+    send_q_ref[...] = picked[:cut]
+    send_ref[2 * rows :, :] = picked[cut:]
     for n in range(1, 3):
         send_ref[(n - 1) * rows : n * rows, :] = dot(peer_pick, grads_ref[n]).astype(BF16)
     for n in range(3):
@@ -189,45 +192,61 @@
     c = lax.axis_index("context")
     copies = []
     own = [own_ref.at[n * rows : (n + 1) * rows, :] for n in range(3)]
-    peer = [peer_q_ref, peer_ref.at[:rows, :], peer_ref.at[rows:, :]]
+    cut = peer_q_ref.shape[0]
+    peer = [peer_q_ref, peer_ref.at[:rows, :], peer_ref.at[rows : 2 * rows, :]]
     for side, sources in enumerate((own, peer)):
         at = pl.ds(pl.multiple_of((c if side == 0 else 1 - c) * part, part), part)
         for n, ref in enumerate((q_ref, k_ref, v_ref)):
-            copies.append(pltpu.make_async_copy(sources[n], ref.at[:, at], sems.at[side, n]))
+            to = ref.at[:cut, at] if side == 1 and n == 0 else ref.at[:, at]
+            copies.append(pltpu.make_async_copy(sources[n], to, sems.at[side, n]))
+    rest = q_ref.at[cut:, pl.ds(pl.multiple_of((1 - c) * part, part), part)]
+    copies.append(pltpu.make_async_copy(peer_ref.at[2 * rows :, :], rest, sems.at[2, 0]))
     for copy in copies:
         copy.start()
     for copy in copies:
         copy.wait()
 
 
+def weight_operands(grads, outputs, left_ref, right_ref):
+    pair = grads[0].shape[0]
+    half, part = pair // 2, right_ref.shape[1] // 2
+    c = lax.axis_index("context")
+    for which, ref in enumerate(grads):
+        for s in range(2):
+            row = s * pair + (c if which == 0 else 1 - c) * half
+            left_ref[pl.ds(pl.multiple_of(row, half), half), :] = ref[s * half : (s + 1) * half, :]
+    for side, refs in enumerate(outputs):
+        at = pl.ds(pl.multiple_of((c if side == 0 else 1 - c) * part, part), part)
+        for s, ref in enumerate(refs):
+            right_ref[s * pair : (s + 1) * pair, at] = ref[...]
+
+
+def own_weight_kernel(
+    own_g_ref, own_p_ref, mine_ref, mine_x_ref, away_ref, away_x_ref,
+    total_ref, left_ref, right_ref,
+):
+    outputs = (mine_ref, mine_x_ref), (away_ref, away_x_ref)
+    weight_operands((own_g_ref, own_p_ref), outputs, left_ref, right_ref)
+    block = left_ref.shape[1] // 4
+    for n in range(4):
+        rows = slice(n * block, (n + 1) * block)
+        total_ref[rows, :] = dot(left_ref[:, rows], right_ref[...], TN).astype(BF16)
+
+
 def weight_kernel(
-    own_g_ref, near_g_ref, own_p_ref, bundle_ref, mine_ref, mine_x_ref, away_ref, away_x_ref,
-    weight_ref, left_ref, right_ref, done_ref, sems,
+    total_ref, near_g_ref, bundle_ref, weight_ref, left_ref, right_ref, done_ref, sems
 ):
-    pair, width = own_g_ref.shape
-    half, part = pair // 2, width // 2
+    pair, part = near_g_ref.shape[0], near_g_ref.shape[1] // 2
+    outputs = [
+        [bundle_ref.at[n * pair : (n + 1) * pair, s * part : (s + 1) * part] for s in range(2)]
+        for n in (1, 2)
+    ]
+    weight_operands((near_g_ref, bundle_ref.at[:pair]), outputs, left_ref, right_ref)
     blocks, block = done_ref.shape[:2]
-    c = lax.axis_index("context")
-    pieces = (own_g_ref, near_g_ref), (own_p_ref, bundle_ref.at[:pair])
-    for which, refs in enumerate(pieces):
-        for n, ref in enumerate(refs):
-            for s in range(2):
-                row = (2 * n + s) * pair + (c if which == 0 else 1 - c) * half
-                left_ref[pl.ds(pl.multiple_of(row, half), half), :] = ref[
-                    s * half : (s + 1) * half, :
-                ]
-    sides = (mine_ref, mine_x_ref), (away_ref, away_x_ref)
-    for side, refs in enumerate(sides):
-        at = pl.ds(pl.multiple_of((c if side == 0 else 1 - c) * part, part), part)
-        near = (side + 1) * pair
-        for s in range(2):
-            cols = slice(s * part, (s + 1) * part)
-            right_ref[s * pair : (s + 1) * pair, at] = refs[s][...]
-            right_ref[(s + 2) * pair : (s + 3) * pair, at] = bundle_ref[near : near + pair, cols]
     copies = []
     for n in range(blocks):
         rows = slice(n * block, (n + 1) * block)
-        done_ref[n] = dot(left_ref[:, rows], right_ref[...], TN)
+        done_ref[n] = total_ref[rows, :].astype(F32) + dot(left_ref[:, rows], right_ref[...], TN)
         copies.append(pltpu.make_async_copy(done_ref.at[n], weight_ref.at[rows, :], sems.at[n]))
         copies[-1].start()
     for copy in copies:
@@ -315,20 +334,22 @@
         [(c * 4 + f, (1 - c) * 4 + (f ^ 2)) for c in range(2) for f in range(4)],
     )
     from_x, from_y = over_x(send_x), over_y(send_y)
-    from_x, from_y, from_xy, peer_output = after((from_x, from_y, from_xy, peer_output))
+    from_x, from_y, from_xy, peer_output, out_x = after((from_x, from_y, from_xy, peer_output, out_x))
     own, send, send_q = call(
         backward_kernel,
         (
             shape((3 * rows, part), BF16),
-            shape((2 * rows, part), BF16),
-            shape((rows, part), BF16),
+            shape((5 * rows // 2, part), BF16),
+            shape((rows // 2, part), BF16),
         ),
         (counts, q, k, v, probs, output, keep, from_x, from_y, from_xy),
         smem=(0,),
         scratch=(pltpu.VMEM((total, part), BF16), pltpu.VMEM((3, total, part), BF16)),
     )
     peer = over_y(send)
-    near_g, peer_second, peer_output = after((near_g, peer_second, peer_output, send))[:3]
+    near_g, peer_second, peer_output, peer_first_z = after(
+        (near_g, peer_second, peer_output, peer_first_z, send)
+    )[:4]
     near_g = over_core(near_g)
     peer_second_z = over_z(peer_second)
     peer_x = over_x(peer_output)
@@ -343,18 +364,24 @@
         bundled,
     )
     bundle = over_core(bundle)
+    operands = (pltpu.VMEM((2 * total, width), BF16), pltpu.VMEM((2 * total, width), BF16))
+    weight_grad = call(
+        own_weight_kernel,
+        shape(out_weight.shape, BF16),
+        (own_g, own_p, output, out_x, peer_output, peer_x),
+        scratch=operands,
+    )
     weight_grad = call(
         weight_kernel,
         shape(out_weight.shape, F32),
-        (own_g, near_g, own_p, bundle, output, out_x, peer_output, peer_x),
+        (weight_grad, near_g, bundle),
         out=pl.ANY,
         scratch=(
-            pltpu.VMEM((4 * total, width), BF16),
-            pltpu.VMEM((4 * total, width), BF16),
+            *operands,
             pltpu.VMEM((4, width // 4, width), F32),
             pltpu.SemaphoreType.DMA((4,)),
         ),
-        vmem=16,
+        vmem=8,
     )
     weight_grad, own = after((weight_grad, own))
     grads = call(
@@ -362,7 +389,7 @@
         tuple(shape((rows, width), BF16) for _ in range(3)),
         (own, peer, peer_q),
         out=pl.ANY,
-        scratch=(pltpu.SemaphoreType.DMA((2, 3)),),
+        scratch=(pltpu.SemaphoreType.DMA((3, 3)),),
     )
     return (grads[0][None], grads[1][None], grads[2][None], weight_grad)
 

time: 57.3 us -> 55.3 us (0.965)
  waiting for transfers between devices: 16.9 us -> 11.1 us
  starting transfers between devices: 26 us -> 28.8 us
  Pallas kernels: 8.9 us -> 9.72 us
    ppermute x3, starting transfers between devices: 3.11 us -> 5.46 us  [packed_device(): over_x = lambda a: lax.ppermute(a, 'fsdp', [(i, i ^ 2) for i in range(4)])]
    ppermute x4, waiting for transfers between devices: 6.53 us -> 4.41 us  [packed_device(): over_z = lambda a: lax.ppermute(a, 'tensor', [(i, i ^ 1) for i in range(4)])]
    ppermute x8, waiting for transfers between devices: 1.99 us -> 0.08 us  [packed_device(): over_y = lambda a: lax.ppermute(a, 'context', [(0, 1), (1, 0)])]
    ppermute x3, waiting for transfers between devices: 1.54 us -> 0.01 us  [packed_device(): lax.ppermute(a, 'fsdp', [(i, i ^ 1) for i in range(4)])]
    pallas_call x7 -> x8, Pallas kernels: 8.9 us -> 9.72 us  [call(): pl.pallas_call(body, out_shape=outs, in_specs=[pl.BlockSpec(memory_space=...]
  transfers between devices with their start and end apart: 21 -> 21, of which waited for: 12 -> 8; matrix products, arithmetic and copies ran while one was open for 5% -> 5% of each run, Pallas kernels for 11% -> 16%
where the time goes in v4:
time: 55.3 us; the launch traced here: 55.1 us
  starting transfers between devices  28.8 us (52%)
  waiting for transfers between devices  11.1 us (20%)
  Pallas kernels  9.72 us (18%)
  local copies, waits for them, and re-layouts  3.14 us (6%)
  between operations  1.51 us (3%)
  other arithmetic  0.72 us (1%)
    ppermute x8, starting transfers between devices, packed_device(): over_y = lambda a: lax.ppermute(a, 'context', [(0, 1), (1, 0)])  10.9 us
    pallas_call x8, Pallas kernels, call(): pl.pallas_call(body, out_shape=outs, in_specs=[pl.BlockSpec(memory_space=...  9.72 us
    ppermute x4, starting transfers between devices, packed_device(): over_z = lambda a: lax.ppermute(a, 'tensor', [(i, i ^ 1) for i in range(4)])  7.02 us
    ppermute x3, starting transfers between devices, packed_device(): over_x = lambda a: lax.ppermute(a, 'fsdp', [(i, i ^ 2) for i in range(4)])  5.46 us
    ppermute x4, waiting for transfers between devices, packed_device(): over_z = lambda a: lax.ppermute(a, 'tensor', [(i, i ^ 1) for i in range(4)])  4.41 us
    ppermute x2, starting transfers between devices, packed_device(): lax.ppermute(packed, ('tensor', 'fsdp'), spread(a))  3.25 us
    ppermute x3, waiting for transfers between devices, packed_device(): over_x = lambda a: lax.ppermute(a, 'fsdp', [(i, i ^ 2) for i in range(4)])  2.66 us
    ppermute x2, waiting for transfers between devices, packed_device(): lax.ppermute(packed, ('tensor', 'fsdp'), spread(a))  2.38 us
  transfers between devices with their start and end apart: 21, of which 8 were waited for; matrix products, arithmetic and copies ran while one was open for 5% of the time, Pallas kernels for 16%

profile of v4, /device:TPU:0, one launch (start us, length us, event | category | flops | bytes accessed | tf_op | source)
XLA Modules:
  0.0 55.1 jit_solution(8114733987115758677)
XLA Ops:
  0.7 1.0 %slice_bitcast_fusion.1 = bf16[48,1024]{1,0:T(8,128)(2,1)S(1)} fusion(bf16[1,128,1024]{2,1,0:T(8,128)(2,1)} %param.11), kind=kLoop, calls=%fused_computation.10 | loop fusion | bytes 196608 | tf_op jit(solution)/shard_map/slice | solution.py:285
  2.1 2.6 %collective-permute-start = (bf16[48,1024]{1,0:T(8,128)(2,1)S(1)}, bf16[48,1024]{1,0:T(8,128)(2,1)S(1)}, u32[]{:S(2)}, u32[]{:S(2)}) collective-permute-start(bf16[48,1024]{1,0:T(8,128)(2,1)S(1)} %slice_bitcast_fusion.1), channel_id=1, source_target_pairs={{0,16},{16,0},{1,17},{17,1},{2,18},{18,2},{3,19},{19,3},{4,20},{20... | collective-permute-start | bytes 294920 | tf_op jit(solution)/shard_map/ppermute | solution.py:272
  5.3 1.0 %dynamic-slice_bitcast_fusion = (bf16[128,512]{1,0:T(8,128)(2,1)S(1)}, bf16[128,512]{1,0:T(8,128)(2,1)S(1)}) fusion(bf16[1,128,1024]{2,1,0:T(8,128)(2,1)} %param.10, s32[]{:T(128)S(6)} %select_n.5, bf16[1,128,1024]{2,1,0:T(8,128)(2,1)} %param.9), kind=kLoop, calls=%fused_computation.4 | loop fusion | bytes 524292 | tf_op jit(solution)/shard_map/dynamic_slice | solution.py:281
  6.3 0.7 %convert_bitcast_fusion = bf16[128]{0:T(256)(128)(2,1)S(1)} fusion(s32[1,128]{1,0:T(1,128)} %param.15), kind=kLoop, calls=%fused_computation.11 | loop fusion | flops 128 | bytes 768 | tf_op jit(solution)/shard_map/broadcast_in_dim | solution.py:289
  7.0 1.1 %slice_bitcast_fusion.own_ref = bf16[80,1024]{1,0:T(8,128)(2,1)S(1)} fusion(bf16[1,128,1024]{2,1,0:T(8,128)(2,1)} %param.11), kind=kLoop, calls=%fused_computation.3 | loop fusion | bytes 327680 | tf_op jit(solution)/shard_map/slice | solution.py:293
  8.5 1.8 %collective-permute-start.6 = (bf16[400,512]{1,0:T(8,128)(2,1)S(1)}, bf16[400,512]{1,0:T(8,128)(2,1)S(1)}, u32[]{:S(2)}, u32[]{:S(2)}) collective-permute-start(bf16[400,512]{1,0:T(8,128)(2,1)S(1)} %get-tuple-element.120), channel_id=1, source_target_pairs={{0,16},{16,0},{1,17},{17,1},{2,18},{18,2},{3,19},{19,3},{4,20},{20... | collective-permute-start | bytes 1228808 | tf_op jit(solution)/shard_map/ppermute | solution.py:272
  10.3 2.6 %collective-permute-start.4 = (bf16[80,1024]{1,0:T(8,128)(2,1)S(1)}, bf16[80,1024]{1,0:T(8,128)(2,1)S(1)}, u32[]{:S(2)}, u32[]{:S(2)}) collective-permute-start(bf16[80,1024]{1,0:T(8,128)(2,1)S(1)} %shard_map.111), channel_id=1, source_target_pairs={{0,8},{1,9},{2,0},{3,1},{4,12},{5,13},{6,4},{7,5},{8,10},{9,11},{1... | collective-permute-start | bytes 491528 | tf_op jit(solution)/shard_map/ppermute | solution.py:298
  13.6 2.4 %collective-permute-done.4.b10_ref = bf16[80,1024]{1,0:T(8,128)(2,1)S(1)} collective-permute-done((bf16[80,1024]{1,0:T(8,128)(2,1)S(1)}, bf16[80,1024]{1,0:T(8,128)(2,1)S(1)}, u32[]{:S(2)}, u32[]{:S(2)}) %collective-permute-start.4) | collective-permute-done | bytes 163872 | tf_op jit(solution)/shard_map/ppermute | solution.py:298
  15.9 0.8 %collective-permute-start.8 = (bf16[80,1024]{1,0:T(8,128)(2,1)S(1)}, bf16[80,1024]{1,0:T(8,128)(2,1)S(1)}, u32[]{:S(2)}, u32[]{:S(2)}) collective-permute-start(bf16[80,1024]{1,0:T(8,128)(2,1)S(1)} %collective-permute-done.4.b10_ref), channel_id=1, source_target_pairs={{0,16},{16,0},{1,17},{17,1},{2,18},{18,2},{3,19},{19,3},{4,20},{20... | collective-permute-start | bytes 491528 | tf_op jit(solution)/shard_map/ppermute | solution.py:272
  16.8 4.9 %collective-permute-start.5 = (bf16[80,1024]{1,0:T(8,128)(2,1)S(1)}, bf16[80,1024]{1,0:T(8,128)(2,1)S(1)}, u32[]{:S(2)}, u32[]{:S(2)}) collective-permute-start(bf16[80,1024]{1,0:T(8,128)(2,1)S(1)} %collective-permute-done.4.b10_ref), channel_id=1, source_target_pairs={{0,4},{4,0},{8,12},{12,8},{1,5},{5,1},{9,13},{13,9},{2,6},{6,2},{1... | collective-permute-start | bytes 491528 | tf_op jit(solution)/shard_map/ppermute | solution.py:299
  21.7 1.2 %collective-permute-start.7 = (bf16[80,1024]{1,0:T(8,128)(2,1)S(1)}, bf16[80,1024]{1,0:T(8,128)(2,1)S(1)}, u32[]{:S(2)}, u32[]{:S(2)}) collective-permute-start(bf16[80,1024]{1,0:T(8,128)(2,1)S(1)} %collective-permute-done.2.b00_ref), channel_id=1, source_target_pairs={{0,16},{16,0},{1,17},{17,1},{2,18},{18,2},{3,19},{19,3},{4,20},{20... | collective-permute-start | bytes 491528 | tf_op jit(solution)/shard_map/ppermute | solution.py:272
  22.9 1.9 %shard_map.112 = (bf16[160,512]{1,0:T(8,128)(2,1)S(1)}, bf16[160,512]{1,0:T(8,128)(2,1)S(1)}, bf16[160,512]{1,0:T(8,128)(2,1)S(1)}, f32[4,160,160]{2,1,0:T(8,128)S(1)}, bf16[160,512]{1,0:T(8,128)(2,1)S(1)}) custom-call(s32[1,1]{1,0:T(1,128)S(6)} %copy.12.count_ref, f32[8]{0:T(128)S(1)} %copy-done.2, bf16[400,512]{1,0:T(8,128)(2,1)S(1)} %get-tuple-element.121.mine_ref, ...), custom_call_target="tpu_custom_call" | custom-call | tf_op jit(solution)/shard_map/pallas_call | solution.py:31
  24.8 3.5 %collective-permute-start.13 = (bf16[160,512]{1,0:T(8,128)(2,1)S(1)}, bf16[160,512]{1,0:T(8,128)(2,1)S(1)}, u32[]{:S(2)}, u32[]{:S(2)}) collective-permute-start(bf16[160,512]{1,0:T(8,128)(2,1)S(1)} %get-tuple-element.105.output_ref.mine_ref), channel_id=1, source_target_pairs={{0,2},{1,3},{2,0},{3,1},{4,6},{5,7},{6,4},{7,5},{8,10},{9,11},{10,... | collective-permute-start | bytes 491528 | tf_op jit(solution)/shard_map/ppermute | solution.py:273
  28.3 1.2 %collective-permute-start.12 = (bf16[160,512]{1,0:T(8,128)(2,1)S(1)}, bf16[160,512]{1,0:T(8,128)(2,1)S(1)}, u32[]{:S(2)}, u32[]{:S(2)}) collective-permute-start(bf16[160,512]{1,0:T(8,128)(2,1)S(1)} %get-tuple-element.105.output_ref.mine_ref), channel_id=1, source_target_pairs={{0,16},{16,0},{1,17},{17,1},{2,18},{18,2},{3,19},{19,3},{4,20},{20... | collective-permute-start | bytes 491528 | tf_op jit(solution)/shard_map/ppermute | solution.py:272
  29.5 0.8 %collective-permute-done.3.b01_ref = bf16[80,1024]{1,0:T(8,128)(2,1)S(1)} collective-permute-done((bf16[80,1024]{1,0:T(8,128)(2,1)S(1)}, bf16[80,1024]{1,0:T(8,128)(2,1)S(1)}, u32[]{:S(2)}, u32[]{:S(2)}) %collective-permute-start.3) | collective-permute-done | bytes 163872 | tf_op jit(solution)/shard_map/ppermute | solution.py:299
  30.3 1.0 %shard_map.113 = (f32[80,512]{1,0:T(8,128)S(1)}, bf16[80,512]{1,0:T(8,128)(2,1)S(1)}, bf16[80,512]{1,0:T(8,128)(2,1)S(1)}, bf16[80,512]{1,0:T(8,128)(2,1)S(1)}, ...) custom-call(bf16[80,1024]{1,0:T(8,128)(2,1)S(1)} %collective-permute-done.2.b00_ref, ...), custom_call_target="tpu_custom_call" | custom-call | tf_op jit(solution)/shard_map/pallas_call | solution.py:31
  31.3 1.1 %collective-permute-start.9 = (bf16[80,512]{1,0:T(8,128)(2,1)S(1)}, bf16[80,512]{1,0:T(8,128)(2,1)S(1)}, u32[]{:S(2)}, u32[]{:S(2)}) collective-permute-start(bf16[80,512]{1,0:T(8,128)(2,1)S(1)} %get-tuple-element.82), channel_id=1, source_target_pairs={{0,2},{1,3},{2,0},{3,1},{4,6},{5,7},{6,4},{7,5},{8,10},{9,11},{10,... | collective-permute-start | bytes 245768 | tf_op jit(solution)/shard_map/ppermute | solution.py:273
  32.4 1.2 %collective-permute-start.10 = (bf16[80,512]{1,0:T(8,128)(2,1)S(1)}, bf16[80,512]{1,0:T(8,128)(2,1)S(1)}, u32[]{:S(2)}, u32[]{:S(2)}) collective-permute-start(bf16[80,512]{1,0:T(8,128)(2,1)S(1)} %get-tuple-element.83), channel_id=1, source_target_pairs={{0,16},{16,0},{1,17},{17,1},{2,18},{18,2},{3,19},{19,3},{4,20},{20... | collective-permute-start | bytes 245768 | tf_op jit(solution)/shard_map/ppermute | solution.py:272
  33.6 1.2 %collective-permute-start.11 = (bf16[80,512]{1,0:T(8,128)(2,1)S(1)}, bf16[80,512]{1,0:T(8,128)(2,1)S(1)}, u32[]{:S(2)}, u32[]{:S(2)}) collective-permute-start(bf16[80,512]{1,0:T(8,128)(2,1)S(1)} %get-tuple-element.84), channel_id=1, source_target_pairs={{0,18},{1,19},{2,16},{3,17},{16,2},{17,3},{18,0},{19,1},{4,22},{5,... | collective-permute-start | bytes 245768 | tf_op jit(solution)/shard_map/ppermute | solution.py:331
  34.8 1.5 %collective-permute-done.9.from_x_ref = bf16[80,512]{1,0:T(8,128)(2,1)S(1)} collective-permute-done((bf16[80,512]{1,0:T(8,128)(2,1)S(1)}, bf16[80,512]{1,0:T(8,128)(2,1)S(1)}, u32[]{:S(2)}, u32[]{:S(2)}) %collective-permute-start.9) | collective-permute-done | bytes 81952 | tf_op jit(solution)/shard_map/ppermute | solution.py:273
  36.3 0.9 %collective-permute-start.14 = (bf16[80,1024]{1,0:T(8,128)(2,1)S(1)}, bf16[80,1024]{1,0:T(8,128)(2,1)S(1)}, u32[]{:S(2)}, u32[]{:S(2)}) collective-permute-start(bf16[80,1024]{1,0:T(8,128)(2,1)S(1)} %collective-permute-done.7.p00_ref), channel_id=1, source_target_pairs={{0,4},{4,0},{8,12},{12,8},{1,5},{5,1},{9,13},{13,9},{2,6},{6,2},{1... | collective-permute-start | bytes 491528 | tf_op jit(solution)/shard_map/ppermute | solution.py:299
  37.3 1.6 %collective-permute-done.11.from_xy_ref = bf16[80,512]{1,0:T(8,128)(2,1)S(1)} collective-permute-done((bf16[80,512]{1,0:T(8,128)(2,1)S(1)}, bf16[80,512]{1,0:T(8,128)(2,1)S(1)}, u32[]{:S(2)}, u32[]{:S(2)}) %collective-permute-start.11) | collective-permute-done | bytes 81952 | tf_op jit(solution)/shard_map/ppermute | solution.py:331
  38.9 1.5 %shard_map.114 = (bf16[384,512]{1,0:T(8,128)(2,1)S(1)}, bf16[320,512]{1,0:T(8,128)(2,1)S(1)}, bf16[64,512]{1,0:T(8,128)(2,1)S(1)}) custom-call(s32[1,1]{1,0:T(1,128)S(6)} %copy.12.count_ref, bf16[160,512]{1,0:T(8,128)(2,1)S(1)} %get-tuple-element.86.q_ref, bf16[160,512]{1,0:T(8,128)(2,1)S(1)} %get-tuple-element.87.k_ref, ...), custom_call_target="tpu_custom_call" | custom-call | tf_op jit(solution)/shard_map/pallas_call | solution.py:31
  40.5 0.9 %collective-permute-start.17 = (bf16[320,512]{1,0:T(8,128)(2,1)S(1)}, bf16[320,512]{1,0:T(8,128)(2,1)S(1)}, u32[]{:S(2)}, u32[]{:S(2)}) collective-permute-start(bf16[320,512]{1,0:T(8,128)(2,1)S(1)} %get-tuple-element.95), channel_id=1, source_target_pairs={{0,16},{16,0},{1,17},{17,1},{2,18},{18,2},{3,19},{19,3},{4,20},{20... | collective-permute-start | bytes 983048 | tf_op jit(solution)/shard_map/ppermute | solution.py:272
  41.7 1.1 %collective-permute-start.15 = (bf16[80,1024]{1,0:T(8,128)(2,1)S(1)}, bf16[80,1024]{1,0:T(8,128)(2,1)S(1)}, u32[]{:S(2)}, u32[]{:S(2)}) collective-permute-start(bf16[80,1024]{1,0:T(8,128)(2,1)S(1)} %collective-permute-done.8.p10_ref), channel_id=1, source_target_pairs={{0,4},{4,0},{8,12},{12,8},{1,5},{5,1},{9,13},{13,9},{2,6},{6,2},{1... | collective-permute-start | bytes 491528 | tf_op jit(solution)/shard_map/ppermute | solution.py:299
  42.8 0.9 %collective-permute-start.16 = (bf16[160,512]{1,0:T(8,128)(2,1)S(1)}, bf16[160,512]{1,0:T(8,128)(2,1)S(1)}, u32[]{:S(2)}, u32[]{:S(2)}) collective-permute-start(bf16[160,512]{1,0:T(8,128)(2,1)S(1)} %collective-permute-done.12.away_ref), channel_id=1, source_target_pairs={{0,2},{1,3},{2,0},{3,1},{4,6},{5,7},{6,4},{7,5},{8,10},{9,11},{10,... | collective-permute-start | bytes 491528 | tf_op jit(solution)/shard_map/ppermute | solution.py:273
  43.7 3.3 %collective-permute-done.15.p11_ref = bf16[80,1024]{1,0:T(8,128)(2,1)S(1)} collective-permute-done((bf16[80,1024]{1,0:T(8,128)(2,1)S(1)}, bf16[80,1024]{1,0:T(8,128)(2,1)S(1)}, u32[]{:S(2)}, u32[]{:S(2)}) %collective-permute-start.15) | collective-permute-done | bytes 163872 | tf_op jit(solution)/shard_map/ppermute | solution.py:299
  47.0 1.1 %collective-permute-done.16.away_x_ref = bf16[160,512]{1,0:T(8,128)(2,1)S(1)} collective-permute-done((bf16[160,512]{1,0:T(8,128)(2,1)S(1)}, bf16[160,512]{1,0:T(8,128)(2,1)S(1)}, u32[]{:S(2)}, u32[]{:S(2)}) %collective-permute-start.16) | collective-permute-done | bytes 163872 | tf_op jit(solution)/shard_map/ppermute | solution.py:273
  48.8 1.2 %collective-permute-start.20 = (bf16[64,512]{1,0:T(8,128)(2,1)S(1)}, bf16[64,512]{1,0:T(8,128)(2,1)S(1)}, u32[]{:S(2)}, u32[]{:S(2)}) collective-permute-start(bf16[64,512]{1,0:T(8,128)(2,1)S(1)} %get-tuple-element.115), channel_id=1, source_target_pairs={{0,16},{16,0},{1,17},{17,1},{2,18},{18,2},{3,19},{19,3},{4,20},{20... | collective-permute-start | bytes 196616 | tf_op jit(solution)/shard_map/ppermute | solution.py:272
  50.0 1.4 %shard_map.116.total_ref = bf16[1024,1024]{1,0:T(8,128)(2,1)S(1)} custom-call(bf16[160,1024]{1,0:T(8,128)(2,1)S(1)} %get-tuple-element.78.own_g_ref, bf16[160,1024]{1,0:T(8,128)(2,1)S(1)} %get-tuple-element.109.own_p_ref, bf16[160,512]{1,0:T(8,128)(2,1)S(1)} %get-tuple-element.105.output_ref.mine_ref, ...), custom_call_target="tpu_custom_call" | custom-call | tf_op jit(solution)/shard_map/pallas_call | solution.py:31
  51.4 2.6 %shard_map.117 = f32[1024,1024]{1,0:T(8,128)} custom-call(bf16[1024,1024]{1,0:T(8,128)(2,1)S(1)} %shard_map.116.total_ref, bf16[160,1024]{1,0:T(8,128)(2,1)S(1)} %collective-permute-done.18.near_g_ref, bf16[480,1024]{1,0:T(8,128)(2,1)S(1)} %collective-permute-done.19.bundle_ref), custom_call_target="tpu_custom_call" | custom-call | tf_op jit(solution)/shard_map/pallas_call | solution.py:31
  54.1 1.0 %shard_map.118 = (bf16[128,1024]{1,0:T(8,128)(2,1)}, bf16[128,1024]{1,0:T(8,128)(2,1)}, bf16[128,1024]{1,0:T(8,128)(2,1)}) custom-call(bf16[384,512]{1,0:T(8,128)(2,1)S(1)} %get-tuple-element.113.own_ref, bf16[320,512]{1,0:T(8,128)(2,1)S(1)} %collective-permute-done.17.peer_ref, bf16[64,512]{1,0:T(8,128)(2,1)S(1)} %collective-permute-done.20.peer_q_ref), custom_call_target="tpu_custom_call" | custom-call | tf_op jit(solution)/shard_map/pallas_call | solution.py:31
  (37 shorter events, 2.6 us)
Async XLA Ops:
  0.6 7.5 %copy-start = (bf16[1,128,1024]{2,1,0:T(8,128)(2,1)S(1)}, bf16[1,128,1024]{2,1,0:T(8,128)(2,1)}, u32[]{:S(2)}) copy-start(bf16[1,128,1024]{2,1,0:T(8,128)(2,1)} %param.8) | copy-start | bytes 786436
  0.6 7.8 %copy-start.3 = (bf16[1,128,1024]{2,1,0:T(8,128)(2,1)S(1)}, bf16[1,128,1024]{2,1,0:T(8,128)(2,1)}, u32[]{:S(2)}) copy-start(bf16[1,128,1024]{2,1,0:T(8,128)(2,1)} %param.10) | copy-start | bytes 786436
  0.7 7.8 %copy-start.4 = (bf16[1,128,1024]{2,1,0:T(8,128)(2,1)S(1)}, bf16[1,128,1024]{2,1,0:T(8,128)(2,1)}, u32[]{:S(2)}) copy-start(bf16[1,128,1024]{2,1,0:T(8,128)(2,1)} %param.9) | copy-start | bytes 786436
  0.7 22.2 %copy-start.2 = (f32[8]{0:T(128)S(1)}, f32[8]{0:T(128)}, u32[]{:S(2)}) copy-start(f32[8]{0:T(128)} %slopes_ref.1) | copy-start | bytes 100
  1.6 6.7 %collective-permute-start.1 = (bf16[1024,1024]{1,0:T(8,128)(2,1)}, bf16[1024,1024]{1,0:T(8,128)(2,1)S(1)}, u32[]{:S(2)}, u32[]{:S(2)}) collective-permute-start(bf16[1024,1024]{1,0:T(8,128)(2,1)} %own_w_ref.1), channel_id=1, source_target_pairs={{0,1},{1,0},{2,3},{3,2},{4,5},{5,4},{6,7},{7,6},{8,9},{9,8},{10,11... | collective-permute-start | bytes 6291464 | tf_op jit(solution)/shard_map/ppermute | solution.py:274
  2.1 6.0 %collective-permute-start = (bf16[48,1024]{1,0:T(8,128)(2,1)S(1)}, bf16[48,1024]{1,0:T(8,128)(2,1)S(1)}, u32[]{:S(2)}, u32[]{:S(2)}) collective-permute-start(bf16[48,1024]{1,0:T(8,128)(2,1)S(1)} %slice_bitcast_fusion.1), channel_id=1, source_target_pairs={{0,16},{16,0},{1,17},{17,1},{2,18},{18,2},{3,19},{19,3},{4,20},{20... | collective-permute-start | bytes 294920 | tf_op jit(solution)/shard_map/ppermute | solution.py:272
  7.0 23.3 %copy-start.1 = (bf16[1024,1024]{1,0:T(8,128)(2,1)S(1)}, bf16[1024,1024]{1,0:T(8,128)(2,1)}, u32[]{:S(2)}) copy-start(bf16[1024,1024]{1,0:T(8,128)(2,1)} %own_w_ref.1) | copy-start | bytes 6291460
  8.5 14.4 %collective-permute-start.6 = (bf16[400,512]{1,0:T(8,128)(2,1)S(1)}, bf16[400,512]{1,0:T(8,128)(2,1)S(1)}, u32[]{:S(2)}, u32[]{:S(2)}) collective-permute-start(bf16[400,512]{1,0:T(8,128)(2,1)S(1)} %get-tuple-element.120), channel_id=1, source_target_pairs={{0,16},{16,0},{1,17},{17,1},{2,18},{18,2},{3,19},{19,3},{4,20},{20... | collective-permute-start | bytes 1228808 | tf_op jit(solution)/shard_map/ppermute | solution.py:272
  10.3 5.6 %collective-permute-start.4 = (bf16[80,1024]{1,0:T(8,128)(2,1)S(1)}, bf16[80,1024]{1,0:T(8,128)(2,1)S(1)}, u32[]{:S(2)}, u32[]{:S(2)}) collective-permute-start(bf16[80,1024]{1,0:T(8,128)(2,1)S(1)} %shard_map.111), channel_id=1, source_target_pairs={{0,8},{1,9},{2,0},{3,1},{4,12},{5,13},{6,4},{7,5},{8,10},{9,11},{1... | collective-permute-start | bytes 491528 | tf_op jit(solution)/shard_map/ppermute | solution.py:298
  12.9 8.8 %collective-permute-start.2 = (bf16[80,1024]{1,0:T(8,128)(2,1)S(1)}, bf16[80,1024]{1,0:T(8,128)(2,1)S(1)}, u32[]{:S(2)}, u32[]{:S(2)}) collective-permute-start(bf16[80,1024]{1,0:T(8,128)(2,1)S(1)} %shard_map.111), channel_id=1, source_target_pairs={{0,0},{1,1},{2,8},{3,9},{4,4},{5,5},{6,12},{7,13},{8,2},{9,3},{10,... | collective-permute-start | bytes 491528 | tf_op jit(solution)/shard_map/ppermute | solution.py:298
  15.9 12.3 %collective-permute-start.8 = (bf16[80,1024]{1,0:T(8,128)(2,1)S(1)}, bf16[80,1024]{1,0:T(8,128)(2,1)S(1)}, u32[]{:S(2)}, u32[]{:S(2)}) collective-permute-start(bf16[80,1024]{1,0:T(8,128)(2,1)S(1)} %collective-permute-done.4.b10_ref), channel_id=1, source_target_pairs={{0,16},{16,0},{1,17},{17,1},{2,18},{18,2},{3,19},{19,3},{4,20},{20... | collective-permute-start | bytes 491528 | tf_op jit(solution)/shard_map/ppermute | solution.py:272
  16.8 12.7 %collective-permute-start.5 = (bf16[80,1024]{1,0:T(8,128)(2,1)S(1)}, bf16[80,1024]{1,0:T(8,128)(2,1)S(1)}, u32[]{:S(2)}, u32[]{:S(2)}) collective-permute-start(bf16[80,1024]{1,0:T(8,128)(2,1)S(1)} %collective-permute-done.4.b10_ref), channel_id=1, source_target_pairs={{0,4},{4,0},{8,12},{12,8},{1,5},{5,1},{9,13},{13,9},{2,6},{6,2},{1... | collective-permute-start | bytes 491528 | tf_op jit(solution)/shard_map/ppermute | solution.py:299
  21.7 7.8 %collective-permute-start.7 = (bf16[80,1024]{1,0:T(8,128)(2,1)S(1)}, bf16[80,1024]{1,0:T(8,128)(2,1)S(1)}, u32[]{:S(2)}, u32[]{:S(2)}) collective-permute-start(bf16[80,1024]{1,0:T(8,128)(2,1)S(1)} %collective-permute-done.2.b00_ref), channel_id=1, source_target_pairs={{0,16},{16,0},{1,17},{17,1},{2,18},{18,2},{3,19},{19,3},{4,20},{20... | collective-permute-start | bytes 491528 | tf_op jit(solution)/shard_map/ppermute | solution.py:272
  22.9 7.4 %collective-permute-start.3 = (bf16[80,1024]{1,0:T(8,128)(2,1)S(1)}, bf16[80,1024]{1,0:T(8,128)(2,1)S(1)}, u32[]{:S(2)}, u32[]{:S(2)}) collective-permute-start(bf16[80,1024]{1,0:T(8,128)(2,1)S(1)} %collective-permute-done.2.b00_ref), channel_id=1, source_target_pairs={{0,4},{4,0},{8,12},{12,8},{1,5},{5,1},{9,13},{13,9},{2,6},{6,2},{1... | collective-permute-start | bytes 491528 | tf_op jit(solution)/shard_map/ppermute | solution.py:299
  24.8 14.1 %collective-permute-start.13 = (bf16[160,512]{1,0:T(8,128)(2,1)S(1)}, bf16[160,512]{1,0:T(8,128)(2,1)S(1)}, u32[]{:S(2)}, u32[]{:S(2)}) collective-permute-start(bf16[160,512]{1,0:T(8,128)(2,1)S(1)} %get-tuple-element.105.output_ref.mine_ref), channel_id=1, source_target_pairs={{0,2},{1,3},{2,0},{3,1},{4,6},{5,7},{6,4},{7,5},{8,10},{9,11},{10,... | collective-permute-start | bytes 491528 | tf_op jit(solution)/shard_map/ppermute | solution.py:273
  28.3 10.7 %collective-permute-start.12 = (bf16[160,512]{1,0:T(8,128)(2,1)S(1)}, bf16[160,512]{1,0:T(8,128)(2,1)S(1)}, u32[]{:S(2)}, u32[]{:S(2)}) collective-permute-start(bf16[160,512]{1,0:T(8,128)(2,1)S(1)} %get-tuple-element.105.output_ref.mine_ref), channel_id=1, source_target_pairs={{0,16},{16,0},{1,17},{17,1},{2,18},{18,2},{3,19},{19,3},{4,20},{20... | collective-permute-start | bytes 491528 | tf_op jit(solution)/shard_map/ppermute | solution.py:272
  31.3 5.1 %collective-permute-start.9 = (bf16[80,512]{1,0:T(8,128)(2,1)S(1)}, bf16[80,512]{1,0:T(8,128)(2,1)S(1)}, u32[]{:S(2)}, u32[]{:S(2)}) collective-permute-start(bf16[80,512]{1,0:T(8,128)(2,1)S(1)} %get-tuple-element.82), channel_id=1, source_target_pairs={{0,2},{1,3},{2,0},{3,1},{4,6},{5,7},{6,4},{7,5},{8,10},{9,11},{10,... | collective-permute-start | bytes 245768 | tf_op jit(solution)/shard_map/ppermute | solution.py:273
  32.4 5.0 %collective-permute-start.10 = (bf16[80,512]{1,0:T(8,128)(2,1)S(1)}, bf16[80,512]{1,0:T(8,128)(2,1)S(1)}, u32[]{:S(2)}, u32[]{:S(2)}) collective-permute-start(bf16[80,512]{1,0:T(8,128)(2,1)S(1)} %get-tuple-element.83), channel_id=1, source_target_pairs={{0,16},{16,0},{1,17},{17,1},{2,18},{18,2},{3,19},{19,3},{4,20},{20... | collective-permute-start | bytes 245768 | tf_op jit(solution)/shard_map/ppermute | solution.py:272
  33.6 5.3 %collective-permute-start.11 = (bf16[80,512]{1,0:T(8,128)(2,1)S(1)}, bf16[80,512]{1,0:T(8,128)(2,1)S(1)}, u32[]{:S(2)}, u32[]{:S(2)}) collective-permute-start(bf16[80,512]{1,0:T(8,128)(2,1)S(1)} %get-tuple-element.84), channel_id=1, source_target_pairs={{0,18},{1,19},{2,16},{3,17},{16,2},{17,3},{18,0},{19,1},{4,22},{5,... | collective-permute-start | bytes 245768 | tf_op jit(solution)/shard_map/ppermute | solution.py:331
  36.3 5.3 %collective-permute-start.14 = (bf16[80,1024]{1,0:T(8,128)(2,1)S(1)}, bf16[80,1024]{1,0:T(8,128)(2,1)S(1)}, u32[]{:S(2)}, u32[]{:S(2)}) collective-permute-start(bf16[80,1024]{1,0:T(8,128)(2,1)S(1)} %collective-permute-done.7.p00_ref), channel_id=1, source_target_pairs={{0,4},{4,0},{8,12},{12,8},{1,5},{5,1},{9,13},{13,9},{2,6},{6,2},{1... | collective-permute-start | bytes 491528 | tf_op jit(solution)/shard_map/ppermute | solution.py:299
  40.5 7.7 %collective-permute-start.17 = (bf16[320,512]{1,0:T(8,128)(2,1)S(1)}, bf16[320,512]{1,0:T(8,128)(2,1)S(1)}, u32[]{:S(2)}, u32[]{:S(2)}) collective-permute-start(bf16[320,512]{1,0:T(8,128)(2,1)S(1)} %get-tuple-element.95), channel_id=1, source_target_pairs={{0,16},{16,0},{1,17},{17,1},{2,18},{18,2},{3,19},{19,3},{4,20},{20... | collective-permute-start | bytes 983048 | tf_op jit(solution)/shard_map/ppermute | solution.py:272
  41.7 5.3 %collective-permute-start.15 = (bf16[80,1024]{1,0:T(8,128)(2,1)S(1)}, bf16[80,1024]{1,0:T(8,128)(2,1)S(1)}, u32[]{:S(2)}, u32[]{:S(2)}) collective-permute-start(bf16[80,1024]{1,0:T(8,128)(2,1)S(1)} %collective-permute-done.8.p10_ref), channel_id=1, source_target_pairs={{0,4},{4,0},{8,12},{12,8},{1,5},{5,1},{9,13},{13,9},{2,6},{6,2},{1... | collective-permute-start | bytes 491528 | tf_op jit(solution)/shard_map/ppermute | solution.py:299
  42.8 5.3 %collective-permute-start.16 = (bf16[160,512]{1,0:T(8,128)(2,1)S(1)}, bf16[160,512]{1,0:T(8,128)(2,1)S(1)}, u32[]{:S(2)}, u32[]{:S(2)}) collective-permute-start(bf16[160,512]{1,0:T(8,128)(2,1)S(1)} %collective-permute-done.12.away_ref), channel_id=1, source_target_pairs={{0,2},{1,3},{2,0},{3,1},{4,6},{5,7},{6,4},{7,5},{8,10},{9,11},{10,... | collective-permute-start | bytes 491528 | tf_op jit(solution)/shard_map/ppermute | solution.py:273
  48.2 3.2 %collective-permute-start.19 = (bf16[480,1024]{1,0:T(8,128)(2,1)S(1)}, bf16[480,1024]{1,0:T(8,128)(2,1)S(1)}, u32[]{:S(2)}, u32[]{:S(2)}) collective-permute-start(bf16[480,1024]{1,0:T(8,128)(2,1)S(1)} %get-tuple-element.111), channel_id=1, source_target_pairs={{0,1},{1,0},{2,3},{3,2},{4,5},{5,4},{6,7},{7,6},{8,9},{9,8},{10,11... | collective-permute-start | bytes 2949128 | tf_op jit(solution)/shard_map/ppermute | solution.py:274
  48.3 3.1 %collective-permute-start.18 = (bf16[160,1024]{1,0:T(8,128)(2,1)S(1)}, bf16[160,1024]{1,0:T(8,128)(2,1)S(1)}, u32[]{:S(2)}, u32[]{:S(2)}) collective-permute-start(bf16[160,1024]{1,0:T(8,128)(2,1)S(1)} %get-tuple-element.110), channel_id=1, source_target_pairs={{0,1},{1,0},{2,3},{3,2},{4,5},{5,4},{6,7},{7,6},{8,9},{9,8},{10,11... | collective-permute-start | bytes 983048 | tf_op jit(solution)/shard_map/ppermute | solution.py:274
  48.8 5.3 %collective-permute-start.20 = (bf16[64,512]{1,0:T(8,128)(2,1)S(1)}, bf16[64,512]{1,0:T(8,128)(2,1)S(1)}, u32[]{:S(2)}, u32[]{:S(2)}) collective-permute-start(bf16[64,512]{1,0:T(8,128)(2,1)S(1)} %get-tuple-element.115), channel_id=1, source_target_pairs={{0,16},{16,0},{1,17},{17,1},{2,18},{18,2},{3,19},{19,3},{4,20},{20... | collective-permute-start | bytes 196616 | tf_op jit(solution)/shard_map/ppermute | solution.py:272

commit v5 on v4

--- a/solution.py
+++ b/solution.py
@@ -313,8 +313,8 @@
     out_x = over_x(output)
     peer_output = over_y(output)
     peer_first, peer_second = over_y(first), over_y(second)
-    peer_first_z = over_z(peer_first)
-    *blocks, output, peer_first, peer_second = after((*blocks, output, peer_first, peer_second))
+    peer_second_z = over_z(peer_second)
+    *blocks, output, peer_second = after((*blocks, output, peer_second))
     keep, send_x, send_y, send_xy, own_g, near_g = call(
         partial_kernel,
         (
@@ -334,7 +334,9 @@
         [(c * 4 + f, (1 - c) * 4 + (f ^ 2)) for c in range(2) for f in range(4)],
     )
     from_x, from_y = over_x(send_x), over_y(send_y)
-    from_x, from_y, from_xy, peer_output, out_x = after((from_x, from_y, from_xy, peer_output, out_x))
+    from_x, from_y, from_xy, peer_output, out_x, peer_first = after(
+        (from_x, from_y, from_xy, peer_output, out_x, peer_first)
+    )
     own, send, send_q = call(
         backward_kernel,
         (
@@ -347,11 +349,11 @@
         scratch=(pltpu.VMEM((total, part), BF16), pltpu.VMEM((3, total, part), BF16)),
     )
     peer = over_y(send)
-    near_g, peer_second, peer_output, peer_first_z = after(
-        (near_g, peer_second, peer_output, peer_first_z, send)
+    near_g, peer_first, peer_output, peer_second_z = after(
+        (near_g, peer_first, peer_output, peer_second_z, send)
     )[:4]
     near_g = over_core(near_g)
-    peer_second_z = over_z(peer_second)
+    peer_first_z = over_z(peer_first)
     peer_x = over_x(peer_output)
     bundled = (
         peer_first, peer_first_z, peer_second, peer_second_z, output, out_x, peer_output, peer_x
@@ -378,8 +380,8 @@
         out=pl.ANY,
         scratch=(
             *operands,
-            pltpu.VMEM((4, width // 4, width), F32),
-            pltpu.SemaphoreType.DMA((4,)),
+            pltpu.VMEM((8, width // 8, width), F32),
+            pltpu.SemaphoreType.DMA((8,)),
         ),
         vmem=8,
     )

time: 55.3 us -> 55.1 us (level)
  waiting for transfers between devices: 11.1 us -> 11.8 us
  starting transfers between devices: 28.8 us -> 28.1 us
    ppermute x4, starting transfers between devices: 7.02 us -> 6.37 us  [packed_device(): over_z = lambda a: lax.ppermute(a, 'tensor', [(i, i ^ 1) for i in range(4)])]
    ppermute x8, waiting for transfers between devices: 0.08 us -> 0.68 us  [packed_device(): over_y = lambda a: lax.ppermute(a, 'context', [(0, 1), (1, 0)])]
    ppermute x4, waiting for transfers between devices: 4.41 us -> 5 us  [packed_device(): over_z = lambda a: lax.ppermute(a, 'tensor', [(i, i ^ 1) for i in range(4)])]
  transfers between devices with their start and end apart: 21 -> 21, of which waited for: 8 -> 9; matrix products, arithmetic and copies ran while one was open for 5% -> 5% of each run, Pallas kernels for 16% -> 16%
where the time goes in v5:
time: 55.1 us; the launch traced here: 54.9 us
  starting transfers between devices  28.1 us (51%)
  waiting for transfers between devices  11.8 us (21%)
  Pallas kernels  9.6 us (17%)
  local copies, waits for them, and re-layouts  3.14 us (6%)
  between operations  1.51 us (3%)
  other arithmetic  0.72 us (1%)
    ppermute x8, starting transfers between devices, packed_device(): over_y = lambda a: lax.ppermute(a, 'context', [(0, 1), (1, 0)])  10.9 us
    pallas_call x8, Pallas kernels, call(): pl.pallas_call(body, out_shape=outs, in_specs=[pl.BlockSpec(memory_space=...  9.6 us
    ppermute x4, starting transfers between devices, packed_device(): over_z = lambda a: lax.ppermute(a, 'tensor', [(i, i ^ 1) for i in range(4)])  6.37 us
    ppermute x3, starting transfers between devices, packed_device(): over_x = lambda a: lax.ppermute(a, 'fsdp', [(i, i ^ 2) for i in range(4)])  5.26 us
    ppermute x4, waiting for transfers between devices, packed_device(): over_z = lambda a: lax.ppermute(a, 'tensor', [(i, i ^ 1) for i in range(4)])  5 us
    ppermute x2, starting transfers between devices, packed_device(): lax.ppermute(packed, ('tensor', 'fsdp'), spread(a))  3.25 us
    ppermute x2, waiting for transfers between devices, packed_device(): lax.ppermute(packed, ('tensor', 'fsdp'), spread(a))  2.38 us
    ppermute x3, waiting for transfers between devices, packed_device(): over_x = lambda a: lax.ppermute(a, 'fsdp', [(i, i ^ 2) for i in range(4)])  2.24 us
  transfers between devices with their start and end apart: 21, of which 9 were waited for; matrix products, arithmetic and copies ran while one was open for 5% of the time, Pallas kernels for 16%

profile of v5, /device:TPU:0, one launch (start us, length us, event | category | flops | bytes accessed | tf_op | source)
XLA Modules:
  0.0 54.9 jit_solution(363241106982553629)
XLA Ops:
  0.7 1.0 %slice_bitcast_fusion.1 = bf16[48,1024]{1,0:T(8,128)(2,1)S(1)} fusion(bf16[1,128,1024]{2,1,0:T(8,128)(2,1)} %param.11), kind=kLoop, calls=%fused_computation.10 | loop fusion | bytes 196608 | tf_op jit(solution)/shard_map/slice | solution.py:285
  2.1 2.6 %collective-permute-start = (bf16[48,1024]{1,0:T(8,128)(2,1)S(1)}, bf16[48,1024]{1,0:T(8,128)(2,1)S(1)}, u32[]{:S(2)}, u32[]{:S(2)}) collective-permute-start(bf16[48,1024]{1,0:T(8,128)(2,1)S(1)} %slice_bitcast_fusion.1), channel_id=1, source_target_pairs={{0,16},{16,0},{1,17},{17,1},{2,18},{18,2},{3,19},{19,3},{4,20},{20... | collective-permute-start | bytes 294920 | tf_op jit(solution)/shard_map/ppermute | solution.py:272
  5.3 1.0 %dynamic-slice_bitcast_fusion = (bf16[128,512]{1,0:T(8,128)(2,1)S(1)}, bf16[128,512]{1,0:T(8,128)(2,1)S(1)}) fusion(bf16[1,128,1024]{2,1,0:T(8,128)(2,1)} %param.10, s32[]{:T(128)S(6)} %select_n.5, bf16[1,128,1024]{2,1,0:T(8,128)(2,1)} %param.9), kind=kLoop, calls=%fused_computation.4 | loop fusion | bytes 524292 | tf_op jit(solution)/shard_map/dynamic_slice | solution.py:281
  6.3 0.7 %convert_bitcast_fusion = bf16[128]{0:T(256)(128)(2,1)S(1)} fusion(s32[1,128]{1,0:T(1,128)} %param.15), kind=kLoop, calls=%fused_computation.11 | loop fusion | flops 128 | bytes 768 | tf_op jit(solution)/shard_map/broadcast_in_dim | solution.py:289
  7.0 1.1 %slice_bitcast_fusion.own_ref = bf16[80,1024]{1,0:T(8,128)(2,1)S(1)} fusion(bf16[1,128,1024]{2,1,0:T(8,128)(2,1)} %param.11), kind=kLoop, calls=%fused_computation.3 | loop fusion | bytes 327680 | tf_op jit(solution)/shard_map/slice | solution.py:293
  8.5 1.8 %collective-permute-start.6 = (bf16[400,512]{1,0:T(8,128)(2,1)S(1)}, bf16[400,512]{1,0:T(8,128)(2,1)S(1)}, u32[]{:S(2)}, u32[]{:S(2)}) collective-permute-start(bf16[400,512]{1,0:T(8,128)(2,1)S(1)} %get-tuple-element.120), channel_id=1, source_target_pairs={{0,16},{16,0},{1,17},{17,1},{2,18},{18,2},{3,19},{19,3},{4,20},{20... | collective-permute-start | bytes 1228808 | tf_op jit(solution)/shard_map/ppermute | solution.py:272
  10.3 2.6 %collective-permute-start.4 = (bf16[80,1024]{1,0:T(8,128)(2,1)S(1)}, bf16[80,1024]{1,0:T(8,128)(2,1)S(1)}, u32[]{:S(2)}, u32[]{:S(2)}) collective-permute-start(bf16[80,1024]{1,0:T(8,128)(2,1)S(1)} %shard_map.111), channel_id=1, source_target_pairs={{0,8},{1,9},{2,0},{3,1},{4,12},{5,13},{6,4},{7,5},{8,10},{9,11},{1... | collective-permute-start | bytes 491528 | tf_op jit(solution)/shard_map/ppermute | solution.py:298
  13.6 2.4 %collective-permute-done.4.b10_ref = bf16[80,1024]{1,0:T(8,128)(2,1)S(1)} collective-permute-done((bf16[80,1024]{1,0:T(8,128)(2,1)S(1)}, bf16[80,1024]{1,0:T(8,128)(2,1)S(1)}, u32[]{:S(2)}, u32[]{:S(2)}) %collective-permute-start.4) | collective-permute-done | bytes 163872 | tf_op jit(solution)/shard_map/ppermute | solution.py:298
  15.9 0.8 %collective-permute-start.7 = (bf16[80,1024]{1,0:T(8,128)(2,1)S(1)}, bf16[80,1024]{1,0:T(8,128)(2,1)S(1)}, u32[]{:S(2)}, u32[]{:S(2)}) collective-permute-start(bf16[80,1024]{1,0:T(8,128)(2,1)S(1)} %collective-permute-done.4.b10_ref), channel_id=1, source_target_pairs={{0,16},{16,0},{1,17},{17,1},{2,18},{18,2},{3,19},{19,3},{4,20},{20... | collective-permute-start | bytes 491528 | tf_op jit(solution)/shard_map/ppermute | solution.py:272
  16.8 4.9 %collective-permute-start.5 = (bf16[80,1024]{1,0:T(8,128)(2,1)S(1)}, bf16[80,1024]{1,0:T(8,128)(2,1)S(1)}, u32[]{:S(2)}, u32[]{:S(2)}) collective-permute-start(bf16[80,1024]{1,0:T(8,128)(2,1)S(1)} %collective-permute-done.4.b10_ref), channel_id=1, source_target_pairs={{0,4},{4,0},{8,12},{12,8},{1,5},{5,1},{9,13},{13,9},{2,6},{6,2},{1... | collective-permute-start | bytes 491528 | tf_op jit(solution)/shard_map/ppermute | solution.py:299
  21.7 1.2 %collective-permute-start.13 = (bf16[80,1024]{1,0:T(8,128)(2,1)S(1)}, bf16[80,1024]{1,0:T(8,128)(2,1)S(1)}, u32[]{:S(2)}, u32[]{:S(2)}) collective-permute-start(bf16[80,1024]{1,0:T(8,128)(2,1)S(1)} %collective-permute-done.2.b00_ref), channel_id=1, source_target_pairs={{0,16},{16,0},{1,17},{17,1},{2,18},{18,2},{3,19},{19,3},{4,20},{20... | collective-permute-start | bytes 491528 | tf_op jit(solution)/shard_map/ppermute | solution.py:272
  22.9 1.9 %shard_map.112 = (bf16[160,512]{1,0:T(8,128)(2,1)S(1)}, bf16[160,512]{1,0:T(8,128)(2,1)S(1)}, bf16[160,512]{1,0:T(8,128)(2,1)S(1)}, f32[4,160,160]{2,1,0:T(8,128)S(1)}, bf16[160,512]{1,0:T(8,128)(2,1)S(1)}) custom-call(s32[1,1]{1,0:T(1,128)S(6)} %copy.12.count_ref, f32[8]{0:T(128)S(1)} %copy-done.2, bf16[400,512]{1,0:T(8,128)(2,1)S(1)} %get-tuple-element.121.mine_ref, ...), custom_call_target="tpu_custom_call" | custom-call | tf_op jit(solution)/shard_map/pallas_call | solution.py:31
  24.8 3.4 %collective-permute-start.12 = (bf16[160,512]{1,0:T(8,128)(2,1)S(1)}, bf16[160,512]{1,0:T(8,128)(2,1)S(1)}, u32[]{:S(2)}, u32[]{:S(2)}) collective-permute-start(bf16[160,512]{1,0:T(8,128)(2,1)S(1)} %get-tuple-element.105.output_ref.mine_ref), channel_id=1, source_target_pairs={{0,2},{1,3},{2,0},{3,1},{4,6},{5,7},{6,4},{7,5},{8,10},{9,11},{10,... | collective-permute-start | bytes 491528 | tf_op jit(solution)/shard_map/ppermute | solution.py:273
  28.3 1.2 %collective-permute-start.11 = (bf16[160,512]{1,0:T(8,128)(2,1)S(1)}, bf16[160,512]{1,0:T(8,128)(2,1)S(1)}, u32[]{:S(2)}, u32[]{:S(2)}) collective-permute-start(bf16[160,512]{1,0:T(8,128)(2,1)S(1)} %get-tuple-element.105.output_ref.mine_ref), channel_id=1, source_target_pairs={{0,16},{16,0},{1,17},{17,1},{2,18},{18,2},{3,19},{19,3},{4,20},{20... | collective-permute-start | bytes 491528 | tf_op jit(solution)/shard_map/ppermute | solution.py:272
  29.5 0.8 %collective-permute-done.3.b01_ref = bf16[80,1024]{1,0:T(8,128)(2,1)S(1)} collective-permute-done((bf16[80,1024]{1,0:T(8,128)(2,1)S(1)}, bf16[80,1024]{1,0:T(8,128)(2,1)S(1)}, u32[]{:S(2)}, u32[]{:S(2)}) %collective-permute-start.3) | collective-permute-done | bytes 163872 | tf_op jit(solution)/shard_map/ppermute | solution.py:299
  30.3 1.0 %shard_map.113 = (f32[80,512]{1,0:T(8,128)S(1)}, bf16[80,512]{1,0:T(8,128)(2,1)S(1)}, bf16[80,512]{1,0:T(8,128)(2,1)S(1)}, bf16[80,512]{1,0:T(8,128)(2,1)S(1)}, ...) custom-call(bf16[80,1024]{1,0:T(8,128)(2,1)S(1)} %collective-permute-done.2.b00_ref, ...), custom_call_target="tpu_custom_call" | custom-call | tf_op jit(solution)/shard_map/pallas_call | solution.py:31
  31.3 1.1 %collective-permute-start.8 = (bf16[80,512]{1,0:T(8,128)(2,1)S(1)}, bf16[80,512]{1,0:T(8,128)(2,1)S(1)}, u32[]{:S(2)}, u32[]{:S(2)}) collective-permute-start(bf16[80,512]{1,0:T(8,128)(2,1)S(1)} %get-tuple-element.80), channel_id=1, source_target_pairs={{0,2},{1,3},{2,0},{3,1},{4,6},{5,7},{6,4},{7,5},{8,10},{9,11},{10,... | collective-permute-start | bytes 245768 | tf_op jit(solution)/shard_map/ppermute | solution.py:273
  32.4 1.1 %collective-permute-start.9 = (bf16[80,512]{1,0:T(8,128)(2,1)S(1)}, bf16[80,512]{1,0:T(8,128)(2,1)S(1)}, u32[]{:S(2)}, u32[]{:S(2)}) collective-permute-start(bf16[80,512]{1,0:T(8,128)(2,1)S(1)} %get-tuple-element.81), channel_id=1, source_target_pairs={{0,16},{16,0},{1,17},{17,1},{2,18},{18,2},{3,19},{19,3},{4,20},{20... | collective-permute-start | bytes 245768 | tf_op jit(solution)/shard_map/ppermute | solution.py:272
  33.5 1.3 %collective-permute-start.10 = (bf16[80,512]{1,0:T(8,128)(2,1)S(1)}, bf16[80,512]{1,0:T(8,128)(2,1)S(1)}, u32[]{:S(2)}, u32[]{:S(2)}) collective-permute-start(bf16[80,512]{1,0:T(8,128)(2,1)S(1)} %get-tuple-element.82), channel_id=1, source_target_pairs={{0,18},{1,19},{2,16},{3,17},{16,2},{17,3},{18,0},{19,1},{4,22},{5,... | collective-permute-start | bytes 245768 | tf_op jit(solution)/shard_map/ppermute | solution.py:331
  34.8 1.5 %collective-permute-done.8.from_x_ref = bf16[80,512]{1,0:T(8,128)(2,1)S(1)} collective-permute-done((bf16[80,512]{1,0:T(8,128)(2,1)S(1)}, bf16[80,512]{1,0:T(8,128)(2,1)S(1)}, u32[]{:S(2)}, u32[]{:S(2)}) %collective-permute-start.8) | collective-permute-done | bytes 81952 | tf_op jit(solution)/shard_map/ppermute | solution.py:273
  36.3 0.7 %collective-permute-start.14 = (bf16[80,1024]{1,0:T(8,128)(2,1)S(1)}, bf16[80,1024]{1,0:T(8,128)(2,1)S(1)}, u32[]{:S(2)}, u32[]{:S(2)}) collective-permute-start(bf16[80,1024]{1,0:T(8,128)(2,1)S(1)} %collective-permute-done.7.p10_ref), channel_id=1, source_target_pairs={{0,4},{4,0},{8,12},{12,8},{1,5},{5,1},{9,13},{13,9},{2,6},{6,2},{1... | collective-permute-start | bytes 491528 | tf_op jit(solution)/shard_map/ppermute | solution.py:299
  37.3 1.5 %collective-permute-done.10.from_xy_ref = bf16[80,512]{1,0:T(8,128)(2,1)S(1)} collective-permute-done((bf16[80,512]{1,0:T(8,128)(2,1)S(1)}, bf16[80,512]{1,0:T(8,128)(2,1)S(1)}, u32[]{:S(2)}, u32[]{:S(2)}) %collective-permute-start.10) | collective-permute-done | bytes 81952 | tf_op jit(solution)/shard_map/ppermute | solution.py:331
  38.8 1.5 %shard_map.114 = (bf16[384,512]{1,0:T(8,128)(2,1)S(1)}, bf16[320,512]{1,0:T(8,128)(2,1)S(1)}, bf16[64,512]{1,0:T(8,128)(2,1)S(1)}) custom-call(s32[1,1]{1,0:T(1,128)S(6)} %copy.12.count_ref, bf16[160,512]{1,0:T(8,128)(2,1)S(1)} %get-tuple-element.85.q_ref, bf16[160,512]{1,0:T(8,128)(2,1)S(1)} %get-tuple-element.86.k_ref, ...), custom_call_target="tpu_custom_call" | custom-call | tf_op jit(solution)/shard_map/pallas_call | solution.py:31
  40.4 1.0 %collective-permute-start.17 = (bf16[320,512]{1,0:T(8,128)(2,1)S(1)}, bf16[320,512]{1,0:T(8,128)(2,1)S(1)}, u32[]{:S(2)}, u32[]{:S(2)}) collective-permute-start(bf16[320,512]{1,0:T(8,128)(2,1)S(1)} %get-tuple-element.94), channel_id=1, source_target_pairs={{0,16},{16,0},{1,17},{17,1},{2,18},{18,2},{3,19},{19,3},{4,20},{20... | collective-permute-start | bytes 983048 | tf_op jit(solution)/shard_map/ppermute | solution.py:272
  41.7 0.7 %collective-permute-start.15 = (bf16[80,1024]{1,0:T(8,128)(2,1)S(1)}, bf16[80,1024]{1,0:T(8,128)(2,1)S(1)}, u32[]{:S(2)}, u32[]{:S(2)}) collective-permute-start(bf16[80,1024]{1,0:T(8,128)(2,1)S(1)} %collective-permute-done.13.p00_ref), channel_id=1, source_target_pairs={{0,4},{4,0},{8,12},{12,8},{1,5},{5,1},{9,13},{13,9},{2,6},{6,2},{1... | collective-permute-start | bytes 491528 | tf_op jit(solution)/shard_map/ppermute | solution.py:299
  42.4 0.7 %collective-permute-start.16 = (bf16[160,512]{1,0:T(8,128)(2,1)S(1)}, bf16[160,512]{1,0:T(8,128)(2,1)S(1)}, u32[]{:S(2)}, u32[]{:S(2)}) collective-permute-start(bf16[160,512]{1,0:T(8,128)(2,1)S(1)} %collective-permute-done.11.away_ref), channel_id=1, source_target_pairs={{0,2},{1,3},{2,0},{3,1},{4,6},{5,7},{6,4},{7,5},{8,10},{9,11},{10,... | collective-permute-start | bytes 491528 | tf_op jit(solution)/shard_map/ppermute | solution.py:273
  43.1 3.9 %collective-permute-done.15.p01_ref = bf16[80,1024]{1,0:T(8,128)(2,1)S(1)} collective-permute-done((bf16[80,1024]{1,0:T(8,128)(2,1)S(1)}, bf16[80,1024]{1,0:T(8,128)(2,1)S(1)}, u32[]{:S(2)}, u32[]{:S(2)}) %collective-permute-start.15) | collective-permute-done | bytes 163872 | tf_op jit(solution)/shard_map/ppermute | solution.py:299
  47.0 0.7 %collective-permute-done.16.away_x_ref = bf16[160,512]{1,0:T(8,128)(2,1)S(1)} collective-permute-done((bf16[160,512]{1,0:T(8,128)(2,1)S(1)}, bf16[160,512]{1,0:T(8,128)(2,1)S(1)}, u32[]{:S(2)}, u32[]{:S(2)}) %collective-permute-start.16) | collective-permute-done | bytes 163872 | tf_op jit(solution)/shard_map/ppermute | solution.py:273
  48.7 1.2 %collective-permute-start.20 = (bf16[64,512]{1,0:T(8,128)(2,1)S(1)}, bf16[64,512]{1,0:T(8,128)(2,1)S(1)}, u32[]{:S(2)}, u32[]{:S(2)}) collective-permute-start(bf16[64,512]{1,0:T(8,128)(2,1)S(1)} %get-tuple-element.115), channel_id=1, source_target_pairs={{0,16},{16,0},{1,17},{17,1},{2,18},{18,2},{3,19},{19,3},{4,20},{20... | collective-permute-start | bytes 196616 | tf_op jit(solution)/shard_map/ppermute | solution.py:272
  49.9 1.4 %shard_map.116.total_ref = bf16[1024,1024]{1,0:T(8,128)(2,1)S(1)} custom-call(bf16[160,1024]{1,0:T(8,128)(2,1)S(1)} %get-tuple-element.78.own_g_ref, bf16[160,1024]{1,0:T(8,128)(2,1)S(1)} %get-tuple-element.109.own_p_ref, bf16[160,512]{1,0:T(8,128)(2,1)S(1)} %get-tuple-element.105.output_ref.mine_ref, ...), custom_call_target="tpu_custom_call" | custom-call | tf_op jit(solution)/shard_map/pallas_call | solution.py:31
  51.4 2.5 %shard_map.117 = f32[1024,1024]{1,0:T(8,128)} custom-call(bf16[1024,1024]{1,0:T(8,128)(2,1)S(1)} %shard_map.116.total_ref, bf16[160,1024]{1,0:T(8,128)(2,1)S(1)} %collective-permute-done.18.near_g_ref, bf16[480,1024]{1,0:T(8,128)(2,1)S(1)} %collective-permute-done.19.bundle_ref), custom_call_target="tpu_custom_call" | custom-call | tf_op jit(solution)/shard_map/pallas_call | solution.py:31
  53.9 1.0 %shard_map.118 = (bf16[128,1024]{1,0:T(8,128)(2,1)}, bf16[128,1024]{1,0:T(8,128)(2,1)}, bf16[128,1024]{1,0:T(8,128)(2,1)}) custom-call(bf16[384,512]{1,0:T(8,128)(2,1)S(1)} %get-tuple-element.113.own_ref, bf16[320,512]{1,0:T(8,128)(2,1)S(1)} %collective-permute-done.17.peer_ref, bf16[64,512]{1,0:T(8,128)(2,1)S(1)} %collective-permute-done.20.peer_q_ref), custom_call_target="tpu_custom_call" | custom-call | tf_op jit(solution)/shard_map/pallas_call | solution.py:31
  (37 shorter events, 3.2 us)
Async XLA Ops:
  0.6 7.5 %copy-start = (bf16[1,128,1024]{2,1,0:T(8,128)(2,1)S(1)}, bf16[1,128,1024]{2,1,0:T(8,128)(2,1)}, u32[]{:S(2)}) copy-start(bf16[1,128,1024]{2,1,0:T(8,128)(2,1)} %param.8) | copy-start | bytes 786436
  0.6 7.8 %copy-start.3 = (bf16[1,128,1024]{2,1,0:T(8,128)(2,1)S(1)}, bf16[1,128,1024]{2,1,0:T(8,128)(2,1)}, u32[]{:S(2)}) copy-start(bf16[1,128,1024]{2,1,0:T(8,128)(2,1)} %param.10) | copy-start | bytes 786436
  0.7 7.8 %copy-start.4 = (bf16[1,128,1024]{2,1,0:T(8,128)(2,1)S(1)}, bf16[1,128,1024]{2,1,0:T(8,128)(2,1)}, u32[]{:S(2)}) copy-start(bf16[1,128,1024]{2,1,0:T(8,128)(2,1)} %param.9) | copy-start | bytes 786436
  0.7 22.3 %copy-start.2 = (f32[8]{0:T(128)S(1)}, f32[8]{0:T(128)}, u32[]{:S(2)}) copy-start(f32[8]{0:T(128)} %slopes_ref.1) | copy-start | bytes 100
  1.6 6.7 %collective-permute-start.1 = (bf16[1024,1024]{1,0:T(8,128)(2,1)}, bf16[1024,1024]{1,0:T(8,128)(2,1)S(1)}, u32[]{:S(2)}, u32[]{:S(2)}) collective-permute-start(bf16[1024,1024]{1,0:T(8,128)(2,1)} %own_w_ref.1), channel_id=1, source_target_pairs={{0,1},{1,0},{2,3},{3,2},{4,5},{5,4},{6,7},{7,6},{8,9},{9,8},{10,11... | collective-permute-start | bytes 6291464 | tf_op jit(solution)/shard_map/ppermute | solution.py:274
  2.1 6.0 %collective-permute-start = (bf16[48,1024]{1,0:T(8,128)(2,1)S(1)}, bf16[48,1024]{1,0:T(8,128)(2,1)S(1)}, u32[]{:S(2)}, u32[]{:S(2)}) collective-permute-start(bf16[48,1024]{1,0:T(8,128)(2,1)S(1)} %slice_bitcast_fusion.1), channel_id=1, source_target_pairs={{0,16},{16,0},{1,17},{17,1},{2,18},{18,2},{3,19},{19,3},{4,20},{20... | collective-permute-start | bytes 294920 | tf_op jit(solution)/shard_map/ppermute | solution.py:272
  7.0 23.3 %copy-start.1 = (bf16[1024,1024]{1,0:T(8,128)(2,1)S(1)}, bf16[1024,1024]{1,0:T(8,128)(2,1)}, u32[]{:S(2)}) copy-start(bf16[1024,1024]{1,0:T(8,128)(2,1)} %own_w_ref.1) | copy-start | bytes 6291460
  8.5 14.4 %collective-permute-start.6 = (bf16[400,512]{1,0:T(8,128)(2,1)S(1)}, bf16[400,512]{1,0:T(8,128)(2,1)S(1)}, u32[]{:S(2)}, u32[]{:S(2)}) collective-permute-start(bf16[400,512]{1,0:T(8,128)(2,1)S(1)} %get-tuple-element.120), channel_id=1, source_target_pairs={{0,16},{16,0},{1,17},{17,1},{2,18},{18,2},{3,19},{19,3},{4,20},{20... | collective-permute-start | bytes 1228808 | tf_op jit(solution)/shard_map/ppermute | solution.py:272
  10.3 5.6 %collective-permute-start.4 = (bf16[80,1024]{1,0:T(8,128)(2,1)S(1)}, bf16[80,1024]{1,0:T(8,128)(2,1)S(1)}, u32[]{:S(2)}, u32[]{:S(2)}) collective-permute-start(bf16[80,1024]{1,0:T(8,128)(2,1)S(1)} %shard_map.111), channel_id=1, source_target_pairs={{0,8},{1,9},{2,0},{3,1},{4,12},{5,13},{6,4},{7,5},{8,10},{9,11},{1... | collective-permute-start | bytes 491528 | tf_op jit(solution)/shard_map/ppermute | solution.py:298
  12.9 8.8 %collective-permute-start.2 = (bf16[80,1024]{1,0:T(8,128)(2,1)S(1)}, bf16[80,1024]{1,0:T(8,128)(2,1)S(1)}, u32[]{:S(2)}, u32[]{:S(2)}) collective-permute-start(bf16[80,1024]{1,0:T(8,128)(2,1)S(1)} %shard_map.111), channel_id=1, source_target_pairs={{0,0},{1,1},{2,8},{3,9},{4,4},{5,5},{6,12},{7,13},{8,2},{9,3},{10,... | collective-permute-start | bytes 491528 | tf_op jit(solution)/shard_map/ppermute | solution.py:298
  15.9 12.3 %collective-permute-start.7 = (bf16[80,1024]{1,0:T(8,128)(2,1)S(1)}, bf16[80,1024]{1,0:T(8,128)(2,1)S(1)}, u32[]{:S(2)}, u32[]{:S(2)}) collective-permute-start(bf16[80,1024]{1,0:T(8,128)(2,1)S(1)} %collective-permute-done.4.b10_ref), channel_id=1, source_target_pairs={{0,16},{16,0},{1,17},{17,1},{2,18},{18,2},{3,19},{19,3},{4,20},{20... | collective-permute-start | bytes 491528 | tf_op jit(solution)/shard_map/ppermute | solution.py:272
  16.8 12.7 %collective-permute-start.5 = (bf16[80,1024]{1,0:T(8,128)(2,1)S(1)}, bf16[80,1024]{1,0:T(8,128)(2,1)S(1)}, u32[]{:S(2)}, u32[]{:S(2)}) collective-permute-start(bf16[80,1024]{1,0:T(8,128)(2,1)S(1)} %collective-permute-done.4.b10_ref), channel_id=1, source_target_pairs={{0,4},{4,0},{8,12},{12,8},{1,5},{5,1},{9,13},{13,9},{2,6},{6,2},{1... | collective-permute-start | bytes 491528 | tf_op jit(solution)/shard_map/ppermute | solution.py:299
  21.7 8.6 %collective-permute-start.3 = (bf16[80,1024]{1,0:T(8,128)(2,1)S(1)}, bf16[80,1024]{1,0:T(8,128)(2,1)S(1)}, u32[]{:S(2)}, u32[]{:S(2)}) collective-permute-start(bf16[80,1024]{1,0:T(8,128)(2,1)S(1)} %collective-permute-done.2.b00_ref), channel_id=1, source_target_pairs={{0,4},{4,0},{8,12},{12,8},{1,5},{5,1},{9,13},{13,9},{2,6},{6,2},{1... | collective-permute-start | bytes 491528 | tf_op jit(solution)/shard_map/ppermute | solution.py:299
  21.7 11.8 %collective-permute-start.13 = (bf16[80,1024]{1,0:T(8,128)(2,1)S(1)}, bf16[80,1024]{1,0:T(8,128)(2,1)S(1)}, u32[]{:S(2)}, u32[]{:S(2)}) collective-permute-start(bf16[80,1024]{1,0:T(8,128)(2,1)S(1)} %collective-permute-done.2.b00_ref), channel_id=1, source_target_pairs={{0,16},{16,0},{1,17},{17,1},{2,18},{18,2},{3,19},{19,3},{4,20},{20... | collective-permute-start | bytes 491528 | tf_op jit(solution)/shard_map/ppermute | solution.py:272
  24.8 14.0 %collective-permute-start.12 = (bf16[160,512]{1,0:T(8,128)(2,1)S(1)}, bf16[160,512]{1,0:T(8,128)(2,1)S(1)}, u32[]{:S(2)}, u32[]{:S(2)}) collective-permute-start(bf16[160,512]{1,0:T(8,128)(2,1)S(1)} %get-tuple-element.105.output_ref.mine_ref), channel_id=1, source_target_pairs={{0,2},{1,3},{2,0},{3,1},{4,6},{5,7},{6,4},{7,5},{8,10},{9,11},{10,... | collective-permute-start | bytes 491528 | tf_op jit(solution)/shard_map/ppermute | solution.py:273
  28.3 10.6 %collective-permute-start.11 = (bf16[160,512]{1,0:T(8,128)(2,1)S(1)}, bf16[160,512]{1,0:T(8,128)(2,1)S(1)}, u32[]{:S(2)}, u32[]{:S(2)}) collective-permute-start(bf16[160,512]{1,0:T(8,128)(2,1)S(1)} %get-tuple-element.105.output_ref.mine_ref), channel_id=1, source_target_pairs={{0,16},{16,0},{1,17},{17,1},{2,18},{18,2},{3,19},{19,3},{4,20},{20... | collective-permute-start | bytes 491528 | tf_op jit(solution)/shard_map/ppermute | solution.py:272
  31.3 5.1 %collective-permute-start.8 = (bf16[80,512]{1,0:T(8,128)(2,1)S(1)}, bf16[80,512]{1,0:T(8,128)(2,1)S(1)}, u32[]{:S(2)}, u32[]{:S(2)}) collective-permute-start(bf16[80,512]{1,0:T(8,128)(2,1)S(1)} %get-tuple-element.80), channel_id=1, source_target_pairs={{0,2},{1,3},{2,0},{3,1},{4,6},{5,7},{6,4},{7,5},{8,10},{9,11},{10,... | collective-permute-start | bytes 245768 | tf_op jit(solution)/shard_map/ppermute | solution.py:273
  32.4 5.0 %collective-permute-start.9 = (bf16[80,512]{1,0:T(8,128)(2,1)S(1)}, bf16[80,512]{1,0:T(8,128)(2,1)S(1)}, u32[]{:S(2)}, u32[]{:S(2)}) collective-permute-start(bf16[80,512]{1,0:T(8,128)(2,1)S(1)} %get-tuple-element.81), channel_id=1, source_target_pairs={{0,16},{16,0},{1,17},{17,1},{2,18},{18,2},{3,19},{19,3},{4,20},{20... | collective-permute-start | bytes 245768 | tf_op jit(solution)/shard_map/ppermute | solution.py:272
  33.5 5.3 %collective-permute-start.10 = (bf16[80,512]{1,0:T(8,128)(2,1)S(1)}, bf16[80,512]{1,0:T(8,128)(2,1)S(1)}, u32[]{:S(2)}, u32[]{:S(2)}) collective-permute-start(bf16[80,512]{1,0:T(8,128)(2,1)S(1)} %get-tuple-element.82), channel_id=1, source_target_pairs={{0,18},{1,19},{2,16},{3,17},{16,2},{17,3},{18,0},{19,1},{4,22},{5,... | collective-permute-start | bytes 245768 | tf_op jit(solution)/shard_map/ppermute | solution.py:331
  36.3 5.3 %collective-permute-start.14 = (bf16[80,1024]{1,0:T(8,128)(2,1)S(1)}, bf16[80,1024]{1,0:T(8,128)(2,1)S(1)}, u32[]{:S(2)}, u32[]{:S(2)}) collective-permute-start(bf16[80,1024]{1,0:T(8,128)(2,1)S(1)} %collective-permute-done.7.p10_ref), channel_id=1, source_target_pairs={{0,4},{4,0},{8,12},{12,8},{1,5},{5,1},{9,13},{13,9},{2,6},{6,2},{1... | collective-permute-start | bytes 491528 | tf_op jit(solution)/shard_map/ppermute | solution.py:299
  40.4 7.7 %collective-permute-start.17 = (bf16[320,512]{1,0:T(8,128)(2,1)S(1)}, bf16[320,512]{1,0:T(8,128)(2,1)S(1)}, u32[]{:S(2)}, u32[]{:S(2)}) collective-permute-start(bf16[320,512]{1,0:T(8,128)(2,1)S(1)} %get-tuple-element.94), channel_id=1, source_target_pairs={{0,16},{16,0},{1,17},{17,1},{2,18},{18,2},{3,19},{19,3},{4,20},{20... | collective-permute-start | bytes 983048 | tf_op jit(solution)/shard_map/ppermute | solution.py:272
  41.7 5.3 %collective-permute-start.15 = (bf16[80,1024]{1,0:T(8,128)(2,1)S(1)}, bf16[80,1024]{1,0:T(8,128)(2,1)S(1)}, u32[]{:S(2)}, u32[]{:S(2)}) collective-permute-start(bf16[80,1024]{1,0:T(8,128)(2,1)S(1)} %collective-permute-done.13.p00_ref), channel_id=1, source_target_pairs={{0,4},{4,0},{8,12},{12,8},{1,5},{5,1},{9,13},{13,9},{2,6},{6,2},{1... | collective-permute-start | bytes 491528 | tf_op jit(solution)/shard_map/ppermute | solution.py:299
  42.4 5.3 %collective-permute-start.16 = (bf16[160,512]{1,0:T(8,128)(2,1)S(1)}, bf16[160,512]{1,0:T(8,128)(2,1)S(1)}, u32[]{:S(2)}, u32[]{:S(2)}) collective-permute-start(bf16[160,512]{1,0:T(8,128)(2,1)S(1)} %collective-permute-done.11.away_ref), channel_id=1, source_target_pairs={{0,2},{1,3},{2,0},{3,1},{4,6},{5,7},{6,4},{7,5},{8,10},{9,11},{10,... | collective-permute-start | bytes 491528 | tf_op jit(solution)/shard_map/ppermute | solution.py:273
  48.2 3.2 %collective-permute-start.19 = (bf16[480,1024]{1,0:T(8,128)(2,1)S(1)}, bf16[480,1024]{1,0:T(8,128)(2,1)S(1)}, u32[]{:S(2)}, u32[]{:S(2)}) collective-permute-start(bf16[480,1024]{1,0:T(8,128)(2,1)S(1)} %get-tuple-element.111), channel_id=1, source_target_pairs={{0,1},{1,0},{2,3},{3,2},{4,5},{5,4},{6,7},{7,6},{8,9},{9,8},{10,11... | collective-permute-start | bytes 2949128 | tf_op jit(solution)/shard_map/ppermute | solution.py:274
  48.2 3.1 %collective-permute-start.18 = (bf16[160,1024]{1,0:T(8,128)(2,1)S(1)}, bf16[160,1024]{1,0:T(8,128)(2,1)S(1)}, u32[]{:S(2)}, u32[]{:S(2)}) collective-permute-start(bf16[160,1024]{1,0:T(8,128)(2,1)S(1)} %get-tuple-element.110), channel_id=1, source_target_pairs={{0,1},{1,0},{2,3},{3,2},{4,5},{5,4},{6,7},{7,6},{8,9},{9,8},{10,11... | collective-permute-start | bytes 983048 | tf_op jit(solution)/shard_map/ppermute | solution.py:274
  48.7 5.2 %collective-permute-start.20 = (bf16[64,512]{1,0:T(8,128)(2,1)S(1)}, bf16[64,512]{1,0:T(8,128)(2,1)S(1)}, u32[]{:S(2)}, u32[]{:S(2)}) collective-permute-start(bf16[64,512]{1,0:T(8,128)(2,1)S(1)} %get-tuple-element.115), channel_id=1, source_target_pairs={{0,16},{16,0},{1,17},{17,1},{2,18},{18,2},{3,19},{19,3},{4,20},{20... | collective-permute-start | bytes 196616 | tf_op jit(solution)/shard_map/ppermute | solution.py:272
